TPU v7x, 32 devices: a whole 2x2x4 slice. The times are simulated.
32 devices in a mesh: groups: 2 (over x), expert: 16 (over z, y, core), dp: 1.
Axes of the slice: x: 2, y: 2, z: 4, core: 2. Of those that a mesh axis runs over, the one named last changes fastest.
Arguments:
- queries: bfloat16 [4, 64, 64, 576], P(None, ('groups', 'expert', 'dp')), parts along dimension 1, may hold values from -400 to 400
- latent_cache: bfloat16 [64, 256, 576], P(('groups', 'expert', 'dp')), parts along dimension 0, may hold values from -8 to 8
- new_latents: bfloat16 [4, 64, 576], P(None, ('groups', 'expert', 'dp')), parts along dimension 1, may hold values from -8 to 8
- lengths: int32 [64], P(('groups', 'expert', 'dp')), parts along dimension 0, may hold values from 2 to 252, as said below
- hidden_in: bfloat16 [4, 64, 3584], P(None, ('groups', 'expert', 'dp')), parts along dimension 1, may hold values from -6 to 6
- first_routes: int32 [2, 64, 8], P(None, ('groups', 'expert')), parts along dimension 1, may hold values from 0 to 15, all different within a row; in each aligned block of 4 rows (0 to 3, 4 to 7, ..., all dimensions but the last counted through in order) at most 4 rows name the same one
- second_routes: int32 [2, 64, 8], P(None, ('groups', 'expert')), parts along dimension 1, may hold values from 0 to 17, all different within a row; in each aligned block of 4 rows (0 to 3, 4 to 7, ..., all dimensions but the last counted through in order) at most 4 rows name the same one
- route_weights: float32 [4, 64, 8], P(None, ('groups', 'expert')), parts along dimension 1, may hold values from 0.05 to 1
- gate_weights: bfloat16 [16, 3584, 1024], P('expert', None, 'dp'), may hold values from -0.09375 to 0.09375
- up_weights: bfloat16 [16, 3584, 1024], P('expert', None, 'dp'), may hold values from -0.09375 to 0.09375
- down_weights: bfloat16 [16, 1024, 3584], P('expert', 'dp'), may hold values from -0.1875 to 0.1875
- hot_experts: int32 [2], replicated, may hold values from 0 to 15
Outputs:
- context: bfloat16 [4, 64, 64, 512], P(None, ('groups', 'expert', 'dp')), parts along dimension 1
- moe_out: bfloat16 [4, 64, 3584], P(None, ('groups', 'expert', 'dp')), parts along dimension 1
There are 2 independent parts, one for each index of `groups`. A program takes and returns all parts, laid end to end along the dimension named above; an argument that names none is the same for every part. Nothing has to cross between parts.
Inputs may be any that keep to these rules, and one draw needn't show every extreme that they name: `lengths`: each row holds at least 2 filled slots; some row of every draw holds exactly 252. `first_routes`: each row names 8 distinct experts. In every step the 4 rows held by one index of expert name no expert more than 4 times, and in some steps and indices one expert exactly 4 times. `second_routes`: each row names 8 distinct slots; slot 16 + r stands for the copy of hot_experts[r]. In every step the 4 rows held by one index of expert name no slot more than 4 times, and in some steps and indices one slot exactly 4 times.
All inputs are finite; a program needn't handle non-finite values.
Results may differ from a plain program's by a relative error of at most 0.015.
Values may be sent and summed in bfloat16 or wider, within the bound.
No kernel may reach another device: no remote copies, remote signals or barrier semaphores. Data moves between devices by JAX's collectives and lax.ppermute only.
A program may use at most 192 MiB of HBM per device.

v0:
```python
import jax
import jax.numpy as jnp
from jax import lax
from jax.sharding import PartitionSpec as P

RANK = 512


SCORE_SCALE = 0.07216878364870322


def from_root(value, axis, source):
    kept = jnp.where(lax.axis_index(axis) == source, value, 0).astype(value.dtype)
    return lax.psum(kept, axis)


def expert_apply(token_rows, gate_weight, up_weight, down_weight):
    gate_act = jnp.dot(token_rows, gate_weight, preferred_element_type=jnp.float32)
    up_act = jnp.dot(token_rows, up_weight, preferred_element_type=jnp.float32)
    hidden_act = (jax.nn.silu(gate_act) * up_act).astype(jnp.bfloat16)
    return jnp.dot(hidden_act, down_weight, preferred_element_type=jnp.float32)


def attend(queries_now, latent_cache, new_latents, lengths, step_index):
    old_scores = (
        jnp.einsum("bhl,bjl->bhj", queries_now, latent_cache, preferred_element_type=jnp.float32)
        * SCORE_SCALE
    )
    new_scores = (
        jnp.einsum("bhl,tbl->bht", queries_now, new_latents, preferred_element_type=jnp.float32)
        * SCORE_SCALE
    )
    keep_old = (jnp.arange(latent_cache.shape[1], dtype=jnp.int32)[None, :] < lengths[:, None])[
        :, None, :
    ]
    keep_new = (jnp.arange(new_latents.shape[0], dtype=jnp.int32) <= step_index)[None, None, :]
    old_scores = jnp.where(keep_old, old_scores, -1e30)
    new_scores = jnp.where(keep_new, new_scores, -1e30)
    row_max = jnp.maximum(
        jnp.max(old_scores, axis=2, keepdims=True), jnp.max(new_scores, axis=2, keepdims=True)
    )
    old_exp = jnp.where(keep_old, jnp.exp(old_scores - row_max), 0.0)
    new_exp = jnp.where(keep_new, jnp.exp(new_scores - row_max), 0.0)
    denominator = jnp.sum(old_exp, axis=2, keepdims=True) + jnp.sum(new_exp, axis=2, keepdims=True)
    old_probs = (old_exp / denominator).astype(jnp.bfloat16)
    new_probs = (new_exp / denominator).astype(jnp.bfloat16)
    context = jnp.einsum(
        "bhj,bjr->bhr", old_probs, latent_cache[:, :, :RANK], preferred_element_type=jnp.float32
    )
    context = context + jnp.einsum(
        "bht,tbr->bhr", new_probs, new_latents[:, :, :RANK], preferred_element_type=jnp.float32
    )
    return context.astype(jnp.bfloat16)


def routing_tables(slots, weights, expert_count, capacity):
    row_count, top_count = slots.shape
    flat_ids = slots.reshape(row_count * top_count)
    is_live = flat_ids < expert_count
    hit_table = (
        (flat_ids[:, None] == jnp.arange(expert_count, dtype=jnp.int32)[None, :]) & is_live[:, None]
    ).astype(jnp.int32)
    ranking = jnp.sum(jnp.cumsum(hit_table, axis=0) * hit_table, axis=1) - 1
    target = jnp.where(is_live, flat_ids * capacity + ranking, -1)
    slot_table = (
        target[:, None] == jnp.arange(expert_count * capacity, dtype=jnp.int32)[None, :]
    ).astype(jnp.float32)
    slot_table = slot_table.reshape(row_count, top_count, expert_count * capacity)
    choose = jnp.sum(slot_table, axis=1)
    blend_table = jnp.sum(slot_table * weights[:, :, None], axis=1)
    return (choose, blend_table)


def mixture(
    pair_rows, slots, weights, gate_weights, up_weights, down_weights, expert_count, capacity
):
    model_width = pair_rows.shape[1]
    choose, blend_table = routing_tables(slots, weights, expert_count, capacity)
    buffer = jnp.dot(
        jnp.transpose(choose).astype(jnp.bfloat16), pair_rows, preferred_element_type=jnp.float32
    ).astype(jnp.bfloat16)
    buffer = buffer.reshape(expert_count, capacity, model_width)
    arrived = lax.all_to_all(buffer, "expert", split_axis=0, concat_axis=0, tiled=True)
    outputs = expert_apply(
        arrived.reshape(-1, model_width), gate_weights[0], up_weights[0], down_weights[0]
    )
    outputs = outputs.reshape(arrived.shape[0], arrived.shape[1], model_width)
    returned = lax.all_to_all(
        outputs.astype(jnp.bfloat16), "expert", split_axis=0, concat_axis=0, tiled=True
    ).astype(outputs.dtype)
    return jnp.dot(
        blend_table,
        returned.reshape(expert_count * capacity, model_width),
        precision=lax.Precision.HIGHEST,
        preferred_element_type=jnp.float32,
    )


def per_device(
    queries,
    latent_cache,
    new_latents,
    lengths,
    hidden_in,
    first_routes,
    second_routes,
    route_weights,
    gate_weights,
    up_weights,
    down_weights,
    hot_experts,
):
    expert_count = lax.axis_size("expert")
    step_total = queries.shape[0]
    before = first_routes.shape[0]
    rows_dev = hidden_in.shape[1]
    top_count = first_routes.shape[2]
    capacity = min(2 * rows_dev, 4 * rows_dev * top_count // expert_count)
    contexts = []
    outputs = []
    copies = []
    for step_index in range(step_total):
        contexts.append(attend(queries[step_index], latent_cache, new_latents, lengths, step_index))
        if step_index == before:
            for slot_index in range(hot_experts.shape[0]):
                copies.append(
                    (
                        from_root(gate_weights, "expert", hot_experts[slot_index]),
                        from_root(up_weights, "expert", hot_experts[slot_index]),
                        from_root(down_weights, "expert", hot_experts[slot_index]),
                    )
                )
        pair_rows = lax.all_gather(hidden_in[step_index], "dp", axis=0, tiled=True)
        weights = route_weights[step_index]
        if step_index < before:
            slots = first_routes[step_index]
        else:
            slots = second_routes[step_index - before]
        partial_value = mixture(
            pair_rows,
            slots,
            weights,
            gate_weights,
            up_weights,
            down_weights,
            expert_count,
            capacity,
        )
        if step_index >= before:
            results = [
                expert_apply(pair_rows, copied[0][0], copied[1][0], copied[2][0])
                for copied in copies
            ]
            for slot_index in range(hot_experts.shape[0]):
                share_of = jnp.sum(
                    weights * (slots == expert_count + slot_index).astype(jnp.float32), axis=1
                )
                partial_value = partial_value + share_of[:, None] * results[slot_index]
        summed = lax.psum_scatter(
            partial_value.astype(jnp.bfloat16), "dp", scatter_dimension=0, tiled=True
        )
        outputs.append(summed)
    return (jnp.stack(contexts, axis=0), jnp.stack(outputs, axis=0))


def solution(mesh):
    placed = (
        P(None, ("groups", "expert", "dp"), None, None),
        P(("groups", "expert", "dp"), None, None),
        P(None, ("groups", "expert", "dp"), None),
        P(("groups", "expert", "dp")),
        P(None, ("groups", "expert", "dp"), None),
        P(None, ("groups", "expert"), None),
        P(None, ("groups", "expert"), None),
        P(None, ("groups", "expert"), None),
        P("expert", None, "dp"),
        P("expert", None, "dp"),
        P("expert", "dp", None),
        P(),
    )
    return jax.shard_map(
        per_device,
        mesh=mesh,
        in_specs=placed,
        out_specs=(
            P(None, ("groups", "expert", "dp"), None, None),
            P(None, ("groups", "expert", "dp"), None),
        ),
        check_vma=False,
    )
```

profile of v0, /device:TPU:0, one launch (start us, length us, event | category | flops | bytes accessed | tf_op | source)
XLA Modules:
  0.0 894.1 jit_solution(18053985587837200169)
XLA Ops:
  7.2 1.3 fusion.248
  9.8 9.1 %select_bitcast_fusion = (bf16[1024,3584]{1,0:T(8,128)(2,1)}, bf16[1024,3584]{1,0:T(8,128)(2,1)}) fusion(bf16[1,1024,3584]{2,1,0:T(8,128)(2,1)} %param.22, pred[]{:T(512)S(6)} %eq.176, pred[]{:T(512)S(6)} %eq.173), kind=kLoop, calls=%fused_computation.24 | loop fusion | flops 7340032 | bytes 22020098 | tf_op jit(solution)/shard_map/squeeze | solution.py:151
  18.9 14.1 %select_bitcast_fusion.1 = (bf16[3584,1024]{1,0:T(8,128)(2,1)}, bf16[3584,1024]{1,0:T(8,128)(2,1)}, bf16[3584,1024]{1,0:T(8,128)(2,1)}, bf16[3584,1024]{1,0:T(8,128)(2,1)}) fusion(bf16[1,3584,1024]{2,1,0:T(8,128)(2,1)} %param.21, pred[]{:T(512)S(6)} %eq.176, pred[]{:T(512)S(6)} %eq.173, bf16[1,3584,1024]{2,1,0:T(8,128)(2,1)} %param.20), kind=kLoop, calls=%fused_computation.25 | loop fusion | flops 14680064 | bytes 44040192 | tf_op jit(solution)/shard_map/squeeze | solution.py:151
  36.7 7.4 all-to-all-start.4
  50.8 1.6 fusion.253
  52.4 1.1 fusion.256
  53.6 1.5 fusion.255
  57.2 2.0 fusion.77
  61.2 3.9 all-to-all-done.4
  65.1 4.2 all-to-all-start.6
  69.3 1.9 reshape.288
  71.2 4.9 fusion.18
  76.2 1.4 fusion.65
  77.6 12.7 %all-to-all-done.6 = bf16[16,4,3584]{2,1,0:T(4,128)(2,1)} async-done(((bf16[16,4,3584]{2,1,0:T(4,128)(2,1)}), bf16[16,4,3584]{2,1,0:T(4,128)(2,1)}, u32[]{:S(2)}, u32[]{:S(2)}) %all-to-all-start.6) | async-done | bytes 458784 | tf_op jit(solution)/shard_map/all_to_all | solution.py:83
  90.3 3.6 all-to-all-start
  93.9 4.6 fusion.30
  98.4 1.1 copy.63
  99.6 1.1 reshape.291
  100.7 4.5 fusion.16
  105.2 9.7 %all-to-all-done = bf16[16,4,3584]{2,1,0:T(4,128)(2,1)S(1)} async-done(((bf16[16,4,3584]{2,1,0:T(4,128)(2,1)}), bf16[16,4,3584]{2,1,0:T(4,128)(2,1)S(1)}, u32[]{:S(2)}, u32[]{:S(2)}) %all-to-all-start) | async-done | bytes 458784 | tf_op jit(solution)/shard_map/all_to_all | solution.py:83
  114.8 3.7 all-to-all-start.2
  118.6 4.6 fusion.62
  123.2 4.5 fusion.33
  127.7 1.1 copy.65
  128.9 10.4 %all-to-all-done.2 = bf16[16,4,3584]{2,1,0:T(4,128)(2,1)S(1)} async-done(((bf16[16,4,3584]{2,1,0:T(4,128)(2,1)}), bf16[16,4,3584]{2,1,0:T(4,128)(2,1)S(1)}, u32[]{:S(2)}, u32[]{:S(2)}) %all-to-all-start.2) | async-done | bytes 458784 | tf_op jit(solution)/shard_map/all_to_all | solution.py:83
  139.4 3.6 all-to-all-start.5
  142.9 4.9 fusion.22
  147.8 4.5 fusion.71
  152.3 11.5 %all-to-all-done.5 = bf16[16,4,3584]{2,1,0:T(4,128)(2,1)S(1)} async-done(((bf16[16,4,3584]{2,1,0:T(4,128)(2,1)}), bf16[16,4,3584]{2,1,0:T(4,128)(2,1)S(1)}, u32[]{:S(2)}, u32[]{:S(2)}) %all-to-all-start.5) | async-done | bytes 458784 | tf_op jit(solution)/shard_map/all_to_all | solution.py:88
  163.8 3.6 all-to-all-start.7
  167.4 4.5 fusion.24
  171.9 1.1 copy.59
  173.2 4.5 fusion.20
  177.6 10.1 %all-to-all-done.7 = bf16[16,4,3584]{2,1,0:T(4,128)(2,1)S(1)} async-done(((bf16[16,4,3584]{2,1,0:T(4,128)(2,1)}), bf16[16,4,3584]{2,1,0:T(4,128)(2,1)S(1)}, u32[]{:S(2)}, u32[]{:S(2)}) %all-to-all-start.7) | async-done | bytes 458784 | tf_op jit(solution)/shard_map/all_to_all | solution.py:88
  187.8 3.6 all-to-all-start.1
  191.3 4.6 fusion.68
  196.2 4.6 fusion.27
  200.8 1.1 copy.61
  201.9 8.9 all-to-all-done.1
  210.9 3.8 all-to-all-start.3
  216.1 1.8 pad_maximum_fusion
  218.2 14.9 %all-to-all-done.3 = bf16[16,4,3584]{2,1,0:T(4,128)(2,1)S(1)} async-done(((bf16[16,4,3584]{2,1,0:T(4,128)(2,1)}), bf16[16,4,3584]{2,1,0:T(4,128)(2,1)S(1)}, u32[]{:S(2)}, u32[]{:S(2)}) %all-to-all-start.3) | async-done | bytes 458784 | tf_op jit(solution)/shard_map/all_to_all | solution.py:88
  234.4 613.8 %all-reduce.3.cloned.1.call-done = (bf16[1024,3584]{1,0:T(8,128)(2,1)}, bf16[3584,1024]{1,0:T(8,128)(2,1)}, bf16[3584,1024]{1,0:T(8,128)(2,1)}, bf16[1024,3584]{...) async-done(((bf16[1024,3584]{1,0:T(8,128)(2,1)}, bf16[3584,1024]{1,0:T(8,128)(2,1)}, bf16[3584,1024]{1,0:T(8,128)(2,1)}, ...) | async-done | bytes 44040208 | tf_op jit(solution)/shard_map/psum | solution.py:14
  848.3 4.3 convolution_bitcast_fusion.7
  857.6 7.2 fusion.39
  864.9 7.2 fusion.37
  872.1 7.2 fusion.45
  879.3 7.2 fusion.44
  (178 shorter events, 23.3 us)
Async XLA Ops:
  7.2 841.1 %all-reduce.3.cloned.1.call-start = ((), (), s32[]{:S(2)}) async-start(), calls=%async_computation.8 | async-start | bytes 88080384 | tf_op jit(solution)/shard_map/psum | solution.py:14
  33.1 2.3 copy-start.8
  33.1 12.2 %copy-start.25 = (s32[2,2,8]{2,1,0:T(2,128)S(1)}, s32[2,2,8]{2,1,0:T(2,128)}, u32[]{:S(2)}) copy-start(s32[2,2,8]{2,1,0:T(2,128)} %param.17) | copy-start | bytes 388
  33.1 16.3 %copy-start.22 = (bf16[4,2,576]{2,1,0:T(2,128)(2,1)S(1)}, bf16[4,2,576]{2,1,0:T(2,128)(2,1)}, u32[]{:S(2)}) copy-start(bf16[4,2,576]{2,1,0:T(2,128)(2,1)} %param.14) | copy-start | bytes 27652
  33.1 16.3 %copy-start.38 = (s32[2]{0:T(128)S(1)}, s32[2]{0:T(128)}, u32[]{:S(2)}) copy-start(s32[2]{0:T(128)} %param.15) | copy-start | bytes 28
  33.1 16.4 %copy-start.5 = (bf16[4,2,64,576]{3,2,1,0:T(8,128)(2,1)S(1)}, bf16[4,2,64,576]{3,2,1,0:T(8,128)(2,1)}, u32[]{:S(2)}) copy-start(bf16[4,2,64,576]{3,2,1,0:T(8,128)(2,1)} %param.12) | copy-start | bytes 1769476
  33.1 16.6 %copy-start.2 = (bf16[2,256,576]{1,2,0:T(8,128)(2,1)S(1)}, bf16[2,256,576]{1,2,0:T(8,128)(2,1)}, u32[]{:S(2)}) copy-start(bf16[2,256,576]{1,2,0:T(8,128)(2,1)} %param.13) | copy-start | bytes 1769476
  36.7 28.4 %all-to-all-start.4 = ((bf16[16,4,3584]{2,1,0:T(4,128)(2,1)}), bf16[16,4,3584]{2,1,0:T(4,128)(2,1)}, u32[]{:S(2)}, u32[]{:S(2)}) async-start(bf16[16,4,3584]{2,1,0:T(4,128)(2,1)} %reshape.287), calls=%async_computation.4 | async-start | bytes 917504 | tf_op jit(solution)/shard_map/all_to_all | solution.py:83
  50.6 8.6 copy-start.14
  50.8 25.4 %slice-start = ((s8[7340032]{0:T(1024)(128)(4,1)}), s8[3145728]{0:T(1024)(128)(4,1)S(1)}, s32[]{:S(2)}) async-start(s8[7340032]{0:T(1024)(128)(4,1)} %bitcast.282), calls=%async_computation.9 | async-start | bytes 6291456
  52.4 7.7 copy-start.16
  52.4 4.4 copy-start.36
  53.5 3.3 copy-start.20
  55.1 16.1 %copy-start.6 = (f32[2,64,256]{2,1,0:T(8,128)}, f32[2,64,256]{2,1,0:T(8,128)S(1)}, u32[]{:S(2)}) copy-start(f32[2,64,256]{2,1,0:T(8,128)S(1)} %get-tuple-element.57) | copy-start | bytes 393220
  55.1 1.7 copy-start.18
  56.8 3.3 copy-start.33
  56.9 3.3 copy-start.31
  65.1 25.2 %all-to-all-start.6 = ((bf16[16,4,3584]{2,1,0:T(4,128)(2,1)}), bf16[16,4,3584]{2,1,0:T(4,128)(2,1)}, u32[]{:S(2)}, u32[]{:S(2)}) async-start(bf16[16,4,3584]{2,1,0:T(4,128)(2,1)} %reshape.290), calls=%async_computation.6 | async-start | bytes 917504 | tf_op jit(solution)/shard_map/all_to_all | solution.py:83
  71.2 4.9 slice-start.1
  71.2 4.9 copy-start.4
  90.3 24.5 %all-to-all-start = ((bf16[16,4,3584]{2,1,0:T(4,128)(2,1)}), bf16[16,4,3584]{2,1,0:T(4,128)(2,1)S(1)}, u32[]{:S(2)}, u32[]{:S(2)}) async-start(bf16[16,4,3584]{2,1,0:T(4,128)(2,1)} %reshape.281), calls=%async_computation | async-start | bytes 917504 | tf_op jit(solution)/shard_map/all_to_all | solution.py:83
  114.8 24.5 %all-to-all-start.2 = ((bf16[16,4,3584]{2,1,0:T(4,128)(2,1)}), bf16[16,4,3584]{2,1,0:T(4,128)(2,1)S(1)}, u32[]{:S(2)}, u32[]{:S(2)}) async-start(bf16[16,4,3584]{2,1,0:T(4,128)(2,1)} %reshape.284), calls=%async_computation.2 | async-start | bytes 917504 | tf_op jit(solution)/shard_map/all_to_all | solution.py:83
  139.4 24.4 %all-to-all-start.5 = ((bf16[16,4,3584]{2,1,0:T(4,128)(2,1)}), bf16[16,4,3584]{2,1,0:T(4,128)(2,1)S(1)}, u32[]{:S(2)}, u32[]{:S(2)}) async-start(bf16[16,4,3584]{2,1,0:T(4,128)(2,1)} %copy.63), calls=%async_computation.5 | async-start | bytes 917504 | tf_op jit(solution)/shard_map/all_to_all | solution.py:88
  163.8 23.9 %all-to-all-start.7 = ((bf16[16,4,3584]{2,1,0:T(4,128)(2,1)}), bf16[16,4,3584]{2,1,0:T(4,128)(2,1)S(1)}, u32[]{:S(2)}, u32[]{:S(2)}) async-start(bf16[16,4,3584]{2,1,0:T(4,128)(2,1)} %copy.65), calls=%async_computation.7 | async-start | bytes 917504 | tf_op jit(solution)/shard_map/all_to_all | solution.py:88
  187.8 23.1 %all-to-all-start.1 = ((bf16[16,4,3584]{2,1,0:T(4,128)(2,1)}), bf16[16,4,3584]{2,1,0:T(4,128)(2,1)S(1)}, u32[]{:S(2)}, u32[]{:S(2)}) async-start(bf16[16,4,3584]{2,1,0:T(4,128)(2,1)} %copy.59), calls=%async_computation.1 | async-start | bytes 917504 | tf_op jit(solution)/shard_map/all_to_all | solution.py:88
  196.0 18.7 %copy-start.13 = (s32[2,2,8]{2,1,0:T(2,128)S(1)}, s32[2,2,8]{2,1,0:T(2,128)}, u32[]{:S(2)}) copy-start(s32[2,2,8]{2,1,0:T(2,128)} %param.18) | copy-start | bytes 388
  196.0 18.7 %copy-start.24 = (f32[4,2,8]{2,1,0:T(2,128)S(1)}, f32[4,2,8]{2,1,0:T(2,128)}, u32[]{:S(2)}) copy-start(f32[4,2,8]{2,1,0:T(2,128)} %param.19) | copy-start | bytes 772
  196.0 18.8 %copy-start.30 = (f32[2,64]{1,0:T(2,128)S(1)}, f32[2,64]{1,0:T(2,128)}, u32[]{:S(2)}) copy-start(f32[2,64]{1,0:T(2,128)} %get-tuple-element.17) | copy-start | bytes 1540
  196.0 18.8 %copy-start.35 = (f32[2,64]{1,0:T(2,128)S(1)}, f32[2,64]{1,0:T(2,128)}, u32[]{:S(2)}) copy-start(f32[2,64]{1,0:T(2,128)} %fusion.183) | copy-start | bytes 1540
  196.0 18.8 %copy-start.3 = (bf16[2,256,576]{1,2,0:T(8,128)(2,1)S(1)}, bf16[2,256,576]{1,2,0:T(8,128)(2,1)}, u32[]{:S(2)}) copy-start(bf16[2,256,576]{1,2,0:T(8,128)(2,1)} %param.13) | copy-start | bytes 1769476
  196.0 18.8 %copy-start.11 = (f32[2,64,512]{2,1,0:T(8,128)S(1)}, f32[2,64,512]{2,1,0:T(8,128)}, u32[]{:S(2)}) copy-start(f32[2,64,512]{2,1,0:T(8,128)} %fusion.188) | copy-start | bytes 786436
  196.0 18.8 %copy-start.15 = (f32[2,64]{1,0:T(2,128)S(1)}, f32[2,64]{1,0:T(2,128)}, u32[]{:S(2)}) copy-start(f32[2,64]{1,0:T(2,128)} %copy-done.14) | copy-start | bytes 1540
  196.0 18.8 %copy-start.34 = (f32[2,64]{1,0:T(2,128)S(1)}, f32[2,64]{1,0:T(2,128)}, u32[]{:S(2)}) copy-start(f32[2,64]{1,0:T(2,128)} %copy-done.33) | copy-start | bytes 1540
  196.0 19.1 %copy-start.10 = (f32[2,64,512]{2,1,0:T(8,128)S(1)}, f32[2,64,512]{2,1,0:T(8,128)}, u32[]{:S(2)}) copy-start(f32[2,64,512]{2,1,0:T(8,128)} %fusion.186) | copy-start | bytes 786436
  196.1 19.1 %copy-start.17 = (f32[2,64]{1,0:T(2,128)S(1)}, f32[2,64]{1,0:T(2,128)}, u32[]{:S(2)}) copy-start(f32[2,64]{1,0:T(2,128)} %copy-done.16) | copy-start | bytes 1540
  196.1 19.1 %copy-start.32 = (f32[2,64]{1,0:T(2,128)S(1)}, f32[2,64]{1,0:T(2,128)}, u32[]{:S(2)}) copy-start(f32[2,64]{1,0:T(2,128)} %copy-done.31) | copy-start | bytes 1540
  196.1 19.4 %copy-start.19 = (f32[2,64]{1,0:T(2,128)S(1)}, f32[2,64]{1,0:T(2,128)}, u32[]{:S(2)}) copy-start(f32[2,64]{1,0:T(2,128)} %copy-done.18) | copy-start | bytes 1540
  196.1 19.4 %copy-start.21 = (f32[2,64,4]{1,2,0:T(4,128)S(1)}, f32[2,64,4]{1,2,0:T(4,128)}, u32[]{:S(2)}) copy-start(f32[2,64,4]{1,2,0:T(4,128)} %copy-done.20) | copy-start | bytes 6148
  196.1 19.4 %copy-start.37 = (pred[4]{0:T(512)(128)(4,1)S(1)}, pred[4]{0:T(512)(128)(4,1)}, u32[]{:S(2)}) copy-start(pred[4]{0:T(512)(128)(4,1)} %copy-done.36) | copy-start | bytes 16
  196.1 19.7 %copy-start.7 = (f32[2,64,256]{2,1,0:T(8,128)S(1)}, f32[2,64,256]{2,1,0:T(8,128)}, u32[]{:S(2)}) copy-start(f32[2,64,256]{2,1,0:T(8,128)} %copy-done.6) | copy-start | bytes 393220
  200.7 32.5 %copy-start.29 = (f32[2,64]{1,0:T(2,128)S(1)}, f32[2,64]{1,0:T(2,128)}, u32[]{:S(2)}) copy-start(f32[2,64]{1,0:T(2,128)} %get-tuple-element.62) | copy-start | bytes 1540
  200.7 32.8 %copy-start.28 = (f32[2,64]{1,0:T(2,128)S(1)}, f32[2,64]{1,0:T(2,128)}, u32[]{:S(2)}) copy-start(f32[2,64]{1,0:T(2,128)} %get-tuple-element.9) | copy-start | bytes 1540
  200.8 33.1 %copy-start.27 = (f32[2,64]{1,0:T(2,128)S(1)}, f32[2,64]{1,0:T(2,128)}, u32[]{:S(2)}) copy-start(f32[2,64]{1,0:T(2,128)} %get-tuple-element.60) | copy-start | bytes 1540
  200.8 33.4 %copy-start.26 = (f32[2,64]{1,0:T(2,128)S(1)}, f32[2,64]{1,0:T(2,128)}, u32[]{:S(2)}) copy-start(f32[2,64]{1,0:T(2,128)} %get-tuple-element.13) | copy-start | bytes 1540
  200.8 647.5 %copy-start.9 = (bf16[4,2,3584]{2,1,0:T(2,128)(2,1)S(1)}, bf16[4,2,3584]{2,1,0:T(2,128)(2,1)}, u32[]{:S(2)}) copy-start(bf16[4,2,3584]{2,1,0:T(2,128)(2,1)} %param.16) | copy-start | bytes 172036
  210.9 22.3 %all-to-all-start.3 = ((bf16[16,4,3584]{2,1,0:T(4,128)(2,1)}), bf16[16,4,3584]{2,1,0:T(4,128)(2,1)S(1)}, u32[]{:S(2)}, u32[]{:S(2)}) async-start(bf16[16,4,3584]{2,1,0:T(4,128)(2,1)} %copy.61), calls=%async_computation.3 | async-start | bytes 917504 | tf_op jit(solution)/shard_map/all_to_all | solution.py:88
  848.3 5.2 copy-start.1
  848.3 7.3 copy-start
  (2 other events, 2.3 us)
Sparse Core Ops, SparseCore 0:
  33.3 814.9 all-reduce.2
where the time goes:
time: 896 us; the launch traced here: 894 us
  waiting for transfers between devices  696 us (78%)
  matrix products  101 us (11%)
  starting transfers between devices  33.5 us (4%)
  other arithmetic  30.3 us (3%)
  local copies, waits for them, and re-layouts  16.7 us (2%)
  between operations  16.2 us (2%)
    psum x1, waiting for transfers between devices, from_root(): return lax.psum(kept, axis)  614 us
    dot_general x8, matrix products, expert_apply(): return jnp.dot(hidden_act, down_weight, preferred_element_type=jnp.float32)  47 us
    all_to_all x4, waiting for transfers between devices, mixture(): lax.all_to_all(outputs.astype(jnp.bfloat16), 'expert', split_axis=0, conc...  45.4 us
    all_to_all x4, waiting for transfers between devices, mixture(): lax.all_to_all(buffer, 'expert', split_axis=0, concat_axis=0, tiled=True)  36.7 us
    dot_general x8, matrix products, expert_apply(): jnp.dot(token_rows, gate_weight, preferred_element_type=jnp.float32)  26.2 us
    all_to_all x4, starting transfers between devices, mixture(): lax.all_to_all(buffer, 'expert', split_axis=0, concat_axis=0, tiled=True)  19 us
  transfers between devices with their start and end apart: 9, of which 9 were waited for; matrix products, arithmetic and copies ran while one was open for 9% of the time, Pallas kernels for 0%

commit v1 on v0

v1 whole, which is shorter than its diff:
```python
import functools

import jax
import jax.numpy as jnp
from jax import lax
from jax.experimental import pallas as pl
from jax.experimental.pallas import tpu as pltpu
from jax.sharding import PartitionSpec as P

RANK = 512
SCORE_SCALE = 0.07216878364870322
LANES = 128
PEERS = ("expert", "dp")
MIB = 1 << 20

VMEM = pl.BlockSpec(memory_space=pltpu.VMEM)
SMEM = pl.BlockSpec(memory_space=pltpu.SMEM)
ANY = pl.BlockSpec(memory_space=pl.ANY)


def pack_kernel(experts, hidden_ref, first_ref, second_ref, weights_ref, hot_ref, out_ref):
    steps, rows_dev, width = hidden_ref.shape
    before, _, top = first_ref.shape
    tail = out_ref.shape[1] - width
    column = lax.broadcasted_iota(jnp.int32, (rows_dev, tail), 1)
    rows, marks = [], []
    for step in range(steps):
        if step < before:
            chosen = first_ref[step]
        else:
            chosen = second_ref[step - before]
            for replica in range(hot_ref.shape[0]):
                chosen = jnp.where(chosen == experts + replica, hot_ref[replica], chosen)
        weight = weights_ref[step]
        total = jnp.zeros((rows_dev, tail), jnp.float32)
        for k in range(top):
            picked = chosen[:, k : k + 1]
            here = (column == picked) | (column == picked + experts)
            total = total + jnp.where(here, weight[:, k : k + 1], 0.0)
        high = total.astype(jnp.bfloat16).astype(jnp.float32)
        rows.append(hidden_ref[step].astype(jnp.float32))
        marks.append(jnp.where(column < experts, high, total - high))
    out_ref[:, :width] = jnp.concatenate(rows, axis=0).astype(jnp.bfloat16)
    out_ref[:, width:] = jnp.concatenate(marks, axis=0).astype(jnp.bfloat16)


def attend_kernel(queries_ref, cache_ref, new_ref, lengths_ref, out_ref, keys):
    steps, rows_dev, heads, _ = queries_ref.shape
    slots = cache_ref.shape[1]
    tail = 16
    fresh = [new_ref[t].astype(jnp.float32) for t in range(steps)]
    for b in range(rows_dev):
        keys[0 : slots - tail] = cache_ref[b, 0 : slots - tail]
        last = cache_ref[b, slots - tail : slots].astype(jnp.float32)
        last = jnp.concatenate([last[: tail - steps]] + [f[b : b + 1] for f in fresh], axis=0)
        keys[slots - tail : slots] = last.astype(jnp.bfloat16)
        queries = queries_ref[:, b].reshape(steps * heads, queries_ref.shape[3])
        scores = lax.dot_general(
            queries, keys[...], (((1,), (1,)), ((), ())), preferred_element_type=jnp.float32
        )
        scores = scores * SCORE_SCALE
        place = lax.broadcasted_iota(jnp.int32, scores.shape, 1)
        step = lax.broadcasted_iota(jnp.int32, scores.shape, 0) // heads
        age = place - (slots - steps)
        keep = (place < lengths_ref[b]) | ((age >= 0) & (age <= step))
        scores = jnp.where(keep, scores, -1e30)
        weight = jnp.exp(scores - jnp.max(scores, axis=1, keepdims=True))
        probs = weight / jnp.sum(weight, axis=1, keepdims=True)
        context = jnp.dot(
            probs.astype(jnp.bfloat16), keys[:, :RANK], preferred_element_type=jnp.float32
        )
        out_ref[:, b] = context.astype(jnp.bfloat16).reshape(steps, heads, RANK)


def expert_kernel(experts, tile, *refs):
    x_refs = refs[:4]
    own_ref, gate_hbm, up_hbm, down_hbm, keep_ref, send_ref = refs[4:10]
    x, gate, up, down, hidden, sems = refs[10:]
    width = down_hbm.shape[2]
    units = down_hbm.shape[1]
    parts = units // tile
    columns = width // parts
    copies = []
    for j in range(parts):
        cut = pl.ds(j * tile, tile)
        copies.append(pltpu.make_async_copy(gate_hbm.at[0, :, cut], gate.at[:, cut], sems.at[0, j]))
        copies.append(pltpu.make_async_copy(up_hbm.at[0, :, cut], up.at[:, cut], sems.at[1, j]))
    for j in range(parts):
        cut = pl.ds(j * columns, columns)
        copies.append(
            pltpu.make_async_copy(down_hbm.at[0, :, cut], down.at[:, cut], sems.at[2, j])
        )
    for copy in copies:
        copy.start()
    piece = x_refs[0].shape[0]
    for i, x_ref in enumerate(x_refs):
        x[i * piece : (i + 1) * piece] = x_ref[...]
    own = own_ref[0]
    marks = x[:, width:].astype(jnp.float32)
    column = lax.broadcasted_iota(jnp.int32, marks.shape, 1)
    here = (column == own) | (column == own + experts)
    share = jnp.sum(jnp.where(here, marks, 0.0), axis=1, keepdims=True)
    for j in range(parts):
        cut = slice(j * tile, (j + 1) * tile)
        copies[2 * j].wait()
        gate_act = jnp.dot(x[:, :width], gate[:, cut], preferred_element_type=jnp.float32)
        copies[2 * j + 1].wait()
        up_act = jnp.dot(x[:, :width], up[:, cut], preferred_element_type=jnp.float32)
        act = gate_act / (1.0 + jnp.exp(-gate_act)) * up_act
        hidden[:, cut] = act.astype(jnp.bfloat16)
    half = 2 * piece
    for j in range(parts):
        cut = slice(j * columns, (j + 1) * columns)
        copies[2 * parts + j].wait()
        out = jnp.dot(hidden[...], down[:, cut], preferred_element_type=jnp.float32) * share
        keep_ref[:, cut] = out[:half].astype(jnp.bfloat16)
        send_ref[:, cut] = out[half:].astype(jnp.bfloat16)


def sum_kernel(*refs):
    *in_refs, out_ref = refs
    steps, rows_dev, _ = out_ref.shape
    total = in_refs[0][...].astype(jnp.float32)
    for ref in in_refs[1:]:
        total = total + ref[...].astype(jnp.float32)
    total = total.astype(jnp.bfloat16).astype(jnp.float32)
    for step in range(steps):
        out_ref[step] = total[step * rows_dev : (step + 1) * rows_dev].astype(jnp.bfloat16)


def swap(value, mask):
    size = lax.axis_size(PEERS)
    return lax.ppermute(value, PEERS, [(i, i ^ mask) for i in range(size)])


def per_device(
    queries,
    latent_cache,
    new_latents,
    lengths,
    hidden_in,
    first_routes,
    second_routes,
    route_weights,
    gate_weights,
    up_weights,
    down_weights,
    hot_experts,
):
    experts = lax.axis_size("expert")
    devices = lax.axis_size(PEERS)
    steps, rows_dev, width = hidden_in.shape
    rows = steps * rows_dev
    units = down_weights.shape[1]
    bits = devices.bit_length() - 1
    if first_routes.shape[1] != rows_dev:
        begin = lax.axis_index("dp") * rows_dev
        first_routes = lax.dynamic_slice_in_dim(first_routes, begin, rows_dev, 1)
        second_routes = lax.dynamic_slice_in_dim(second_routes, begin, rows_dev, 1)
        route_weights = lax.dynamic_slice_in_dim(route_weights, begin, rows_dev, 1)

    tail = -(-2 * experts // LANES) * LANES
    packed = pl.pallas_call(
        functools.partial(pack_kernel, experts),
        out_shape=jax.ShapeDtypeStruct((rows, width + tail), jnp.bfloat16),
        in_specs=[VMEM, VMEM, VMEM, VMEM, SMEM],
        out_specs=VMEM,
        compiler_params=pltpu.CompilerParams(vmem_limit_bytes=4 * MIB),
        name="pack",
    )(hidden_in, first_routes, second_routes, route_weights, hot_experts)

    high = devices // 4
    blocks = [packed] + [swap(packed, k * high) for k in range(1, 4)]
    held = jnp.concatenate(blocks, axis=0)
    for bit in range(bits - 3, 1, -1):
        held = jnp.concatenate([held, swap(held, 1 << bit)], axis=0)
    second = swap(held, 2)
    other = swap(held, 1)
    other_second = swap(second, 1)

    count = 4 * held.shape[0]
    half = count // 2
    tile = min(256, units)
    parts = units // tile
    own = lax.axis_index("expert").astype(jnp.int32).reshape(1)
    keep, send = pl.pallas_call(
        functools.partial(expert_kernel, experts, tile),
        out_shape=[jax.ShapeDtypeStruct((half, width), jnp.bfloat16)] * 2,
        in_specs=[VMEM] * 4 + [SMEM] + [ANY] * 3,
        out_specs=[VMEM, VMEM],
        scratch_shapes=[
            pltpu.VMEM((count, width + tail), jnp.bfloat16),
            pltpu.VMEM((width, units), jnp.bfloat16),
            pltpu.VMEM((width, units), jnp.bfloat16),
            pltpu.VMEM((units, width), jnp.bfloat16),
            pltpu.VMEM((count, units), jnp.bfloat16),
            pltpu.SemaphoreType.DMA((3, parts)),
        ],
        compiler_params=pltpu.CompilerParams(vmem_limit_bytes=48 * MIB),
        cost_estimate=pl.CostEstimate(
            flops=6 * count * width * units,
            bytes_accessed=6 * width * units,
            transcendentals=count * units,
        ),
        name="experts",
    )(held, second, other, other_second, own, gate_weights, up_weights, down_weights)

    back = swap(send, 1)
    value = keep.astype(jnp.float32) + back.astype(jnp.float32)
    for bit in range(1, bits - 2):
        size = value.shape[0] // 2
        back = swap(value[size:].astype(jnp.bfloat16), 1 << bit)
        value = value[:size] + back.astype(jnp.float32)
    value = value.astype(jnp.bfloat16)
    pieces = [value[:rows]] + [
        swap(value[k * rows : (k + 1) * rows], k * high) for k in range(1, 4)
    ]
    moe_out = pl.pallas_call(
        sum_kernel,
        out_shape=jax.ShapeDtypeStruct((steps, rows_dev, width), jnp.bfloat16),
        in_specs=[VMEM] * 4,
        out_specs=VMEM,
        compiler_params=pltpu.CompilerParams(vmem_limit_bytes=4 * MIB),
        name="total",
    )(*pieces)

    heads = queries.shape[2]
    context = pl.pallas_call(
        attend_kernel,
        out_shape=jax.ShapeDtypeStruct((steps, rows_dev, heads, RANK), jnp.bfloat16),
        in_specs=[VMEM, VMEM, VMEM, SMEM],
        out_specs=VMEM,
        scratch_shapes=[pltpu.VMEM(latent_cache.shape[1:], jnp.bfloat16)],
        compiler_params=pltpu.CompilerParams(vmem_limit_bytes=16 * MIB),
        cost_estimate=pl.CostEstimate(
            flops=4 * rows_dev * steps * heads * latent_cache.shape[1] * latent_cache.shape[2],
            bytes_accessed=2 * (2 * queries.size + latent_cache.size),
            transcendentals=rows_dev * steps * heads * latent_cache.shape[1],
        ),
        name="attend",
    )(queries, latent_cache, new_latents, lengths)
    return (context, moe_out)


def solution(mesh):
    every = ("groups", "expert", "dp")
    routed = P(None, ("groups", "expert"), None)
    placed = (
        P(None, every, None, None),
        P(every, None, None),
        P(None, every, None),
        P(every),
        P(None, every, None),
        routed,
        routed,
        routed,
        P("expert", None, "dp"),
        P("expert", None, "dp"),
        P("expert", "dp", None),
        P(),
    )
    return jax.shard_map(
        per_device,
        mesh=mesh,
        in_specs=placed,
        out_specs=(P(None, every, None, None), P(None, every, None)),
        check_vma=False,
    )
```

time: 896 us -> 51 us (0.06)
  waiting for transfers between devices: 696 us -> 19.5 us
  matrix products: 101 us -> 0 us
  other arithmetic: 30.3 us -> 0.16 us
  starting transfers between devices: 33.5 us -> 13.8 us
  between operations: 16.2 us -> 0.72 us
  local copies, waits for them, and re-layouts: 16.7 us -> 3.87 us
  Pallas kernels: 0 us -> 12.7 us
    psum x1 -> x0, waiting for transfers between devices: 614 us -> none  [from_root(): return lax.psum(kept, axis)]
    dot_general x44 -> x0, matrix products: 101 us -> none  [the longest x8 47 us: expert_apply(): return jnp.dot(hidden_act, down_weight, preferred_element_type=jnp.float32)]
    all_to_all x8 -> x0, waiting for transfers between devices: 82.1 us -> none  [the longest x4 45.4 us: mixture(): lax.all_to_all(outputs.astype(jnp.bfloat16), 'expert', split_axis=0, conc...]
    all_to_all x8 -> x0, starting transfers between devices: 33.4 us -> none  [the longest x4 19 us: mixture(): lax.all_to_all(buffer, 'expert', split_axis=0, concat_axis=0, tiled=True)]
    squeeze x2 -> x0, other arithmetic: 23.2 us -> none  [the longest x1 14.1 us: per_device(): copied[1][0]]
    ppermute x0 -> x11, waiting for transfers between devices: none -> 19.5 us  [swap(): return lax.ppermute(value, PEERS, [(i, i ^ mask) for i in range(size)])]
    ppermute x0 -> x11, starting transfers between devices: none -> 13.8 us  [swap(): return lax.ppermute(value, PEERS, [(i, i ^ mask) for i in range(size)])]
    pallas_call x0 -> x4, Pallas kernels: none -> 12.7 us  [the longest x1 8.57 us: per_device(): pl.pallas_call(functools.partial(expert_kernel, experts, tile), out_shape...]
  transfers between devices with their start and end apart: 9 -> 11, of which waited for: 9 -> 7; matrix products, arithmetic and copies ran while one was open for 9% -> 1% of each run, Pallas kernels for 0% -> 5%
where the time goes in v1:
time: 51 us; the launch traced here: 50.7 us
  waiting for transfers between devices  19.5 us (38%)
  starting transfers between devices  13.8 us (27%)
  Pallas kernels  12.7 us (25%)
  local copies, waits for them, and re-layouts  3.87 us (8%)
  between operations  0.72 us (1%)
    ppermute x11, waiting for transfers between devices, swap(): return lax.ppermute(value, PEERS, [(i, i ^ mask) for i in range(size)])  19.5 us
    ppermute x11, starting transfers between devices, swap(): return lax.ppermute(value, PEERS, [(i, i ^ mask) for i in range(size)])  13.8 us
    pallas_call x1, Pallas kernels, per_device(): pl.pallas_call(functools.partial(expert_kernel, experts, tile), out_shape...  8.57 us
    unnamed x19, local copies, waits for them, and re-layouts  3.82 us
    pallas_call x1, Pallas kernels, per_device(): pl.pallas_call(attend_kernel, out_shape=jax.ShapeDtypeStruct((steps, rows...  2.71 us
  transfers between devices with their start and end apart: 11, of which 7 were waited for; matrix products, arithmetic and copies ran while one was open for 1% of the time, Pallas kernels for 5%

profile of v1, /device:TPU:0, one launch (start us, length us, event | category | flops | bytes accessed | tf_op | source)
XLA Modules:
  0.0 50.7 jit_solution(2713329205288710852)
XLA Ops:
  0.6 0.0 copy-start.1
  0.6 0.8 %copy-done.1 = bf16[4,2,3584]{2,1,0:T(2,128)(2,1)S(1)} copy-done((bf16[4,2,3584]{2,1,0:T(2,128)(2,1)S(1)}, bf16[4,2,3584]{2,1,0:T(2,128)(2,1)}, u32[]{:S(2)}) %copy-start.1) | copy-done | bytes 57368
  1.5 0.0 copy-start.3
  1.5 0.7 %copy-done.3 = f32[4,2,8]{2,1,0:T(2,128)S(1)} copy-done((f32[4,2,8]{2,1,0:T(2,128)S(1)}, f32[4,2,8]{2,1,0:T(2,128)}, u32[]{:S(2)}) %copy-start.3) | copy-done | bytes 280
  2.1 0.0 copy-start.4
  2.1 0.7 %copy-done.4 = s32[2,2,8]{2,1,0:T(2,128)S(1)} copy-done((s32[2,2,8]{2,1,0:T(2,128)S(1)}, s32[2,2,8]{2,1,0:T(2,128)}, u32[]{:S(2)}) %copy-start.4) | copy-done | bytes 152
  2.8 0.0 copy-start.5
  2.8 0.7 %copy-done.5 = s32[2,2,8]{2,1,0:T(2,128)S(1)} copy-done((s32[2,2,8]{2,1,0:T(2,128)S(1)}, s32[2,2,8]{2,1,0:T(2,128)}, u32[]{:S(2)}) %copy-start.5) | copy-done | bytes 152
  3.5 0.0 copy-start.6
  3.5 0.7 %copy-done.6 = s32[2]{0:T(128)S(1)} copy-done((s32[2]{0:T(128)S(1)}, s32[2]{0:T(128)}, u32[]{:S(2)}) %copy-start.6) | copy-done | bytes 32
  4.2 0.8 %pack.1 = bf16[8,3712]{1,0:T(8,128)(2,1)S(1)} custom-call(bf16[4,2,3584]{2,1,0:T(2,128)(2,1)S(1)} %copy-done.1, s32[2,2,8]{2,1,0:T(2,128)S(1)} %copy-done.4, s32[2,2,8]{2,1,0:T(2,128)S(1)} %copy-done.5, f32[4,2,8]{2,1,0:T(2,128)S(1)} %copy-done.3, s32[2]{0:T(128)S(1)} %copy-done.6), custom_call_target="tpu_custom_call" | custom-call | tf_op jit(solution)/shard_map/pack/pallas_call | solution.py:163
  4.9 5.1 %collective-permute-start.2 = (bf16[8,3712]{1,0:T(8,128)(2,1)S(1)}, bf16[8,3712]{1,0:T(8,128)(2,1)S(1)}, u32[]{:S(2)}, u32[]{:S(2)}) collective-permute-start(bf16[8,3712]{1,0:T(8,128)(2,1)S(1)} %pack.1), channel_id=1, source_target_pairs={{0,12},{1,13},{2,14},{3,15},{4,8},{5,9},{6,10},{7,11},{8,4},{9,5},... | collective-permute-start | bytes 178184 | tf_op jit(solution)/shard_map/ppermute | solution.py:133
  10.0 0.0 collective-permute-start.1
  10.0 0.6 %collective-permute-start = (bf16[8,3712]{1,0:T(8,128)(2,1)S(1)}, bf16[8,3712]{1,0:T(8,128)(2,1)S(1)}, u32[]{:S(2)}, u32[]{:S(2)}) collective-permute-start(bf16[8,3712]{1,0:T(8,128)(2,1)S(1)} %pack.1), channel_id=1, source_target_pairs={{0,4},{1,5},{2,6},{3,7},{4,0},{5,1},{6,2},{7,3},{8,12},{9,13},{10,... | collective-permute-start | bytes 178184 | tf_op jit(solution)/shard_map/ppermute | solution.py:133
  10.7 1.8 %collective-permute-done.2 = bf16[8,3712]{1,0:T(8,128)(2,1)S(1)} collective-permute-done((bf16[8,3712]{1,0:T(8,128)(2,1)S(1)}, bf16[8,3712]{1,0:T(8,128)(2,1)S(1)}, u32[]{:S(2)}, u32[]{:S(2)}) %collective-permute-start.2) | collective-permute-done | bytes 59424 | tf_op jit(solution)/shard_map/ppermute | solution.py:133
  12.5 2.7 %collective-permute-done.1 = bf16[8,3712]{1,0:T(8,128)(2,1)S(1)} collective-permute-done((bf16[8,3712]{1,0:T(8,128)(2,1)S(1)}, bf16[8,3712]{1,0:T(8,128)(2,1)S(1)}, u32[]{:S(2)}, u32[]{:S(2)}) %collective-permute-start.1) | collective-permute-done | bytes 59424 | tf_op jit(solution)/shard_map/ppermute | solution.py:133
  15.2 0.0 collective-permute-done
  15.2 1.7 %collective-permute-start.3 = (bf16[32,3712]{1,0:T(8,128)(2,1)S(1)}, bf16[32,3712]{1,0:T(8,128)(2,1)S(1)}, u32[]{:S(2)}, u32[]{:S(2)}) collective-permute-start(bf16[32,3712]{1,0:T(8,128)(2,1)S(1)} %pad_maximum_fusion.refs_0_), channel_id=1, source_target_pairs={{0,2},{1,3},{2,0},{3,1},{4,6},{5,7},{6,4},{7,5},{8,10},{9,11},{10,... | collective-permute-start | bytes 712712 | tf_op jit(solution)/shard_map/ppermute | solution.py:133
  16.9 0.0 collective-permute-start.4
  16.9 5.3 %collective-permute-done.3.refs_1_ = bf16[32,3712]{1,0:T(8,128)(2,1)S(1)} collective-permute-done((bf16[32,3712]{1,0:T(8,128)(2,1)S(1)}, bf16[32,3712]{1,0:T(8,128)(2,1)S(1)}, u32[]{:S(2)}, u32[]{:S(2)}) %collective-permute-start.3) | collective-permute-done | bytes 237600 | tf_op jit(solution)/shard_map/ppermute | solution.py:133
  22.2 0.0 collective-permute-start.5
  22.2 0.0 collective-permute-done.4.refs_2_
  22.2 1.5 %collective-permute-done.5.refs_3_ = bf16[32,3712]{1,0:T(8,128)(2,1)S(1)} collective-permute-done((bf16[32,3712]{1,0:T(8,128)(2,1)S(1)}, bf16[32,3712]{1,0:T(8,128)(2,1)S(1)}, u32[]{:S(2)}, u32[]{:S(2)}) %collective-permute-start.5) | collective-permute-done | bytes 237600 | tf_op jit(solution)/shard_map/ppermute | solution.py:133
  23.7 0.0 copy-start.8
  23.7 0.0 copy-start
  23.7 0.0 copy-start.2
  23.7 0.0 copy-start.7
  23.7 8.6 %experts.1 = (bf16[64,3584]{1,0:T(8,128)(2,1)S(1)}, bf16[64,3584]{1,0:T(8,128)(2,1)S(1)}) custom-call(bf16[32,3712]{1,0:T(8,128)(2,1)S(1)} %pad_maximum_fusion.refs_0_, bf16[32,3712]{1,0:T(8,128)(2,1)S(1)} %collective-permute-done.3.refs_1_, bf16[32,3712]{1,0:T(8,128)(2,1)S(1)} %collective-permute-done.4.refs_2_, ...), custom_call_target="tpu_custom_call" | custom-call | flops 2818572288 | bytes 22020096 | tf_op jit(solution)/shard_map/experts/pallas_call | solution.py:186
  32.2 0.2 collective-permute-start.6
  32.4 1.7 %collective-permute-done.6 = bf16[64,3584]{1,0:T(8,128)(2,1)S(1)} collective-permute-done((bf16[64,3584]{1,0:T(8,128)(2,1)S(1)}, bf16[64,3584]{1,0:T(8,128)(2,1)S(1)}, u32[]{:S(2)}, u32[]{:S(2)}) %collective-permute-start.6) | collective-permute-done | bytes 458784 | tf_op jit(solution)/shard_map/ppermute | solution.py:133
  34.1 0.1 convert_add_fusion
  34.3 1.7 %collective-permute-start.7 = (bf16[32,3584]{1,0:T(8,128)(2,1)S(1)}, bf16[32,3584]{1,0:T(8,128)(2,1)S(1)}, u32[]{:S(2)}, u32[]{:S(2)}) collective-permute-start(bf16[32,3584]{1,0:T(8,128)(2,1)S(1)} %slice.35), channel_id=1, source_target_pairs={{0,2},{1,3},{2,0},{3,1},{4,6},{5,7},{6,4},{7,5},{8,10},{9,11},{10,... | collective-permute-start | bytes 688136 | tf_op jit(solution)/shard_map/ppermute | solution.py:133
  35.9 6.0 %collective-permute-done.7 = bf16[32,3584]{1,0:T(8,128)(2,1)S(1)} collective-permute-done((bf16[32,3584]{1,0:T(8,128)(2,1)S(1)}, bf16[32,3584]{1,0:T(8,128)(2,1)S(1)}, u32[]{:S(2)}, u32[]{:S(2)}) %collective-permute-start.7) | collective-permute-done | bytes 229408 | tf_op jit(solution)/shard_map/ppermute | solution.py:133
  42.0 2.3 %collective-permute-start.10 = (bf16[8,3584]{1,0:T(8,128)(2,1)S(1)}, bf16[8,3584]{1,0:T(8,128)(2,1)S(1)}, u32[]{:S(2)}, u32[]{:S(2)}) collective-permute-start(bf16[8,3584]{1,0:T(8,128)(2,1)S(1)} %get-tuple-element.6), channel_id=1, source_target_pairs={{0,12},{1,13},{2,14},{3,15},{4,8},{5,9},{6,10},{7,11},{8,4},{9,5},... | collective-permute-start | bytes 172040 | tf_op jit(solution)/shard_map/ppermute | solution.py:133
  44.3 0.0 collective-permute-start.9
  44.3 2.2 %collective-permute-start.8 = (bf16[8,3584]{1,0:T(8,128)(2,1)S(1)}, bf16[8,3584]{1,0:T(8,128)(2,1)S(1)}, u32[]{:S(2)}, u32[]{:S(2)}) collective-permute-start(bf16[8,3584]{1,0:T(8,128)(2,1)S(1)} %get-tuple-element.8), channel_id=1, source_target_pairs={{0,4},{1,5},{2,6},{3,7},{4,0},{5,1},{6,2},{7,3},{8,12},{9,13},{10,... | collective-permute-start | bytes 172040 | tf_op jit(solution)/shard_map/ppermute | solution.py:133
  46.5 0.0 copy-done.8
  46.5 0.3 copy.14.cache_ref
  46.8 0.0 copy-done
  46.8 0.0 copy-done.2
  46.8 0.0 copy-done.7
  46.8 2.7 %attend.1 = bf16[4,2,64,512]{3,2,1,0:T(8,128)(2,1)} custom-call(bf16[4,2,64,576]{3,2,1,0:T(8,128)(2,1)S(1)} %copy-done, bf16[2,256,576]{2,1,0:T(8,128)(2,1)S(1)} %copy.14.cache_ref, bf16[4,2,576]{2,1,0:T(2,128)(2,1)S(1)} %copy-done.2, s32[2]{0:T(128)S(1)} %copy-done.7), custom_call_target="tpu_custom_call" | custom-call | flops 301989888 | bytes 1769472 | tf_op jit(solution)/shard_map/attend/pallas_call | solution.py:228
  49.5 0.0 collective-permute-done.10.refs_3_
  49.5 0.5 %collective-permute-done.9.refs_2_ = bf16[8,3584]{1,0:T(8,128)(2,1)S(1)} collective-permute-done((bf16[8,3584]{1,0:T(8,128)(2,1)S(1)}, bf16[8,3584]{1,0:T(8,128)(2,1)S(1)}, u32[]{:S(2)}, u32[]{:S(2)}) %collective-permute-start.9) | collective-permute-done | bytes 57376 | tf_op jit(solution)/shard_map/ppermute | solution.py:133
  50.1 0.0 collective-permute-done.8.refs_1_
  50.1 0.7 %total.1 = bf16[4,2,3584]{2,1,0:T(2,128)(2,1)} custom-call(bf16[8,3584]{1,0:T(8,128)(2,1)S(1)} %get-tuple-element.9.refs_0_, bf16[8,3584]{1,0:T(8,128)(2,1)S(1)} %collective-permute-done.8.refs_1_, bf16[8,3584]{1,0:T(8,128)(2,1)S(1)} %collective-permute-done.9.refs_2_, bf16[8,3584]{1,0:T(8,128)(2,1)S(1)} %collective-permute-done.10.refs_3_), custom_call_target="tpu_custom_call" | custom-call | tf_op jit(solution)/shard_map/total/pallas_call | solution.py:218
  (4 shorter events, 0.1 us)
Async XLA Ops:
  0.6 0.8 %copy-start.1 = (bf16[4,2,3584]{2,1,0:T(2,128)(2,1)S(1)}, bf16[4,2,3584]{2,1,0:T(2,128)(2,1)}, u32[]{:S(2)}) copy-start(bf16[4,2,3584]{2,1,0:T(2,128)(2,1)} %hidden_ref.1) | copy-start | bytes 172036
  1.5 0.7 %copy-start.3 = (f32[4,2,8]{2,1,0:T(2,128)S(1)}, f32[4,2,8]{2,1,0:T(2,128)}, u32[]{:S(2)}) copy-start(f32[4,2,8]{2,1,0:T(2,128)} %weights_ref.1) | copy-start | bytes 772
  2.1 0.7 %copy-start.4 = (s32[2,2,8]{2,1,0:T(2,128)S(1)}, s32[2,2,8]{2,1,0:T(2,128)}, u32[]{:S(2)}) copy-start(s32[2,2,8]{2,1,0:T(2,128)} %first_ref.1) | copy-start | bytes 388
  2.8 0.7 %copy-start.5 = (s32[2,2,8]{2,1,0:T(2,128)S(1)}, s32[2,2,8]{2,1,0:T(2,128)}, u32[]{:S(2)}) copy-start(s32[2,2,8]{2,1,0:T(2,128)} %second_ref.1) | copy-start | bytes 388
  3.5 0.7 %copy-start.6 = (s32[2]{0:T(128)S(1)}, s32[2]{0:T(128)}, u32[]{:S(2)}) copy-start(s32[2]{0:T(128)} %hot_ref.1) | copy-start | bytes 28
  4.9 7.6 %collective-permute-start.2 = (bf16[8,3712]{1,0:T(8,128)(2,1)S(1)}, bf16[8,3712]{1,0:T(8,128)(2,1)S(1)}, u32[]{:S(2)}, u32[]{:S(2)}) collective-permute-start(bf16[8,3712]{1,0:T(8,128)(2,1)S(1)} %pack.1), channel_id=1, source_target_pairs={{0,12},{1,13},{2,14},{3,15},{4,8},{5,9},{6,10},{7,11},{8,4},{9,5},... | collective-permute-start | bytes 178184 | tf_op jit(solution)/shard_map/ppermute | solution.py:133
  10.0 5.2 %collective-permute-start.1 = (bf16[8,3712]{1,0:T(8,128)(2,1)S(1)}, bf16[8,3712]{1,0:T(8,128)(2,1)S(1)}, u32[]{:S(2)}, u32[]{:S(2)}) collective-permute-start(bf16[8,3712]{1,0:T(8,128)(2,1)S(1)} %pack.1), channel_id=1, source_target_pairs={{0,8},{1,9},{2,10},{3,11},{4,12},{5,13},{6,14},{7,15},{8,0},{9,1},... | collective-permute-start | bytes 178184 | tf_op jit(solution)/shard_map/ppermute | solution.py:133
  10.0 5.2 %collective-permute-start = (bf16[8,3712]{1,0:T(8,128)(2,1)S(1)}, bf16[8,3712]{1,0:T(8,128)(2,1)S(1)}, u32[]{:S(2)}, u32[]{:S(2)}) collective-permute-start(bf16[8,3712]{1,0:T(8,128)(2,1)S(1)} %pack.1), channel_id=1, source_target_pairs={{0,4},{1,5},{2,6},{3,7},{4,0},{5,1},{6,2},{7,3},{8,12},{9,13},{10,... | collective-permute-start | bytes 178184 | tf_op jit(solution)/shard_map/ppermute | solution.py:133
  15.2 6.9 %collective-permute-start.3 = (bf16[32,3712]{1,0:T(8,128)(2,1)S(1)}, bf16[32,3712]{1,0:T(8,128)(2,1)S(1)}, u32[]{:S(2)}, u32[]{:S(2)}) collective-permute-start(bf16[32,3712]{1,0:T(8,128)(2,1)S(1)} %pad_maximum_fusion.refs_0_), channel_id=1, source_target_pairs={{0,2},{1,3},{2,0},{3,1},{4,6},{5,7},{6,4},{7,5},{8,10},{9,11},{10,... | collective-permute-start | bytes 712712 | tf_op jit(solution)/shard_map/ppermute | solution.py:133
  16.9 5.3 %collective-permute-start.4 = (bf16[32,3712]{1,0:T(8,128)(2,1)S(1)}, bf16[32,3712]{1,0:T(8,128)(2,1)S(1)}, u32[]{:S(2)}, u32[]{:S(2)}) collective-permute-start(bf16[32,3712]{1,0:T(8,128)(2,1)S(1)} %pad_maximum_fusion.refs_0_), channel_id=1, source_target_pairs={{0,1},{1,0},{2,3},{3,2},{4,5},{5,4},{6,7},{7,6},{8,9},{9,8},{10,11... | collective-permute-start | bytes 712712 | tf_op jit(solution)/shard_map/ppermute | solution.py:133
  22.2 1.5 %collective-permute-start.5 = (bf16[32,3712]{1,0:T(8,128)(2,1)S(1)}, bf16[32,3712]{1,0:T(8,128)(2,1)S(1)}, u32[]{:S(2)}, u32[]{:S(2)}) collective-permute-start(bf16[32,3712]{1,0:T(8,128)(2,1)S(1)} %collective-permute-done.3.refs_1_), channel_id=1, source_target_pairs={{0,1},{1,0},{2,3},{3,2},{4,5},{5,4},{6,7},{7,6},{8,9},{9,8},{10,11... | collective-permute-start | bytes 712712 | tf_op jit(solution)/shard_map/ppermute | solution.py:133
  23.7 22.8 %copy-start.8 = (bf16[2,256,576]{1,2,0:T(8,128)(2,1)S(1)}, bf16[2,256,576]{1,2,0:T(8,128)(2,1)}, u32[]{:S(2)}) copy-start(bf16[2,256,576]{1,2,0:T(8,128)(2,1)} %param.13) | copy-start | bytes 1769476
  23.7 23.1 %copy-start = (bf16[4,2,64,576]{3,2,1,0:T(8,128)(2,1)S(1)}, bf16[4,2,64,576]{3,2,1,0:T(8,128)(2,1)}, u32[]{:S(2)}) copy-start(bf16[4,2,64,576]{3,2,1,0:T(8,128)(2,1)} %queries_ref.1) | copy-start | bytes 1769476
  23.7 23.1 %copy-start.2 = (bf16[4,2,576]{2,1,0:T(2,128)(2,1)S(1)}, bf16[4,2,576]{2,1,0:T(2,128)(2,1)}, u32[]{:S(2)}) copy-start(bf16[4,2,576]{2,1,0:T(2,128)(2,1)} %new_ref.1) | copy-start | bytes 27652
  23.7 23.2 %copy-start.7 = (s32[2]{0:T(128)S(1)}, s32[2]{0:T(128)}, u32[]{:S(2)}) copy-start(s32[2]{0:T(128)} %lengths_ref.1) | copy-start | bytes 28
  32.2 1.9 %collective-permute-start.6 = (bf16[64,3584]{1,0:T(8,128)(2,1)S(1)}, bf16[64,3584]{1,0:T(8,128)(2,1)S(1)}, u32[]{:S(2)}, u32[]{:S(2)}) collective-permute-start(bf16[64,3584]{1,0:T(8,128)(2,1)S(1)} %get-tuple-element.5), channel_id=1, source_target_pairs={{0,1},{1,0},{2,3},{3,2},{4,5},{5,4},{6,7},{7,6},{8,9},{9,8},{10,11... | collective-permute-start | bytes 1376264 | tf_op jit(solution)/shard_map/ppermute | solution.py:133
  34.3 7.7 %collective-permute-start.7 = (bf16[32,3584]{1,0:T(8,128)(2,1)S(1)}, bf16[32,3584]{1,0:T(8,128)(2,1)S(1)}, u32[]{:S(2)}, u32[]{:S(2)}) collective-permute-start(bf16[32,3584]{1,0:T(8,128)(2,1)S(1)} %slice.35), channel_id=1, source_target_pairs={{0,2},{1,3},{2,0},{3,1},{4,6},{5,7},{6,4},{7,5},{8,10},{9,11},{10,... | collective-permute-start | bytes 688136 | tf_op jit(solution)/shard_map/ppermute | solution.py:133
  42.0 7.5 %collective-permute-start.10 = (bf16[8,3584]{1,0:T(8,128)(2,1)S(1)}, bf16[8,3584]{1,0:T(8,128)(2,1)S(1)}, u32[]{:S(2)}, u32[]{:S(2)}) collective-permute-start(bf16[8,3584]{1,0:T(8,128)(2,1)S(1)} %get-tuple-element.6), channel_id=1, source_target_pairs={{0,12},{1,13},{2,14},{3,15},{4,8},{5,9},{6,10},{7,11},{8,4},{9,5},... | collective-permute-start | bytes 172040 | tf_op jit(solution)/shard_map/ppermute | solution.py:133
  44.3 5.8 %collective-permute-start.9 = (bf16[8,3584]{1,0:T(8,128)(2,1)S(1)}, bf16[8,3584]{1,0:T(8,128)(2,1)S(1)}, u32[]{:S(2)}, u32[]{:S(2)}) collective-permute-start(bf16[8,3584]{1,0:T(8,128)(2,1)S(1)} %get-tuple-element.7), channel_id=1, source_target_pairs={{0,8},{1,9},{2,10},{3,11},{4,12},{5,13},{6,14},{7,15},{8,0},{9,1},... | collective-permute-start | bytes 172040 | tf_op jit(solution)/shard_map/ppermute | solution.py:133
  44.3 5.8 %collective-permute-start.8 = (bf16[8,3584]{1,0:T(8,128)(2,1)S(1)}, bf16[8,3584]{1,0:T(8,128)(2,1)S(1)}, u32[]{:S(2)}, u32[]{:S(2)}) collective-permute-start(bf16[8,3584]{1,0:T(8,128)(2,1)S(1)} %get-tuple-element.8), channel_id=1, source_target_pairs={{0,4},{1,5},{2,6},{3,7},{4,0},{5,1},{6,2},{7,3},{8,12},{9,13},{10,... | collective-permute-start | bytes 172040 | tf_op jit(solution)/shard_map/ppermute | solution.py:133

commit v2 on v1

--- a/solution.py
+++ b/solution.py
@@ -15,10 +15,21 @@
 
 VMEM = pl.BlockSpec(memory_space=pltpu.VMEM)
 SMEM = pl.BlockSpec(memory_space=pltpu.SMEM)
+HBM = pl.BlockSpec(memory_space=pltpu.HBM)
 ANY = pl.BlockSpec(memory_space=pl.ANY)
 
 
-def pack_kernel(experts, hidden_ref, first_ref, second_ref, weights_ref, hot_ref, out_ref):
+def pack_kernel(experts, *refs):
+    sources, out_ref, held, sems = refs[:5], refs[5], refs[6:11], refs[11]
+    copies = [
+        pltpu.make_async_copy(source, target, sems.at[i])
+        for i, (source, target) in enumerate(zip(sources, held))
+    ]
+    for copy in copies:
+        copy.start()
+    for copy in copies:
+        copy.wait()
+    hidden_ref, first_ref, second_ref, weights_ref, hot_ref = held
     steps, rows_dev, width = hidden_ref.shape
     before, _, top = first_ref.shape
     tail = out_ref.shape[1] - width
@@ -44,20 +55,47 @@
     out_ref[:, width:] = jnp.concatenate(marks, axis=0).astype(jnp.bfloat16)
 
 
-def attend_kernel(queries_ref, cache_ref, new_ref, lengths_ref, out_ref, keys):
+def load_kernel(*refs):
+    count = len(refs) // 2
+    copies = [
+        pltpu.make_async_copy(refs[i], refs[count + i], refs[-1].at[i]) for i in range(count)
+    ]
+    for copy in copies:
+        copy.start()
+    for copy in copies:
+        copy.wait()
+
+
+def load(*arrays):
+    return pl.pallas_call(
+        load_kernel,
+        out_shape=[jax.ShapeDtypeStruct(a.shape, a.dtype) for a in arrays],
+        in_specs=[HBM] * len(arrays),
+        out_specs=[VMEM] * len(arrays),
+        scratch_shapes=[pltpu.SemaphoreType.DMA((len(arrays),))],
+        compiler_params=pltpu.CompilerParams(vmem_limit_bytes=4 * MIB),
+        cost_estimate=pl.CostEstimate(
+            flops=0, bytes_accessed=sum(2 * a.size for a in arrays), transcendentals=0
+        ),
+        name="load",
+    )(*(pltpu.with_memory_space_constraint(a, pltpu.HBM) for a in arrays))
+
+
+def attend_kernel(
+    queries_ref, cache_ref, new_ref, lengths_ref, down_hbm, out_ref, down_ref, keys, sem
+):
+    copy = pltpu.make_async_copy(down_hbm, down_ref, sem)
+    copy.start()
     steps, rows_dev, heads, _ = queries_ref.shape
-    slots = cache_ref.shape[1]
-    tail = 16
+    slots = cache_ref.shape[2]
     fresh = [new_ref[t].astype(jnp.float32) for t in range(steps)]
     for b in range(rows_dev):
-        keys[0 : slots - tail] = cache_ref[b, 0 : slots - tail]
-        last = cache_ref[b, slots - tail : slots].astype(jnp.float32)
-        last = jnp.concatenate([last[: tail - steps]] + [f[b : b + 1] for f in fresh], axis=0)
-        keys[slots - tail : slots] = last.astype(jnp.bfloat16)
+        rest = jnp.zeros((slots - steps, keys.shape[0]), jnp.float32)
+        added = jnp.concatenate([rest] + [f[b : b + 1] for f in fresh], axis=0).astype(jnp.bfloat16)
+        spot = lax.broadcasted_iota(jnp.int32, keys.shape, 1)
+        keys[...] = jnp.where(spot < slots - steps, cache_ref[b], added.T)
         queries = queries_ref[:, b].reshape(steps * heads, queries_ref.shape[3])
-        scores = lax.dot_general(
-            queries, keys[...], (((1,), (1,)), ((), ())), preferred_element_type=jnp.float32
-        )
+        scores = jnp.dot(queries, keys[...], preferred_element_type=jnp.float32)
         scores = scores * SCORE_SCALE
         place = lax.broadcasted_iota(jnp.int32, scores.shape, 1)
         step = lax.broadcasted_iota(jnp.int32, scores.shape, 0) // heads
@@ -66,55 +104,62 @@
         scores = jnp.where(keep, scores, -1e30)
         weight = jnp.exp(scores - jnp.max(scores, axis=1, keepdims=True))
         probs = weight / jnp.sum(weight, axis=1, keepdims=True)
-        context = jnp.dot(
-            probs.astype(jnp.bfloat16), keys[:, :RANK], preferred_element_type=jnp.float32
+        context = lax.dot_general(
+            probs.astype(jnp.bfloat16),
+            keys[:RANK],
+            (((1,), (1,)), ((), ())),
+            preferred_element_type=jnp.float32,
         )
         out_ref[:, b] = context.astype(jnp.bfloat16).reshape(steps, heads, RANK)
+    copy.wait()
 
 
 def expert_kernel(experts, tile, *refs):
     x_refs = refs[:4]
-    own_ref, gate_hbm, up_hbm, down_hbm, keep_ref, send_ref = refs[4:10]
-    x, gate, up, down, hidden, sems = refs[10:]
-    width = down_hbm.shape[2]
-    units = down_hbm.shape[1]
+    gate, up, down, keep_ref, send_ref, x, hidden = refs[4:]
+    width = down.shape[2]
+    units = down.shape[1]
     parts = units // tile
     columns = width // parts
-    copies = []
-    for j in range(parts):
-        cut = pl.ds(j * tile, tile)
-        copies.append(pltpu.make_async_copy(gate_hbm.at[0, :, cut], gate.at[:, cut], sems.at[0, j]))
-        copies.append(pltpu.make_async_copy(up_hbm.at[0, :, cut], up.at[:, cut], sems.at[1, j]))
-    for j in range(parts):
-        cut = pl.ds(j * columns, columns)
-        copies.append(
-            pltpu.make_async_copy(down_hbm.at[0, :, cut], down.at[:, cut], sems.at[2, j])
-        )
-    for copy in copies:
-        copy.start()
     piece = x_refs[0].shape[0]
     for i, x_ref in enumerate(x_refs):
         x[i * piece : (i + 1) * piece] = x_ref[...]
-    own = own_ref[0]
+    own = lax.axis_index("expert")
     marks = x[:, width:].astype(jnp.float32)
     column = lax.broadcasted_iota(jnp.int32, marks.shape, 1)
     here = (column == own) | (column == own + experts)
     share = jnp.sum(jnp.where(here, marks, 0.0), axis=1, keepdims=True)
     for j in range(parts):
         cut = slice(j * tile, (j + 1) * tile)
-        copies[2 * j].wait()
-        gate_act = jnp.dot(x[:, :width], gate[:, cut], preferred_element_type=jnp.float32)
-        copies[2 * j + 1].wait()
-        up_act = jnp.dot(x[:, :width], up[:, cut], preferred_element_type=jnp.float32)
+        gate_act = jnp.dot(x[:, :width], gate[0, :, cut], preferred_element_type=jnp.float32)
+        up_act = jnp.dot(x[:, :width], up[0, :, cut], preferred_element_type=jnp.float32)
         act = gate_act / (1.0 + jnp.exp(-gate_act)) * up_act
         hidden[:, cut] = act.astype(jnp.bfloat16)
     half = 2 * piece
     for j in range(parts):
         cut = slice(j * columns, (j + 1) * columns)
-        copies[2 * parts + j].wait()
-        out = jnp.dot(hidden[...], down[:, cut], preferred_element_type=jnp.float32) * share
+        out = jnp.dot(hidden[...], down[0, :, cut], preferred_element_type=jnp.float32) * share
         keep_ref[:, cut] = out[:half].astype(jnp.bfloat16)
         send_ref[:, cut] = out[half:].astype(jnp.bfloat16)
+
+
+def join_kernel(*refs):
+    *in_refs, out_ref = refs
+    size = in_refs[0].shape[0]
+    for i, ref in enumerate(in_refs):
+        out_ref[i * size : (i + 1) * size] = ref[...]
+
+
+def join(blocks):
+    size, width = blocks[0].shape
+    return pl.pallas_call(
+        join_kernel,
+        out_shape=jax.ShapeDtypeStruct((len(blocks) * size, width), blocks[0].dtype),
+        in_specs=[VMEM] * len(blocks),
+        out_specs=VMEM,
+        compiler_params=pltpu.CompilerParams(vmem_limit_bytes=8 * MIB),
+        name="join",
+    )(*blocks)
 
 
 def sum_kernel(*refs):
@@ -160,21 +205,54 @@
         route_weights = lax.dynamic_slice_in_dim(route_weights, begin, rows_dev, 1)
 
     tail = -(-2 * experts // LANES) * LANES
+    inputs = (hidden_in, first_routes, second_routes, route_weights)
     packed = pl.pallas_call(
         functools.partial(pack_kernel, experts),
         out_shape=jax.ShapeDtypeStruct((rows, width + tail), jnp.bfloat16),
-        in_specs=[VMEM, VMEM, VMEM, VMEM, SMEM],
+        in_specs=[HBM] * 5,
         out_specs=VMEM,
+        scratch_shapes=[pltpu.VMEM(a.shape, a.dtype) for a in inputs]
+        + [pltpu.SMEM(hot_experts.shape, jnp.int32), pltpu.SemaphoreType.DMA((5,))],
         compiler_params=pltpu.CompilerParams(vmem_limit_bytes=4 * MIB),
         name="pack",
-    )(hidden_in, first_routes, second_routes, route_weights, hot_experts)
+    )(*(pltpu.with_memory_space_constraint(a, pltpu.HBM) for a in (*inputs, hot_experts)))
 
     high = devices // 4
+    packed, gate_weights, up_weights = lax.optimization_barrier((packed, gate_weights, up_weights))
+    gate_loaded, up_loaded = load(gate_weights, up_weights)
     blocks = [packed] + [swap(packed, k * high) for k in range(1, 4)]
-    held = jnp.concatenate(blocks, axis=0)
+    held = join(blocks)
     for bit in range(bits - 3, 1, -1):
-        held = jnp.concatenate([held, swap(held, 1 << bit)], axis=0)
+        held = join([held, swap(held, 1 << bit)])
+    held, gate_loaded, up_loaded, lengths = lax.optimization_barrier(
+        (held, gate_loaded, up_loaded, lengths)
+    )
     second = swap(held, 2)
+    heads = queries.shape[2]
+    context, down_loaded = pl.pallas_call(
+        attend_kernel,
+        out_shape=[
+            jax.ShapeDtypeStruct((steps, rows_dev, heads, RANK), jnp.bfloat16),
+            jax.ShapeDtypeStruct(down_weights.shape, jnp.bfloat16),
+        ],
+        in_specs=[VMEM, VMEM, VMEM, SMEM, HBM],
+        out_specs=[VMEM, VMEM],
+        scratch_shapes=[pltpu.VMEM(latent_cache.shape[:0:-1], jnp.bfloat16), pltpu.SemaphoreType.DMA],
+        compiler_params=pltpu.CompilerParams(vmem_limit_bytes=16 * MIB),
+        cost_estimate=pl.CostEstimate(
+            flops=4 * rows_dev * steps * heads * latent_cache.shape[1] * latent_cache.shape[2],
+            bytes_accessed=2 * (2 * queries.size + latent_cache.size),
+            transcendentals=rows_dev * steps * heads * latent_cache.shape[1],
+        ),
+        name="attend",
+    )(
+        queries,
+        jnp.swapaxes(latent_cache, 1, 2),
+        new_latents,
+        lengths,
+        pltpu.with_memory_space_constraint(down_weights, pltpu.HBM),
+    )
+    second, context, down_loaded = lax.optimization_barrier((second, context, down_loaded))
     other = swap(held, 1)
     other_second = swap(second, 1)
 
@@ -182,28 +260,31 @@
     half = count // 2
     tile = min(256, units)
     parts = units // tile
-    own = lax.axis_index("expert").astype(jnp.int32).reshape(1)
     keep, send = pl.pallas_call(
         functools.partial(expert_kernel, experts, tile),
         out_shape=[jax.ShapeDtypeStruct((half, width), jnp.bfloat16)] * 2,
-        in_specs=[VMEM] * 4 + [SMEM] + [ANY] * 3,
+        in_specs=[VMEM] * 7,
         out_specs=[VMEM, VMEM],
         scratch_shapes=[
             pltpu.VMEM((count, width + tail), jnp.bfloat16),
-            pltpu.VMEM((width, units), jnp.bfloat16),
-            pltpu.VMEM((width, units), jnp.bfloat16),
-            pltpu.VMEM((units, width), jnp.bfloat16),
             pltpu.VMEM((count, units), jnp.bfloat16),
-            pltpu.SemaphoreType.DMA((3, parts)),
         ],
-        compiler_params=pltpu.CompilerParams(vmem_limit_bytes=48 * MIB),
+        compiler_params=pltpu.CompilerParams(vmem_limit_bytes=24 * MIB),
         cost_estimate=pl.CostEstimate(
             flops=6 * count * width * units,
             bytes_accessed=6 * width * units,
             transcendentals=count * units,
         ),
         name="experts",
-    )(held, second, other, other_second, own, gate_weights, up_weights, down_weights)
+    )(
+        held,
+        second,
+        other,
+        other_second,
+        gate_loaded,
+        up_loaded,
+        down_loaded,
+    )
 
     back = swap(send, 1)
     value = keep.astype(jnp.float32) + back.astype(jnp.float32)
@@ -224,21 +305,6 @@
         name="total",
     )(*pieces)
 
-    heads = queries.shape[2]
-    context = pl.pallas_call(
-        attend_kernel,
-        out_shape=jax.ShapeDtypeStruct((steps, rows_dev, heads, RANK), jnp.bfloat16),
-        in_specs=[VMEM, VMEM, VMEM, SMEM],
-        out_specs=VMEM,
-        scratch_shapes=[pltpu.VMEM(latent_cache.shape[1:], jnp.bfloat16)],
-        compiler_params=pltpu.CompilerParams(vmem_limit_bytes=16 * MIB),
-        cost_estimate=pl.CostEstimate(
-            flops=4 * rows_dev * steps * heads * latent_cache.shape[1] * latent_cache.shape[2],
-            bytes_accessed=2 * (2 * queries.size + latent_cache.size),
-            transcendentals=rows_dev * steps * heads * latent_cache.shape[1],
-        ),
-        name="attend",
-    )(queries, latent_cache, new_latents, lengths)
     return (context, moe_out)
 
 

time: 51 us -> 44 us (0.86)
  waiting for transfers between devices: 19.5 us -> 14.3 us
  local copies, waits for them, and re-layouts: 3.87 us -> 0.07 us
  Pallas kernels: 12.7 us -> 14.8 us
    pallas_call x1 -> x3, Pallas kernels: 2.71 us -> 9.64 us  [the longest x1 5.19 us: load(): pl.pallas_call(load_kernel, out_shape=[jax.ShapeDtypeStruct(a.shape, a.dt...]
    ppermute x11, waiting for transfers between devices: 19.5 us -> 14.3 us  [swap(): return lax.ppermute(value, PEERS, [(i, i ^ mask) for i in range(size)])]
    pallas_call x1, Pallas kernels: 8.57 us -> 3.4 us  [per_device(): pl.pallas_call(functools.partial(expert_kernel, experts, tile), out_shape...]
    unnamed x19 -> x8, local copies, waits for them, and re-layouts: 3.82 us -> 0.03 us
  transfers between devices with their start and end apart: 11 -> 11, of which waited for: 7 -> 6; matrix products, arithmetic and copies ran while one was open for 1% -> 0% of each run, Pallas kernels for 5% -> 22%
where the time goes in v2:
time: 44 us; the launch traced here: 43.8 us
  Pallas kernels  14.8 us (34%)
  waiting for transfers between devices  14.3 us (32%)
  starting transfers between devices  13.7 us (31%)
  between operations  0.78 us (2%)
    ppermute x11, waiting for transfers between devices, swap(): return lax.ppermute(value, PEERS, [(i, i ^ mask) for i in range(size)])  14.3 us
    ppermute x11, starting transfers between devices, swap(): return lax.ppermute(value, PEERS, [(i, i ^ mask) for i in range(size)])  13.7 us
    pallas_call x1, Pallas kernels, load(): pl.pallas_call(load_kernel, out_shape=[jax.ShapeDtypeStruct(a.shape, a.dt...  5.19 us
    pallas_call x1, Pallas kernels, per_device(): pl.pallas_call(attend_kernel, out_shape=[jax.ShapeDtypeStruct((steps, row...  4.44 us
    pallas_call x1, Pallas kernels, per_device(): pl.pallas_call(functools.partial(expert_kernel, experts, tile), out_shape...  3.4 us
    pallas_call x1, Pallas kernels, per_device(): pl.pallas_call(functools.partial(pack_kernel, experts), out_shape=jax.Sha...  1.1 us
  transfers between devices with their start and end apart: 11, of which 6 were waited for; matrix products, arithmetic and copies ran while one was open for 0% of the time, Pallas kernels for 22%

profile of v2, /device:TPU:0, one launch (start us, length us, event | category | flops | bytes accessed | tf_op | source)
XLA Modules:
  0.0 43.8 jit_solution(12052334120076120009)
XLA Ops:
  0.6 1.1 %pack.1.refs_0_ = bf16[8,3712]{1,0:T(8,128)(2,1)S(1)} custom-call(bf16[4,2,3584]{2,1,0:T(2,128)(2,1)} %refs_0_.1, s32[2,2,8]{2,1,0:T(2,128)} %refs_1_.1, s32[2,2,8]{2,1,0:T(2,128)} %refs_2_.1, f32[4,2,8]{2,1,0:T(2,128)} %refs_3_.1, s32[2]{0:T(128)} %refs_4_.1), custom_call_target="tpu_custom_call" | custom-call | tf_op jit(solution)/shard_map/pack/pallas_call | solution.py:209
  1.7 0.0 copy-start
  1.8 0.0 copy-start.1
  1.8 0.0 copy-start.2
  1.8 0.0 copy-start.3
  1.8 5.1 %collective-permute-start.2 = (bf16[8,3712]{1,0:T(8,128)(2,1)S(1)}, bf16[8,3712]{1,0:T(8,128)(2,1)S(1)}, u32[]{:S(2)}, u32[]{:S(2)}) collective-permute-start(bf16[8,3712]{1,0:T(8,128)(2,1)S(1)} %pack.1.refs_0_), channel_id=1, source_target_pairs={{0,12},{1,13},{2,14},{3,15},{4,8},{5,9},{6,10},{7,11},{8,4},{9,5},... | collective-permute-start | bytes 178184 | tf_op jit(solution)/shard_map/ppermute | solution.py:178
  6.9 0.0 collective-permute-start.1
  6.9 0.6 %collective-permute-start = (bf16[8,3712]{1,0:T(8,128)(2,1)S(1)}, bf16[8,3712]{1,0:T(8,128)(2,1)S(1)}, u32[]{:S(2)}, u32[]{:S(2)}) collective-permute-start(bf16[8,3712]{1,0:T(8,128)(2,1)S(1)} %pack.1.refs_0_), channel_id=1, source_target_pairs={{0,4},{1,5},{2,6},{3,7},{4,0},{5,1},{6,2},{7,3},{8,12},{9,13},{10,... | collective-permute-start | bytes 178184 | tf_op jit(solution)/shard_map/ppermute | solution.py:178
  7.5 5.2 %load.1 = (bf16[1,3584,1024]{2,1,0:T(8,128)(2,1)S(1)}, bf16[1,3584,1024]{2,1,0:T(8,128)(2,1)S(1)}) custom-call(bf16[1,3584,1024]{2,1,0:T(8,128)(2,1)} %refs_0_.2, bf16[1,3584,1024]{2,1,0:T(8,128)(2,1)} %refs_1_.2), custom_call_target="tpu_custom_call" | custom-call | bytes 14680064 | tf_op jit(solution)/shard_map/load/pallas_call | solution.py:70
  12.7 0.0 collective-permute-done.2.refs_3_
  12.8 0.0 collective-permute-done.1.refs_2_
  12.8 0.0 collective-permute-done.refs_1_
  12.8 1.7 %collective-permute-start.3 = (bf16[32,3712]{1,0:T(8,128)(2,1)S(1)}, bf16[32,3712]{1,0:T(8,128)(2,1)S(1)}, u32[]{:S(2)}, u32[]{:S(2)}) collective-permute-start(bf16[32,3712]{1,0:T(8,128)(2,1)S(1)} %join.1.refs_0_), channel_id=1, source_target_pairs={{0,2},{1,3},{2,0},{3,1},{4,6},{5,7},{6,4},{7,5},{8,10},{9,11},{10,... | collective-permute-start | bytes 712712 | tf_op jit(solution)/shard_map/ppermute | solution.py:178
  14.5 0.0 collective-permute-start.4
  14.5 0.0 copy-done
  14.5 0.0 copy-done.1
  14.5 0.0 copy-done.2
  14.6 0.0 copy-done.3
  14.6 4.4 %attend.1 = (bf16[4,2,64,512]{3,2,1,0:T(8,128)(2,1)}, bf16[1,1024,3584]{2,1,0:T(8,128)(2,1)S(1)}) custom-call(bf16[4,2,64,576]{3,2,1,0:T(8,128)(2,1)S(1)} %copy-done, bf16[2,576,256]{2,1,0:T(8,128)(2,1)S(1)} %bitcast.1, bf16[4,2,576]{2,1,0:T(2,128)(2,1)S(1)} %copy-done.2, s32[2]{0:T(128)S(1)} %copy-done.3, bf16[1,1024,3584]{2,1,0:T(8,128)(2,1)} %down_hbm.1), custom_call_target="tpu_custom_call" | custom-call | flops 301989888 | bytes 1769472 | tf_op jit(solution)/shard_map/attend/pallas_call | solution.py:232
  19.0 0.8 %collective-permute-done.3.refs_1_ = bf16[32,3712]{1,0:T(8,128)(2,1)S(1)} collective-permute-done((bf16[32,3712]{1,0:T(8,128)(2,1)S(1)}, bf16[32,3712]{1,0:T(8,128)(2,1)S(1)}, u32[]{:S(2)}, u32[]{:S(2)}) %collective-permute-start.3) | collective-permute-done | bytes 237600 | tf_op jit(solution)/shard_map/ppermute | solution.py:178
  19.8 0.0 collective-permute-start.5
  19.8 0.0 collective-permute-done.4.refs_2_
  19.8 1.5 %collective-permute-done.5.refs_3_ = bf16[32,3712]{1,0:T(8,128)(2,1)S(1)} collective-permute-done((bf16[32,3712]{1,0:T(8,128)(2,1)S(1)}, bf16[32,3712]{1,0:T(8,128)(2,1)S(1)}, u32[]{:S(2)}, u32[]{:S(2)}) %collective-permute-start.5) | collective-permute-done | bytes 237600 | tf_op jit(solution)/shard_map/ppermute | solution.py:178
  21.3 3.4 %experts.1 = (bf16[64,3584]{1,0:T(8,128)(2,1)S(1)}, bf16[64,3584]{1,0:T(8,128)(2,1)S(1)}) custom-call(bf16[32,3712]{1,0:T(8,128)(2,1)S(1)} %join.1.refs_0_, bf16[32,3712]{1,0:T(8,128)(2,1)S(1)} %collective-permute-done.3.refs_1_, bf16[32,3712]{1,0:T(8,128)(2,1)S(1)} %collective-permute-done.4.refs_2_, bf16[32,3712]{1,0:T(8,128)(2,1)S(1)} %collective-permute-done.5.refs_3_, ...), custom_call_target="tpu_custom_call" | custom-call | flops 2818572288 | bytes 22020096 | tf_op jit(solution)/shard_map/experts/pallas_call | solution.py:263
  24.7 0.2 collective-permute-start.6
  24.9 1.7 %collective-permute-done.6 = bf16[64,3584]{1,0:T(8,128)(2,1)S(1)} collective-permute-done((bf16[64,3584]{1,0:T(8,128)(2,1)S(1)}, bf16[64,3584]{1,0:T(8,128)(2,1)S(1)}, u32[]{:S(2)}, u32[]{:S(2)}) %collective-permute-start.6) | collective-permute-done | bytes 458784 | tf_op jit(solution)/shard_map/ppermute | solution.py:178
  26.6 0.1 convert_add_fusion
  26.7 1.6 %collective-permute-start.7 = (bf16[32,3584]{1,0:T(8,128)(2,1)S(1)}, bf16[32,3584]{1,0:T(8,128)(2,1)S(1)}, u32[]{:S(2)}, u32[]{:S(2)}) collective-permute-start(bf16[32,3584]{1,0:T(8,128)(2,1)S(1)} %slice.35), channel_id=1, source_target_pairs={{0,2},{1,3},{2,0},{3,1},{4,6},{5,7},{6,4},{7,5},{8,10},{9,11},{10,... | collective-permute-start | bytes 688136 | tf_op jit(solution)/shard_map/ppermute | solution.py:178
  28.3 6.1 %collective-permute-done.7 = bf16[32,3584]{1,0:T(8,128)(2,1)S(1)} collective-permute-done((bf16[32,3584]{1,0:T(8,128)(2,1)S(1)}, bf16[32,3584]{1,0:T(8,128)(2,1)S(1)}, u32[]{:S(2)}, u32[]{:S(2)}) %collective-permute-start.7) | collective-permute-done | bytes 229408 | tf_op jit(solution)/shard_map/ppermute | solution.py:178
  34.5 0.1 fusion
  34.5 3.5 %collective-permute-start.10 = (bf16[8,3584]{1,0:T(8,128)(2,1)S(1)}, bf16[8,3584]{1,0:T(8,128)(2,1)S(1)}, u32[]{:S(2)}, u32[]{:S(2)}) collective-permute-start(bf16[8,3584]{1,0:T(8,128)(2,1)S(1)} %get-tuple-element.34), channel_id=1, source_target_pairs={{0,12},{1,13},{2,14},{3,15},{4,8},{5,9},{6,10},{7,11},{8,4},{9,5},... | collective-permute-start | bytes 172040 | tf_op jit(solution)/shard_map/ppermute | solution.py:178
  38.1 0.0 collective-permute-start.9
  38.1 0.9 %collective-permute-start.8 = (bf16[8,3584]{1,0:T(8,128)(2,1)S(1)}, bf16[8,3584]{1,0:T(8,128)(2,1)S(1)}, u32[]{:S(2)}, u32[]{:S(2)}) collective-permute-start(bf16[8,3584]{1,0:T(8,128)(2,1)S(1)} %get-tuple-element.36), channel_id=1, source_target_pairs={{0,4},{1,5},{2,6},{3,7},{4,0},{5,1},{6,2},{7,3},{8,12},{9,13},{10,... | collective-permute-start | bytes 172040 | tf_op jit(solution)/shard_map/ppermute | solution.py:178
  39.0 1.8 %collective-permute-done.10.refs_3_ = bf16[8,3584]{1,0:T(8,128)(2,1)S(1)} collective-permute-done((bf16[8,3584]{1,0:T(8,128)(2,1)S(1)}, bf16[8,3584]{1,0:T(8,128)(2,1)S(1)}, u32[]{:S(2)}, u32[]{:S(2)}) %collective-permute-start.10) | collective-permute-done | bytes 57376 | tf_op jit(solution)/shard_map/ppermute | solution.py:178
  40.8 2.3 %collective-permute-done.9.refs_2_ = bf16[8,3584]{1,0:T(8,128)(2,1)S(1)} collective-permute-done((bf16[8,3584]{1,0:T(8,128)(2,1)S(1)}, bf16[8,3584]{1,0:T(8,128)(2,1)S(1)}, u32[]{:S(2)}, u32[]{:S(2)}) %collective-permute-start.9) | collective-permute-done | bytes 57376 | tf_op jit(solution)/shard_map/ppermute | solution.py:178
  43.1 0.0 collective-permute-done.8.refs_1_
  43.1 0.7 %total.1 = bf16[4,2,3584]{2,1,0:T(2,128)(2,1)} custom-call(bf16[8,3584]{1,0:T(8,128)(2,1)S(1)} %get-tuple-element.37.refs_0_, bf16[8,3584]{1,0:T(8,128)(2,1)S(1)} %collective-permute-done.8.refs_1_, bf16[8,3584]{1,0:T(8,128)(2,1)S(1)} %collective-permute-done.9.refs_2_, bf16[8,3584]{1,0:T(8,128)(2,1)S(1)} %collective-permute-done.10.refs_3_), custom_call_target="tpu_custom_call" | custom-call | tf_op jit(solution)/shard_map/total/pallas_call | solution.py:299
  (3 shorter events, 0.1 us)
Async XLA Ops:
  1.7 12.8 %copy-start = (bf16[4,2,64,576]{3,2,1,0:T(8,128)(2,1)S(1)}, bf16[4,2,64,576]{3,2,1,0:T(8,128)(2,1)}, u32[]{:S(2)}) copy-start(bf16[4,2,64,576]{3,2,1,0:T(8,128)(2,1)} %queries_ref.1) | copy-start | bytes 1769476
  1.8 12.8 %copy-start.1 = (bf16[2,256,576]{1,2,0:T(8,128)(2,1)S(1)}, bf16[2,256,576]{1,2,0:T(8,128)(2,1)}, u32[]{:S(2)}) copy-start(bf16[2,256,576]{1,2,0:T(8,128)(2,1)} %param.13) | copy-start | bytes 1769476
  1.8 12.8 %copy-start.2 = (bf16[4,2,576]{2,1,0:T(2,128)(2,1)S(1)}, bf16[4,2,576]{2,1,0:T(2,128)(2,1)}, u32[]{:S(2)}) copy-start(bf16[4,2,576]{2,1,0:T(2,128)(2,1)} %new_ref.1) | copy-start | bytes 27652
  1.8 12.8 %copy-start.3 = (s32[2]{0:T(128)S(1)}, s32[2]{0:T(128)}, u32[]{:S(2)}) copy-start(s32[2]{0:T(128)} %lengths_ref) | copy-start | bytes 28
  1.8 11.0 %collective-permute-start.2 = (bf16[8,3712]{1,0:T(8,128)(2,1)S(1)}, bf16[8,3712]{1,0:T(8,128)(2,1)S(1)}, u32[]{:S(2)}, u32[]{:S(2)}) collective-permute-start(bf16[8,3712]{1,0:T(8,128)(2,1)S(1)} %pack.1.refs_0_), channel_id=1, source_target_pairs={{0,12},{1,13},{2,14},{3,15},{4,8},{5,9},{6,10},{7,11},{8,4},{9,5},... | collective-permute-start | bytes 178184 | tf_op jit(solution)/shard_map/ppermute | solution.py:178
  6.9 5.9 %collective-permute-start.1 = (bf16[8,3712]{1,0:T(8,128)(2,1)S(1)}, bf16[8,3712]{1,0:T(8,128)(2,1)S(1)}, u32[]{:S(2)}, u32[]{:S(2)}) collective-permute-start(bf16[8,3712]{1,0:T(8,128)(2,1)S(1)} %pack.1.refs_0_), channel_id=1, source_target_pairs={{0,8},{1,9},{2,10},{3,11},{4,12},{5,13},{6,14},{7,15},{8,0},{9,1},... | collective-permute-start | bytes 178184 | tf_op jit(solution)/shard_map/ppermute | solution.py:178
  6.9 5.9 %collective-permute-start = (bf16[8,3712]{1,0:T(8,128)(2,1)S(1)}, bf16[8,3712]{1,0:T(8,128)(2,1)S(1)}, u32[]{:S(2)}, u32[]{:S(2)}) collective-permute-start(bf16[8,3712]{1,0:T(8,128)(2,1)S(1)} %pack.1.refs_0_), channel_id=1, source_target_pairs={{0,4},{1,5},{2,6},{3,7},{4,0},{5,1},{6,2},{7,3},{8,12},{9,13},{10,... | collective-permute-start | bytes 178184 | tf_op jit(solution)/shard_map/ppermute | solution.py:178
  12.8 7.0 %collective-permute-start.3 = (bf16[32,3712]{1,0:T(8,128)(2,1)S(1)}, bf16[32,3712]{1,0:T(8,128)(2,1)S(1)}, u32[]{:S(2)}, u32[]{:S(2)}) collective-permute-start(bf16[32,3712]{1,0:T(8,128)(2,1)S(1)} %join.1.refs_0_), channel_id=1, source_target_pairs={{0,2},{1,3},{2,0},{3,1},{4,6},{5,7},{6,4},{7,5},{8,10},{9,11},{10,... | collective-permute-start | bytes 712712 | tf_op jit(solution)/shard_map/ppermute | solution.py:178
  14.5 5.3 %collective-permute-start.4 = (bf16[32,3712]{1,0:T(8,128)(2,1)S(1)}, bf16[32,3712]{1,0:T(8,128)(2,1)S(1)}, u32[]{:S(2)}, u32[]{:S(2)}) collective-permute-start(bf16[32,3712]{1,0:T(8,128)(2,1)S(1)} %join.1.refs_0_), channel_id=1, source_target_pairs={{0,1},{1,0},{2,3},{3,2},{4,5},{5,4},{6,7},{7,6},{8,9},{9,8},{10,11... | collective-permute-start | bytes 712712 | tf_op jit(solution)/shard_map/ppermute | solution.py:178
  19.8 1.5 %collective-permute-start.5 = (bf16[32,3712]{1,0:T(8,128)(2,1)S(1)}, bf16[32,3712]{1,0:T(8,128)(2,1)S(1)}, u32[]{:S(2)}, u32[]{:S(2)}) collective-permute-start(bf16[32,3712]{1,0:T(8,128)(2,1)S(1)} %collective-permute-done.3.refs_1_), channel_id=1, source_target_pairs={{0,1},{1,0},{2,3},{3,2},{4,5},{5,4},{6,7},{7,6},{8,9},{9,8},{10,11... | collective-permute-start | bytes 712712 | tf_op jit(solution)/shard_map/ppermute | solution.py:178
  24.7 1.9 %collective-permute-start.6 = (bf16[64,3584]{1,0:T(8,128)(2,1)S(1)}, bf16[64,3584]{1,0:T(8,128)(2,1)S(1)}, u32[]{:S(2)}, u32[]{:S(2)}) collective-permute-start(bf16[64,3584]{1,0:T(8,128)(2,1)S(1)} %get-tuple-element.33), channel_id=1, source_target_pairs={{0,1},{1,0},{2,3},{3,2},{4,5},{5,4},{6,7},{7,6},{8,9},{9,8},{10,11... | collective-permute-start | bytes 1376264 | tf_op jit(solution)/shard_map/ppermute | solution.py:178
  26.7 7.7 %collective-permute-start.7 = (bf16[32,3584]{1,0:T(8,128)(2,1)S(1)}, bf16[32,3584]{1,0:T(8,128)(2,1)S(1)}, u32[]{:S(2)}, u32[]{:S(2)}) collective-permute-start(bf16[32,3584]{1,0:T(8,128)(2,1)S(1)} %slice.35), channel_id=1, source_target_pairs={{0,2},{1,3},{2,0},{3,1},{4,6},{5,7},{6,4},{7,5},{8,10},{9,11},{10,... | collective-permute-start | bytes 688136 | tf_op jit(solution)/shard_map/ppermute | solution.py:178
  34.5 6.3 %collective-permute-start.10 = (bf16[8,3584]{1,0:T(8,128)(2,1)S(1)}, bf16[8,3584]{1,0:T(8,128)(2,1)S(1)}, u32[]{:S(2)}, u32[]{:S(2)}) collective-permute-start(bf16[8,3584]{1,0:T(8,128)(2,1)S(1)} %get-tuple-element.34), channel_id=1, source_target_pairs={{0,12},{1,13},{2,14},{3,15},{4,8},{5,9},{6,10},{7,11},{8,4},{9,5},... | collective-permute-start | bytes 172040 | tf_op jit(solution)/shard_map/ppermute | solution.py:178
  38.1 5.1 %collective-permute-start.9 = (bf16[8,3584]{1,0:T(8,128)(2,1)S(1)}, bf16[8,3584]{1,0:T(8,128)(2,1)S(1)}, u32[]{:S(2)}, u32[]{:S(2)}) collective-permute-start(bf16[8,3584]{1,0:T(8,128)(2,1)S(1)} %get-tuple-element.35), channel_id=1, source_target_pairs={{0,8},{1,9},{2,10},{3,11},{4,12},{5,13},{6,14},{7,15},{8,0},{9,1},... | collective-permute-start | bytes 172040 | tf_op jit(solution)/shard_map/ppermute | solution.py:178
  38.1 5.1 %collective-permute-start.8 = (bf16[8,3584]{1,0:T(8,128)(2,1)S(1)}, bf16[8,3584]{1,0:T(8,128)(2,1)S(1)}, u32[]{:S(2)}, u32[]{:S(2)}) collective-permute-start(bf16[8,3584]{1,0:T(8,128)(2,1)S(1)} %get-tuple-element.36), channel_id=1, source_target_pairs={{0,4},{1,5},{2,6},{3,7},{4,0},{5,1},{6,2},{7,3},{8,12},{9,13},{10,... | collective-permute-start | bytes 172040 | tf_op jit(solution)/shard_map/ppermute | solution.py:178

commit v3 on v2

--- a/solution.py
+++ b/solution.py
@@ -55,37 +55,7 @@
     out_ref[:, width:] = jnp.concatenate(marks, axis=0).astype(jnp.bfloat16)
 
 
-def load_kernel(*refs):
-    count = len(refs) // 2
-    copies = [
-        pltpu.make_async_copy(refs[i], refs[count + i], refs[-1].at[i]) for i in range(count)
-    ]
-    for copy in copies:
-        copy.start()
-    for copy in copies:
-        copy.wait()
-
-
-def load(*arrays):
-    return pl.pallas_call(
-        load_kernel,
-        out_shape=[jax.ShapeDtypeStruct(a.shape, a.dtype) for a in arrays],
-        in_specs=[HBM] * len(arrays),
-        out_specs=[VMEM] * len(arrays),
-        scratch_shapes=[pltpu.SemaphoreType.DMA((len(arrays),))],
-        compiler_params=pltpu.CompilerParams(vmem_limit_bytes=4 * MIB),
-        cost_estimate=pl.CostEstimate(
-            flops=0, bytes_accessed=sum(2 * a.size for a in arrays), transcendentals=0
-        ),
-        name="load",
-    )(*(pltpu.with_memory_space_constraint(a, pltpu.HBM) for a in arrays))
-
-
-def attend_kernel(
-    queries_ref, cache_ref, new_ref, lengths_ref, down_hbm, out_ref, down_ref, keys, sem
-):
-    copy = pltpu.make_async_copy(down_hbm, down_ref, sem)
-    copy.start()
+def attend_kernel(queries_ref, cache_ref, new_ref, lengths_ref, out_ref, keys):
     steps, rows_dev, heads, _ = queries_ref.shape
     slots = cache_ref.shape[2]
     fresh = [new_ref[t].astype(jnp.float32) for t in range(steps)]
@@ -111,12 +81,11 @@
             preferred_element_type=jnp.float32,
         )
         out_ref[:, b] = context.astype(jnp.bfloat16).reshape(steps, heads, RANK)
-    copy.wait()
-
-
-def expert_kernel(experts, tile, *refs):
-    x_refs = refs[:4]
-    gate, up, down, keep_ref, send_ref, x, hidden = refs[4:]
+
+
+def expert_kernel(experts, tile, pieces, *refs):
+    x_refs, refs = refs[:pieces], refs[pieces:]
+    gate, up, down, keep_far, send_far, keep_near, send_near, x, hidden = refs
     width = down.shape[2]
     units = down.shape[1]
     parts = units // tile
@@ -135,12 +104,12 @@
         up_act = jnp.dot(x[:, :width], up[0, :, cut], preferred_element_type=jnp.float32)
         act = gate_act / (1.0 + jnp.exp(-gate_act)) * up_act
         hidden[:, cut] = act.astype(jnp.bfloat16)
-    half = 2 * piece
+    quarter = keep_far.shape[0]
     for j in range(parts):
         cut = slice(j * columns, (j + 1) * columns)
         out = jnp.dot(hidden[...], down[0, :, cut], preferred_element_type=jnp.float32) * share
-        keep_ref[:, cut] = out[:half].astype(jnp.bfloat16)
-        send_ref[:, cut] = out[half:].astype(jnp.bfloat16)
+        for i, ref in enumerate((keep_near, keep_far, send_near, send_far)):
+            ref[:, cut] = out[i * quarter : (i + 1) * quarter].astype(jnp.bfloat16)
 
 
 def join_kernel(*refs):
@@ -158,6 +127,7 @@
         in_specs=[VMEM] * len(blocks),
         out_specs=VMEM,
         compiler_params=pltpu.CompilerParams(vmem_limit_bytes=8 * MIB),
+        cost_estimate=pl.CostEstimate(flops=10000000000, bytes_accessed=0, transcendentals=0),
         name="join",
     )(*blocks)
 
@@ -176,6 +146,13 @@
 def swap(value, mask):
     size = lax.axis_size(PEERS)
     return lax.ppermute(value, PEERS, [(i, i ^ mask) for i in range(size)])
+
+
+def add(*values):
+    total = values[0].astype(jnp.float32)
+    for value in values[1:]:
+        total = total + value.astype(jnp.float32)
+    return total.astype(jnp.bfloat16)
 
 
 def per_device(
@@ -218,26 +195,55 @@
     )(*(pltpu.with_memory_space_constraint(a, pltpu.HBM) for a in (*inputs, hot_experts)))
 
     high = devices // 4
-    packed, gate_weights, up_weights = lax.optimization_barrier((packed, gate_weights, up_weights))
-    gate_loaded, up_loaded = load(gate_weights, up_weights)
-    blocks = [packed] + [swap(packed, k * high) for k in range(1, 4)]
-    held = join(blocks)
-    for bit in range(bits - 3, 1, -1):
-        held = join([held, swap(held, 1 << bit)])
-    held, gate_loaded, up_loaded, lengths = lax.optimization_barrier(
-        (held, gate_loaded, up_loaded, lengths)
-    )
-    second = swap(held, 2)
+    base = packed
+    for bit in range(2, bits - 2):
+        base = join([base, swap(base, 1 << bit)])
+    size = base.shape[0]
+    third = swap(base, 3 * high)
+    second = swap(base, 2 * high)
+    first = swap(base, high)
+    near = join([base, first])
+    far = join([second, third])
+    near_y = swap(near, 2)
+    far_y = swap(far, 2)
+    parts = [near, far, near_y, far_y]
+    parts = parts + [swap(part, 1) for part in parts]
+
+    count = 16 * size
+    tile = min(256, units)
+    half = jax.ShapeDtypeStruct((4 * size, width), jnp.bfloat16)
+    keep_far, send_far, keep_near, send_near = pl.pallas_call(
+        functools.partial(expert_kernel, experts, tile, len(parts)),
+        out_shape=[half] * 4,
+        in_specs=[VMEM] * (len(parts) + 3),
+        out_specs=[VMEM] * 4,
+        scratch_shapes=[
+            pltpu.VMEM((count, width + tail), jnp.bfloat16),
+            pltpu.VMEM((count, units), jnp.bfloat16),
+        ],
+        compiler_params=pltpu.CompilerParams(vmem_limit_bytes=24 * MIB),
+        cost_estimate=pl.CostEstimate(
+            flops=6 * count * width * units,
+            bytes_accessed=6 * width * units,
+            transcendentals=count * units,
+        ),
+        name="experts",
+    )(*parts, gate_weights, up_weights, down_weights)
+
+    far = add(keep_far, swap(send_far, 1))
+    near = add(keep_near, swap(send_near, 1))
+    far_third, far_second, far_first = far[3 * size :], far[2 * size : 3 * size], far[: 2 * size]
+    far_third, lengths = lax.optimization_barrier((far_third, lengths))
+    third = swap(far_third, 2)
+    second = swap(far_second, 2)
+    first = swap(far_first, 2)
     heads = queries.shape[2]
-    context, down_loaded = pl.pallas_call(
+    context = pl.pallas_call(
         attend_kernel,
-        out_shape=[
-            jax.ShapeDtypeStruct((steps, rows_dev, heads, RANK), jnp.bfloat16),
-            jax.ShapeDtypeStruct(down_weights.shape, jnp.bfloat16),
-        ],
-        in_specs=[VMEM, VMEM, VMEM, SMEM, HBM],
-        out_specs=[VMEM, VMEM],
-        scratch_shapes=[pltpu.VMEM(latent_cache.shape[:0:-1], jnp.bfloat16), pltpu.SemaphoreType.DMA],
+        out_shape=jax.ShapeDtypeStruct((steps, rows_dev, heads, RANK), jnp.bfloat16),
+        in_specs=[VMEM, VMEM, VMEM, SMEM],
+        out_specs=VMEM,
+        scratch_shapes=[pltpu.VMEM(latent_cache.shape[:0:-1], jnp.bfloat16)],
         compiler_params=pltpu.CompilerParams(vmem_limit_bytes=16 * MIB),
         cost_estimate=pl.CostEstimate(
             flops=4 * rows_dev * steps * heads * latent_cache.shape[1] * latent_cache.shape[2],
@@ -250,61 +256,24 @@
         jnp.swapaxes(latent_cache, 1, 2),
         new_latents,
         lengths,
-        pltpu.with_memory_space_constraint(down_weights, pltpu.HBM),
     )
-    second, context, down_loaded = lax.optimization_barrier((second, context, down_loaded))
-    other = swap(held, 1)
-    other_second = swap(second, 1)
-
-    count = 4 * held.shape[0]
-    half = count // 2
-    tile = min(256, units)
-    parts = units // tile
-    keep, send = pl.pallas_call(
-        functools.partial(expert_kernel, experts, tile),
-        out_shape=[jax.ShapeDtypeStruct((half, width), jnp.bfloat16)] * 2,
-        in_specs=[VMEM] * 7,
-        out_specs=[VMEM, VMEM],
-        scratch_shapes=[
-            pltpu.VMEM((count, width + tail), jnp.bfloat16),
-            pltpu.VMEM((count, units), jnp.bfloat16),
-        ],
-        compiler_params=pltpu.CompilerParams(vmem_limit_bytes=24 * MIB),
-        cost_estimate=pl.CostEstimate(
-            flops=6 * count * width * units,
-            bytes_accessed=6 * width * units,
-            transcendentals=count * units,
-        ),
-        name="experts",
-    )(
-        held,
-        second,
-        other,
-        other_second,
-        gate_loaded,
-        up_loaded,
-        down_loaded,
-    )
-
-    back = swap(send, 1)
-    value = keep.astype(jnp.float32) + back.astype(jnp.float32)
-    for bit in range(1, bits - 2):
-        size = value.shape[0] // 2
-        back = swap(value[size:].astype(jnp.bfloat16), 1 << bit)
-        value = value[:size] + back.astype(jnp.float32)
-    value = value.astype(jnp.bfloat16)
-    pieces = [value[:rows]] + [
-        swap(value[k * rows : (k + 1) * rows], k * high) for k in range(1, 4)
-    ]
+    first, context = lax.optimization_barrier((first, context))
+    third = swap(add(near[3 * size :], third), 3 * high)
+    second = swap(add(near[2 * size : 3 * size], second), 2 * high)
+    total = add(near[: 2 * size], first)
+    pieces = [total[:size], swap(total[size:], high), second, third]
+    for bit in range(bits - 3, 1, -1):
+        value = add(*pieces)
+        middle = value.shape[0] // 2
+        pieces = [value[:middle], swap(value[middle:], 1 << bit)]
     moe_out = pl.pallas_call(
         sum_kernel,
         out_shape=jax.ShapeDtypeStruct((steps, rows_dev, width), jnp.bfloat16),
-        in_specs=[VMEM] * 4,
+        in_specs=[VMEM] * len(pieces),
         out_specs=VMEM,
         compiler_params=pltpu.CompilerParams(vmem_limit_bytes=4 * MIB),
         name="total",
     )(*pieces)
-
     return (context, moe_out)
 
 

time: 44 us -> 39.6 us (0.900)
  Pallas kernels: 14.8 us -> 7.84 us
  starting transfers between devices: 13.7 us -> 18.1 us
  waiting for transfers between devices: 14.3 us -> 12.3 us
    pallas_call x3 -> x2, Pallas kernels: 13 us -> 6.05 us  [the longest x1 3.32 us: per_device(): pl.pallas_call(functools.partial(expert_kernel, experts, tile, len(parts)...]
    ppermute x11 -> x17, starting transfers between devices: 13.7 us -> 18.1 us  [swap(): return lax.ppermute(value, PEERS, [(i, i ^ mask) for i in range(size)])]
    ppermute x11 -> x17, waiting for transfers between devices: 14.3 us -> 12.3 us  [swap(): return lax.ppermute(value, PEERS, [(i, i ^ mask) for i in range(size)])]
  transfers between devices with their start and end apart: 11 -> 17, of which waited for: 6 -> 7; matrix products, arithmetic and copies ran while one was open for 0% -> 1% of each run, Pallas kernels for 22% -> 7%
where the time goes in v3:
time: 39.6 us; the launch traced here: 39.4 us
  starting transfers between devices  18.1 us (46%)
  waiting for transfers between devices  12.3 us (31%)
  Pallas kernels  7.84 us (20%)
  between operations  0.87 us (2%)
    ppermute x17, starting transfers between devices, swap(): return lax.ppermute(value, PEERS, [(i, i ^ mask) for i in range(size)])  18.1 us
    ppermute x17, waiting for transfers between devices, swap(): return lax.ppermute(value, PEERS, [(i, i ^ mask) for i in range(size)])  12.3 us
    pallas_call x1, Pallas kernels, per_device(): pl.pallas_call(functools.partial(expert_kernel, experts, tile, len(parts)...  3.32 us
    pallas_call x1, Pallas kernels, per_device(): pl.pallas_call(attend_kernel, out_shape=jax.ShapeDtypeStruct((steps, rows...  2.74 us
    pallas_call x1, Pallas kernels, per_device(): pl.pallas_call(functools.partial(pack_kernel, experts), out_shape=jax.Sha...  1.1 us
  transfers between devices with their start and end apart: 17, of which 7 were waited for; matrix products, arithmetic and copies ran while one was open for 1% of the time, Pallas kernels for 7%

profile of v3, /device:TPU:0, one launch (start us, length us, event | category | flops | bytes accessed | tf_op | source)
XLA Modules:
  0.0 39.4 jit_solution(10537214609045365186)
XLA Ops:
  0.6 1.1 %pack.1.refs_0_ = bf16[8,3712]{1,0:T(8,128)(2,1)S(1)} custom-call(bf16[4,2,3584]{2,1,0:T(2,128)(2,1)} %refs_0_.1, s32[2,2,8]{2,1,0:T(2,128)} %refs_1_.1, s32[2,2,8]{2,1,0:T(2,128)} %refs_2_.1, f32[4,2,8]{2,1,0:T(2,128)} %refs_3_.1, s32[2]{0:T(128)} %refs_4_.1), custom_call_target="tpu_custom_call" | custom-call | tf_op jit(solution)/shard_map/pack/pallas_call | solution.py:186
  1.7 3.1 %collective-permute-start = (bf16[8,3712]{1,0:T(8,128)(2,1)S(1)}, bf16[8,3712]{1,0:T(8,128)(2,1)S(1)}, u32[]{:S(2)}, u32[]{:S(2)}) collective-permute-start(bf16[8,3712]{1,0:T(8,128)(2,1)S(1)} %pack.1.refs_0_), channel_id=1, source_target_pairs={{0,4},{1,5},{2,6},{3,7},{4,0},{5,1},{6,2},{7,3},{8,12},{9,13},{10,... | collective-permute-start | bytes 178184 | tf_op jit(solution)/shard_map/ppermute | solution.py:148
  4.8 2.5 %collective-permute-start.2 = (bf16[8,3712]{1,0:T(8,128)(2,1)S(1)}, bf16[8,3712]{1,0:T(8,128)(2,1)S(1)}, u32[]{:S(2)}, u32[]{:S(2)}) collective-permute-start(bf16[8,3712]{1,0:T(8,128)(2,1)S(1)} %pack.1.refs_0_), channel_id=1, source_target_pairs={{0,12},{1,13},{2,14},{3,15},{4,8},{5,9},{6,10},{7,11},{8,4},{9,5},... | collective-permute-start | bytes 178184 | tf_op jit(solution)/shard_map/ppermute | solution.py:148
  7.3 0.1 collective-permute-start.1
  7.4 0.0 collective-permute-done.refs_1_
  7.5 0.0 slice-start.1
  7.5 0.0 slice-start.3
  7.5 0.0 slice-start.5
  7.5 1.6 %collective-permute-start.3 = (bf16[16,3712]{1,0:T(8,128)(2,1)S(1)}, bf16[16,3712]{1,0:T(8,128)(2,1)S(1)}, u32[]{:S(2)}, u32[]{:S(2)}) collective-permute-start(bf16[16,3712]{1,0:T(8,128)(2,1)S(1)} %join.2.refs_0_), channel_id=1, source_target_pairs={{0,2},{1,3},{2,0},{3,1},{4,6},{5,7},{6,4},{7,5},{8,10},{9,11},{10,... | collective-permute-start | bytes 356360 | tf_op jit(solution)/shard_map/ppermute | solution.py:148
  9.1 2.5 %collective-permute-done.2.refs_1_ = bf16[8,3712]{1,0:T(8,128)(2,1)S(1)} collective-permute-done((bf16[8,3712]{1,0:T(8,128)(2,1)S(1)}, bf16[8,3712]{1,0:T(8,128)(2,1)S(1)}, u32[]{:S(2)}, u32[]{:S(2)}) %collective-permute-start.2) | collective-permute-done | bytes 59424 | tf_op jit(solution)/shard_map/ppermute | solution.py:148
  11.6 1.7 %collective-permute-done.1.refs_0_ = bf16[8,3712]{1,0:T(8,128)(2,1)S(1)} collective-permute-done((bf16[8,3712]{1,0:T(8,128)(2,1)S(1)}, bf16[8,3712]{1,0:T(8,128)(2,1)S(1)}, u32[]{:S(2)}, u32[]{:S(2)}) %collective-permute-start.1) | collective-permute-done | bytes 59424 | tf_op jit(solution)/shard_map/ppermute | solution.py:148
  13.3 0.0 copy-start
  13.3 0.0 copy-start.1
  13.3 0.0 copy-start.2
  13.3 0.0 copy-start.3
  13.4 1.6 %collective-permute-start.4 = (bf16[16,3712]{1,0:T(8,128)(2,1)S(1)}, bf16[16,3712]{1,0:T(8,128)(2,1)S(1)}, u32[]{:S(2)}, u32[]{:S(2)}) collective-permute-start(bf16[16,3712]{1,0:T(8,128)(2,1)S(1)} %join.3.refs_1_), channel_id=1, source_target_pairs={{0,2},{1,3},{2,0},{3,1},{4,6},{5,7},{6,4},{7,5},{8,10},{9,11},{10,... | collective-permute-start | bytes 356360 | tf_op jit(solution)/shard_map/ppermute | solution.py:148
  14.9 0.0 collective-permute-start.5
  14.9 0.5 %collective-permute-start.6 = (bf16[16,3712]{1,0:T(8,128)(2,1)S(1)}, bf16[16,3712]{1,0:T(8,128)(2,1)S(1)}, u32[]{:S(2)}, u32[]{:S(2)}) collective-permute-start(bf16[16,3712]{1,0:T(8,128)(2,1)S(1)} %join.3.refs_1_), channel_id=1, source_target_pairs={{0,1},{1,0},{2,3},{3,2},{4,5},{5,4},{6,7},{7,6},{8,9},{9,8},{10,11... | collective-permute-start | bytes 356360 | tf_op jit(solution)/shard_map/ppermute | solution.py:148
  15.4 0.0 collective-permute-done.3.refs_2_
  15.5 0.0 collective-permute-start.7
  15.5 2.8 %collective-permute-done.4.refs_3_ = bf16[16,3712]{1,0:T(8,128)(2,1)S(1)} collective-permute-done((bf16[16,3712]{1,0:T(8,128)(2,1)S(1)}, bf16[16,3712]{1,0:T(8,128)(2,1)S(1)}, u32[]{:S(2)}, u32[]{:S(2)}) %collective-permute-start.4) | collective-permute-done | bytes 118816 | tf_op jit(solution)/shard_map/ppermute | solution.py:148
  18.3 0.0 collective-permute-start.8
  18.3 0.0 collective-permute-done.5.refs_4_
  18.3 0.0 collective-permute-done.6.refs_5_
  18.3 0.0 collective-permute-done.7.refs_6_
  18.3 1.3 %collective-permute-done.8.refs_7_ = bf16[16,3712]{1,0:T(8,128)(2,1)S(1)} collective-permute-done((bf16[16,3712]{1,0:T(8,128)(2,1)S(1)}, bf16[16,3712]{1,0:T(8,128)(2,1)S(1)}, u32[]{:S(2)}, u32[]{:S(2)}) %collective-permute-start.8) | collective-permute-done | bytes 118816 | tf_op jit(solution)/shard_map/ppermute | solution.py:148
  19.6 0.0 slice-done.2
  19.7 3.3 %experts.1 = (bf16[32,3584]{1,0:T(8,128)(2,1)S(1)}, bf16[32,3584]{1,0:T(8,128)(2,1)S(1)}, bf16[32,3584]{1,0:T(8,128)(2,1)S(1)}, bf16[32,3584]{1,0:T(8,128)(2,1)S(1)}) custom-call(bf16[16,3712]{1,0:T(8,128)(2,1)S(1)} %join.2.refs_0_, bf16[16,3712]{1,0:T(8,128)(2,1)S(1)} %join.3.refs_1_, bf16[16,3712]{1,0:T(8,128)(2,1)S(1)} %collective-permute-done.3.refs_2_, ...), custom_call_target="tpu_custom_call" | custom-call | flops 2818572288 | bytes 22020096 | tf_op jit(solution)/shard_map/experts/pallas_call | solution.py:215
  23.0 0.2 collective-permute-start.9
  23.2 0.4 collective-permute-start.11
  23.6 1.0 %collective-permute-done.9 = bf16[32,3584]{1,0:T(8,128)(2,1)S(1)} collective-permute-done((bf16[32,3584]{1,0:T(8,128)(2,1)S(1)}, bf16[32,3584]{1,0:T(8,128)(2,1)S(1)}, u32[]{:S(2)}, u32[]{:S(2)}) %collective-permute-start.9) | collective-permute-done | bytes 229408 | tf_op jit(solution)/shard_map/ppermute | solution.py:148
  24.5 0.1 add_convert_fusion.1
  24.6 1.6 %collective-permute-start.15 = (bf16[8,3584]{1,0:T(8,128)(2,1)S(1)}, bf16[8,3584]{1,0:T(8,128)(2,1)S(1)}, u32[]{:S(2)}, u32[]{:S(2)}) collective-permute-start(bf16[8,3584]{1,0:T(8,128)(2,1)S(1)} %get-tuple-element.17), channel_id=1, source_target_pairs={{0,2},{1,3},{2,0},{3,1},{4,6},{5,7},{6,4},{7,5},{8,10},{9,11},{10,... | collective-permute-start | bytes 172040 | tf_op jit(solution)/shard_map/ppermute | solution.py:148
  26.2 0.5 %collective-permute-start.13 = (bf16[8,3584]{1,0:T(8,128)(2,1)S(1)}, bf16[8,3584]{1,0:T(8,128)(2,1)S(1)}, u32[]{:S(2)}, u32[]{:S(2)}) collective-permute-start(bf16[8,3584]{1,0:T(8,128)(2,1)S(1)} %get-tuple-element.20), channel_id=1, source_target_pairs={{0,2},{1,3},{2,0},{3,1},{4,6},{5,7},{6,4},{7,5},{8,10},{9,11},{10,... | collective-permute-start | bytes 172040 | tf_op jit(solution)/shard_map/ppermute | solution.py:148
  26.7 1.5 %collective-permute-start.10 = (bf16[16,3584]{1,0:T(8,128)(2,1)S(1)}, bf16[16,3584]{1,0:T(8,128)(2,1)S(1)}, u32[]{:S(2)}, u32[]{:S(2)}) collective-permute-start(bf16[16,3584]{1,0:T(8,128)(2,1)S(1)} %slice.32), channel_id=1, source_target_pairs={{0,2},{1,3},{2,0},{3,1},{4,6},{5,7},{6,4},{7,5},{8,10},{9,11},{10,... | collective-permute-start | bytes 344072 | tf_op jit(solution)/shard_map/ppermute | solution.py:148
  28.3 0.0 collective-permute-done.11
  28.3 0.1 add_convert_fusion
  28.4 2.7 %attend.1 = bf16[4,2,64,512]{3,2,1,0:T(8,128)(2,1)} custom-call(bf16[4,2,64,576]{3,2,1,0:T(8,128)(2,1)S(1)} %copy-done, bf16[2,576,256]{2,1,0:T(8,128)(2,1)S(1)} %bitcast.7, bf16[4,2,576]{2,1,0:T(2,128)(2,1)S(1)} %copy-done.2, s32[2]{0:T(128)S(1)} %copy-done.3), custom_call_target="tpu_custom_call" | custom-call | flops 301989888 | bytes 1769472 | tf_op jit(solution)/shard_map/attend/pallas_call | solution.py:241
  31.1 0.0 collective-permute-done.15
  31.1 0.0 collective-permute-done.13
  31.1 2.5 %collective-permute-start.16 = (bf16[8,3584]{1,0:T(8,128)(2,1)S(1)}, bf16[8,3584]{1,0:T(8,128)(2,1)S(1)}, u32[]{:S(2)}, u32[]{:S(2)}) collective-permute-start(bf16[8,3584]{1,0:T(8,128)(2,1)S(1)} %get-tuple-element.18), channel_id=1, source_target_pairs={{0,12},{1,13},{2,14},{3,15},{4,8},{5,9},{6,10},{7,11},{8,4},{9,5},... | collective-permute-start | bytes 172040 | tf_op jit(solution)/shard_map/ppermute | solution.py:148
  33.6 0.0 collective-permute-start.14
  33.6 0.0 collective-permute-done.10
  33.7 2.0 %collective-permute-start.12 = (bf16[8,3584]{1,0:T(8,128)(2,1)S(1)}, bf16[8,3584]{1,0:T(8,128)(2,1)S(1)}, u32[]{:S(2)}, u32[]{:S(2)}) collective-permute-start(bf16[8,3584]{1,0:T(8,128)(2,1)S(1)} %get-tuple-element.22), channel_id=1, source_target_pairs={{0,4},{1,5},{2,6},{3,7},{4,0},{5,1},{6,2},{7,3},{8,12},{9,13},{10,... | collective-permute-start | bytes 172040 | tf_op jit(solution)/shard_map/ppermute | solution.py:148
  35.7 1.6 %collective-permute-done.16.refs_3_ = bf16[8,3584]{1,0:T(8,128)(2,1)S(1)} collective-permute-done((bf16[8,3584]{1,0:T(8,128)(2,1)S(1)}, bf16[8,3584]{1,0:T(8,128)(2,1)S(1)}, u32[]{:S(2)}, u32[]{:S(2)}) %collective-permute-start.16) | collective-permute-done | bytes 57376 | tf_op jit(solution)/shard_map/ppermute | solution.py:148
  37.3 1.5 %collective-permute-done.14.refs_2_ = bf16[8,3584]{1,0:T(8,128)(2,1)S(1)} collective-permute-done((bf16[8,3584]{1,0:T(8,128)(2,1)S(1)}, bf16[8,3584]{1,0:T(8,128)(2,1)S(1)}, u32[]{:S(2)}, u32[]{:S(2)}) %collective-permute-start.14) | collective-permute-done | bytes 57376 | tf_op jit(solution)/shard_map/ppermute | solution.py:148
  38.8 0.0 collective-permute-done.12.refs_1_
  38.8 0.7 %total.1 = bf16[4,2,3584]{2,1,0:T(2,128)(2,1)} custom-call(bf16[8,3584]{1,0:T(8,128)(2,1)S(1)} %get-tuple-element.23.refs_0_, bf16[8,3584]{1,0:T(8,128)(2,1)S(1)} %collective-permute-done.12.refs_1_, bf16[8,3584]{1,0:T(8,128)(2,1)S(1)} %collective-permute-done.14.refs_2_, bf16[8,3584]{1,0:T(8,128)(2,1)S(1)} %collective-permute-done.16.refs_3_), custom_call_target="tpu_custom_call" | custom-call | tf_op jit(solution)/shard_map/total/pallas_call | solution.py:269
  (22 shorter events, 0.1 us)
Async XLA Ops:
  1.7 5.7 %collective-permute-start = (bf16[8,3712]{1,0:T(8,128)(2,1)S(1)}, bf16[8,3712]{1,0:T(8,128)(2,1)S(1)}, u32[]{:S(2)}, u32[]{:S(2)}) collective-permute-start(bf16[8,3712]{1,0:T(8,128)(2,1)S(1)} %pack.1.refs_0_), channel_id=1, source_target_pairs={{0,4},{1,5},{2,6},{3,7},{4,0},{5,1},{6,2},{7,3},{8,12},{9,13},{10,... | collective-permute-start | bytes 178184 | tf_op jit(solution)/shard_map/ppermute | solution.py:148
  4.8 6.7 %collective-permute-start.2 = (bf16[8,3712]{1,0:T(8,128)(2,1)S(1)}, bf16[8,3712]{1,0:T(8,128)(2,1)S(1)}, u32[]{:S(2)}, u32[]{:S(2)}) collective-permute-start(bf16[8,3712]{1,0:T(8,128)(2,1)S(1)} %pack.1.refs_0_), channel_id=1, source_target_pairs={{0,12},{1,13},{2,14},{3,15},{4,8},{5,9},{6,10},{7,11},{8,4},{9,5},... | collective-permute-start | bytes 178184 | tf_op jit(solution)/shard_map/ppermute | solution.py:148
  7.3 6.0 %collective-permute-start.1 = (bf16[8,3712]{1,0:T(8,128)(2,1)S(1)}, bf16[8,3712]{1,0:T(8,128)(2,1)S(1)}, u32[]{:S(2)}, u32[]{:S(2)}) collective-permute-start(bf16[8,3712]{1,0:T(8,128)(2,1)S(1)} %pack.1.refs_0_), channel_id=1, source_target_pairs={{0,8},{1,9},{2,10},{3,11},{4,12},{5,13},{6,14},{7,15},{8,0},{9,1},... | collective-permute-start | bytes 178184 | tf_op jit(solution)/shard_map/ppermute | solution.py:148
  7.4 12.2 %slice-start = ((s8[7340032]{0:T(1024)(128)(4,1)}), s8[4194304]{0:T(1024)(128)(4,1)S(1)}, s32[]{:S(2)}) async-start(s8[7340032]{0:T(1024)(128)(4,1)} %bitcast.1), calls=%async_computation | async-start | bytes 8388608
  7.4 12.2 %slice-start.2 = ((s8[7340032]{0:T(1024)(128)(4,1)}), s8[4194304]{0:T(1024)(128)(4,1)S(1)}, s32[]{:S(2)}) async-start(s8[7340032]{0:T(1024)(128)(4,1)} %bitcast.3), calls=%async_computation.2 | async-start | bytes 8388608
  7.4 12.2 %slice-start.4 = ((s8[7340032]{0:T(1024)(128)(4,1)}), s8[4194304]{0:T(1024)(128)(4,1)S(1)}, s32[]{:S(2)}) async-start(s8[7340032]{0:T(1024)(128)(4,1)} %bitcast.5), calls=%async_computation.4 | async-start | bytes 8388608
  7.5 12.1 %slice-start.1 = ((s8[7340032]{0:T(1024)(128)(4,1)}), s8[3145728]{0:T(1024)(128)(4,1)S(1)}, s32[]{:S(2)}) async-start(s8[7340032]{0:T(1024)(128)(4,1)} %bitcast.1), calls=%async_computation.1 | async-start | bytes 6291456
  7.5 12.1 %slice-start.3 = ((s8[7340032]{0:T(1024)(128)(4,1)}), s8[3145728]{0:T(1024)(128)(4,1)S(1)}, s32[]{:S(2)}) async-start(s8[7340032]{0:T(1024)(128)(4,1)} %bitcast.3), calls=%async_computation.3 | async-start | bytes 6291456
  7.5 12.1 %slice-start.5 = ((s8[7340032]{0:T(1024)(128)(4,1)}), s8[3145728]{0:T(1024)(128)(4,1)S(1)}, s32[]{:S(2)}) async-start(s8[7340032]{0:T(1024)(128)(4,1)} %bitcast.5), calls=%async_computation.5 | async-start | bytes 6291456
  7.5 8.0 %collective-permute-start.3 = (bf16[16,3712]{1,0:T(8,128)(2,1)S(1)}, bf16[16,3712]{1,0:T(8,128)(2,1)S(1)}, u32[]{:S(2)}, u32[]{:S(2)}) collective-permute-start(bf16[16,3712]{1,0:T(8,128)(2,1)S(1)} %join.2.refs_0_), channel_id=1, source_target_pairs={{0,2},{1,3},{2,0},{3,1},{4,6},{5,7},{6,4},{7,5},{8,10},{9,11},{10,... | collective-permute-start | bytes 356360 | tf_op jit(solution)/shard_map/ppermute | solution.py:148
  13.3 15.0 %copy-start = (bf16[4,2,64,576]{3,2,1,0:T(8,128)(2,1)S(1)}, bf16[4,2,64,576]{3,2,1,0:T(8,128)(2,1)}, u32[]{:S(2)}) copy-start(bf16[4,2,64,576]{3,2,1,0:T(8,128)(2,1)} %queries_ref.1) | copy-start | bytes 1769476
  13.3 15.0 %copy-start.1 = (bf16[2,256,576]{1,2,0:T(8,128)(2,1)S(1)}, bf16[2,256,576]{1,2,0:T(8,128)(2,1)}, u32[]{:S(2)}) copy-start(bf16[2,256,576]{1,2,0:T(8,128)(2,1)} %param.13) | copy-start | bytes 1769476
  13.3 15.0 %copy-start.2 = (bf16[4,2,576]{2,1,0:T(2,128)(2,1)S(1)}, bf16[4,2,576]{2,1,0:T(2,128)(2,1)}, u32[]{:S(2)}) copy-start(bf16[4,2,576]{2,1,0:T(2,128)(2,1)} %new_ref.1) | copy-start | bytes 27652
  13.3 15.0 %copy-start.3 = (s32[2]{0:T(128)S(1)}, s32[2]{0:T(128)}, u32[]{:S(2)}) copy-start(s32[2]{0:T(128)} %lengths_ref) | copy-start | bytes 28
  13.4 4.9 %collective-permute-start.4 = (bf16[16,3712]{1,0:T(8,128)(2,1)S(1)}, bf16[16,3712]{1,0:T(8,128)(2,1)S(1)}, u32[]{:S(2)}, u32[]{:S(2)}) collective-permute-start(bf16[16,3712]{1,0:T(8,128)(2,1)S(1)} %join.3.refs_1_), channel_id=1, source_target_pairs={{0,2},{1,3},{2,0},{3,1},{4,6},{5,7},{6,4},{7,5},{8,10},{9,11},{10,... | collective-permute-start | bytes 356360 | tf_op jit(solution)/shard_map/ppermute | solution.py:148
  14.9 3.3 %collective-permute-start.5 = (bf16[16,3712]{1,0:T(8,128)(2,1)S(1)}, bf16[16,3712]{1,0:T(8,128)(2,1)S(1)}, u32[]{:S(2)}, u32[]{:S(2)}) collective-permute-start(bf16[16,3712]{1,0:T(8,128)(2,1)S(1)} %join.2.refs_0_), channel_id=1, source_target_pairs={{0,1},{1,0},{2,3},{3,2},{4,5},{5,4},{6,7},{7,6},{8,9},{9,8},{10,11... | collective-permute-start | bytes 356360 | tf_op jit(solution)/shard_map/ppermute | solution.py:148
  14.9 3.3 %collective-permute-start.6 = (bf16[16,3712]{1,0:T(8,128)(2,1)S(1)}, bf16[16,3712]{1,0:T(8,128)(2,1)S(1)}, u32[]{:S(2)}, u32[]{:S(2)}) collective-permute-start(bf16[16,3712]{1,0:T(8,128)(2,1)S(1)} %join.3.refs_1_), channel_id=1, source_target_pairs={{0,1},{1,0},{2,3},{3,2},{4,5},{5,4},{6,7},{7,6},{8,9},{9,8},{10,11... | collective-permute-start | bytes 356360 | tf_op jit(solution)/shard_map/ppermute | solution.py:148
  15.5 2.8 %collective-permute-start.7 = (bf16[16,3712]{1,0:T(8,128)(2,1)S(1)}, bf16[16,3712]{1,0:T(8,128)(2,1)S(1)}, u32[]{:S(2)}, u32[]{:S(2)}) collective-permute-start(bf16[16,3712]{1,0:T(8,128)(2,1)S(1)} %collective-permute-done.3.refs_2_), channel_id=1, source_target_pairs={{0,1},{1,0},{2,3},{3,2},{4,5},{5,4},{6,7},{7,6},{8,9},{9,8},{10,11... | collective-permute-start | bytes 356360 | tf_op jit(solution)/shard_map/ppermute | solution.py:148
  18.3 1.3 %collective-permute-start.8 = (bf16[16,3712]{1,0:T(8,128)(2,1)S(1)}, bf16[16,3712]{1,0:T(8,128)(2,1)S(1)}, u32[]{:S(2)}, u32[]{:S(2)}) collective-permute-start(bf16[16,3712]{1,0:T(8,128)(2,1)S(1)} %collective-permute-done.4.refs_3_), channel_id=1, source_target_pairs={{0,1},{1,0},{2,3},{3,2},{4,5},{5,4},{6,7},{7,6},{8,9},{9,8},{10,11... | collective-permute-start | bytes 356360 | tf_op jit(solution)/shard_map/ppermute | solution.py:148
  23.0 1.6 %collective-permute-start.9 = (bf16[32,3584]{1,0:T(8,128)(2,1)S(1)}, bf16[32,3584]{1,0:T(8,128)(2,1)S(1)}, u32[]{:S(2)}, u32[]{:S(2)}) collective-permute-start(bf16[32,3584]{1,0:T(8,128)(2,1)S(1)} %get-tuple-element.11), channel_id=1, source_target_pairs={{0,1},{1,0},{2,3},{3,2},{4,5},{5,4},{6,7},{7,6},{8,9},{9,8},{10,11... | collective-permute-start | bytes 688136 | tf_op jit(solution)/shard_map/ppermute | solution.py:148
  23.2 5.1 %collective-permute-start.11 = (bf16[32,3584]{1,0:T(8,128)(2,1)S(1)}, bf16[32,3584]{1,0:T(8,128)(2,1)S(1)}, u32[]{:S(2)}, u32[]{:S(2)}) collective-permute-start(bf16[32,3584]{1,0:T(8,128)(2,1)S(1)} %get-tuple-element.15), channel_id=1, source_target_pairs={{0,1},{1,0},{2,3},{3,2},{4,5},{5,4},{6,7},{7,6},{8,9},{9,8},{10,11... | collective-permute-start | bytes 688136 | tf_op jit(solution)/shard_map/ppermute | solution.py:148
  24.6 6.5 %collective-permute-start.15 = (bf16[8,3584]{1,0:T(8,128)(2,1)S(1)}, bf16[8,3584]{1,0:T(8,128)(2,1)S(1)}, u32[]{:S(2)}, u32[]{:S(2)}) collective-permute-start(bf16[8,3584]{1,0:T(8,128)(2,1)S(1)} %get-tuple-element.17), channel_id=1, source_target_pairs={{0,2},{1,3},{2,0},{3,1},{4,6},{5,7},{6,4},{7,5},{8,10},{9,11},{10,... | collective-permute-start | bytes 172040 | tf_op jit(solution)/shard_map/ppermute | solution.py:148
  26.2 4.9 %collective-permute-start.13 = (bf16[8,3584]{1,0:T(8,128)(2,1)S(1)}, bf16[8,3584]{1,0:T(8,128)(2,1)S(1)}, u32[]{:S(2)}, u32[]{:S(2)}) collective-permute-start(bf16[8,3584]{1,0:T(8,128)(2,1)S(1)} %get-tuple-element.20), channel_id=1, source_target_pairs={{0,2},{1,3},{2,0},{3,1},{4,6},{5,7},{6,4},{7,5},{8,10},{9,11},{10,... | collective-permute-start | bytes 172040 | tf_op jit(solution)/shard_map/ppermute | solution.py:148
  26.7 6.9 %collective-permute-start.10 = (bf16[16,3584]{1,0:T(8,128)(2,1)S(1)}, bf16[16,3584]{1,0:T(8,128)(2,1)S(1)}, u32[]{:S(2)}, u32[]{:S(2)}) collective-permute-start(bf16[16,3584]{1,0:T(8,128)(2,1)S(1)} %slice.32), channel_id=1, source_target_pairs={{0,2},{1,3},{2,0},{3,1},{4,6},{5,7},{6,4},{7,5},{8,10},{9,11},{10,... | collective-permute-start | bytes 344072 | tf_op jit(solution)/shard_map/ppermute | solution.py:148
  31.1 6.1 %collective-permute-start.16 = (bf16[8,3584]{1,0:T(8,128)(2,1)S(1)}, bf16[8,3584]{1,0:T(8,128)(2,1)S(1)}, u32[]{:S(2)}, u32[]{:S(2)}) collective-permute-start(bf16[8,3584]{1,0:T(8,128)(2,1)S(1)} %get-tuple-element.18), channel_id=1, source_target_pairs={{0,12},{1,13},{2,14},{3,15},{4,8},{5,9},{6,10},{7,11},{8,4},{9,5},... | collective-permute-start | bytes 172040 | tf_op jit(solution)/shard_map/ppermute | solution.py:148
  33.6 5.1 %collective-permute-start.14 = (bf16[8,3584]{1,0:T(8,128)(2,1)S(1)}, bf16[8,3584]{1,0:T(8,128)(2,1)S(1)}, u32[]{:S(2)}, u32[]{:S(2)}) collective-permute-start(bf16[8,3584]{1,0:T(8,128)(2,1)S(1)} %get-tuple-element.19), channel_id=1, source_target_pairs={{0,8},{1,9},{2,10},{3,11},{4,12},{5,13},{6,14},{7,15},{8,0},{9,1},... | collective-permute-start | bytes 172040 | tf_op jit(solution)/shard_map/ppermute | solution.py:148
  33.7 5.1 %collective-permute-start.12 = (bf16[8,3584]{1,0:T(8,128)(2,1)S(1)}, bf16[8,3584]{1,0:T(8,128)(2,1)S(1)}, u32[]{:S(2)}, u32[]{:S(2)}) collective-permute-start(bf16[8,3584]{1,0:T(8,128)(2,1)S(1)} %get-tuple-element.22), channel_id=1, source_target_pairs={{0,4},{1,5},{2,6},{3,7},{4,0},{5,1},{6,2},{7,3},{8,12},{9,13},{10,... | collective-permute-start | bytes 172040 | tf_op jit(solution)/shard_map/ppermute | solution.py:148

commit v4 on v3

--- a/solution.py
+++ b/solution.py
@@ -10,6 +10,7 @@
 RANK = 512
 SCORE_SCALE = 0.07216878364870322
 LANES = 128
+SUBLANES = 8
 PEERS = ("expert", "dp")
 MIB = 1 << 20
 
@@ -55,32 +56,50 @@
     out_ref[:, width:] = jnp.concatenate(marks, axis=0).astype(jnp.bfloat16)
 
 
-def attend_kernel(queries_ref, cache_ref, new_ref, lengths_ref, out_ref, keys):
+def attend_kernel(queries_ref, cache_ref, new_ref, lengths_ref, out_hbm, keys, context, sems):
     steps, rows_dev, heads, _ = queries_ref.shape
     slots = cache_ref.shape[2]
+    whole = slots - LANES
     fresh = [new_ref[t].astype(jnp.float32) for t in range(steps)]
+    spare = jnp.zeros((SUBLANES - steps, keys.shape[1]), jnp.float32)
+    target = lax.broadcasted_iota(jnp.int32, (SUBLANES, LANES), 1) - (LANES - steps)
+    source = lax.broadcasted_iota(jnp.int32, (SUBLANES, LANES), 0)
+    spots = jnp.where(target == source, 1.0, 0.0).astype(jnp.bfloat16)
+    spot = lax.broadcasted_iota(jnp.int32, (keys.shape[1], LANES), 1)
+    place = lax.broadcasted_iota(jnp.int32, (steps * heads, slots), 1)
+    step = lax.broadcasted_iota(jnp.int32, (steps * heads, slots), 0) // heads
+    age = place - (slots - steps)
+    recent = (age >= 0) & (age <= step)
+    copies = []
     for b in range(rows_dev):
-        rest = jnp.zeros((slots - steps, keys.shape[0]), jnp.float32)
-        added = jnp.concatenate([rest] + [f[b : b + 1] for f in fresh], axis=0).astype(jnp.bfloat16)
-        spot = lax.broadcasted_iota(jnp.int32, keys.shape, 1)
-        keys[...] = jnp.where(spot < slots - steps, cache_ref[b], added.T)
+        added = jnp.concatenate([f[b : b + 1] for f in fresh] + [spare], axis=0)
+        added = lax.dot_general(
+            added.astype(jnp.bfloat16),
+            spots,
+            (((0,), (0,)), ((), ())),
+            preferred_element_type=jnp.float32,
+        ).astype(jnp.bfloat16)
+        keys[b, :, 0:whole] = cache_ref[b, :, 0:whole]
+        keys[b, :, whole:] = jnp.where(spot < LANES - steps, cache_ref[b, :, whole:], added)
+    scores = []
+    for b in range(rows_dev):
         queries = queries_ref[:, b].reshape(steps * heads, queries_ref.shape[3])
-        scores = jnp.dot(queries, keys[...], preferred_element_type=jnp.float32)
-        scores = scores * SCORE_SCALE
-        place = lax.broadcasted_iota(jnp.int32, scores.shape, 1)
-        step = lax.broadcasted_iota(jnp.int32, scores.shape, 0) // heads
-        age = place - (slots - steps)
-        keep = (place < lengths_ref[b]) | ((age >= 0) & (age <= step))
-        scores = jnp.where(keep, scores, -1e30)
-        weight = jnp.exp(scores - jnp.max(scores, axis=1, keepdims=True))
-        probs = weight / jnp.sum(weight, axis=1, keepdims=True)
-        context = lax.dot_general(
+        raw = jnp.dot(queries, keys[b], preferred_element_type=jnp.float32)
+        scores.append(jnp.where((place < lengths_ref[b]) | recent, raw * SCORE_SCALE, -1e30))
+    for b in range(rows_dev):
+        weight = jnp.exp(scores[b] - jnp.max(scores[b], axis=1, keepdims=True))
+        probs = weight * (1.0 / jnp.sum(weight, axis=1, keepdims=True))
+        result = lax.dot_general(
             probs.astype(jnp.bfloat16),
-            keys[:RANK],
+            keys[b, :RANK],
             (((1,), (1,)), ((), ())),
             preferred_element_type=jnp.float32,
         )
-        out_ref[:, b] = context.astype(jnp.bfloat16).reshape(steps, heads, RANK)
+        context[:, b] = result.astype(jnp.bfloat16).reshape(steps, heads, RANK)
+        copies.append(pltpu.make_async_copy(context.at[:, b], out_hbm.at[:, b], sems.at[b]))
+        copies[b].start()
+    for copy in copies:
+        copy.wait()
 
 
 def expert_kernel(experts, tile, pieces, *refs):
@@ -90,9 +109,10 @@
     units = down.shape[1]
     parts = units // tile
     columns = width // parts
-    piece = x_refs[0].shape[0]
-    for i, x_ref in enumerate(x_refs):
-        x[i * piece : (i + 1) * piece] = x_ref[...]
+    row = 0
+    for x_ref in x_refs:
+        x[row : row + x_ref.shape[0]] = x_ref[...]
+        row += x_ref.shape[0]
     own = lax.axis_index("expert")
     marks = x[:, width:].astype(jnp.float32)
     column = lax.broadcasted_iota(jnp.int32, marks.shape, 1)
@@ -199,9 +219,9 @@
     for bit in range(2, bits - 2):
         base = join([base, swap(base, 1 << bit)])
     size = base.shape[0]
-    third = swap(base, 3 * high)
-    second = swap(base, 2 * high)
-    first = swap(base, high)
+    third = swap(base, 2 * high)
+    second = swap(base, 3 * high)
+    first = swap(base, 1 * high)
     near = join([base, first])
     far = join([second, third])
     near_y = swap(near, 2)
@@ -242,8 +262,14 @@
         attend_kernel,
         out_shape=jax.ShapeDtypeStruct((steps, rows_dev, heads, RANK), jnp.bfloat16),
         in_specs=[VMEM, VMEM, VMEM, SMEM],
-        out_specs=VMEM,
-        scratch_shapes=[pltpu.VMEM(latent_cache.shape[:0:-1], jnp.bfloat16)],
+        out_specs=HBM,
+        scratch_shapes=[
+            pltpu.VMEM(
+                (rows_dev, latent_cache.shape[2], latent_cache.shape[1]), jnp.bfloat16
+            ),
+            pltpu.VMEM((steps, rows_dev, heads, RANK), jnp.bfloat16),
+            pltpu.SemaphoreType.DMA((rows_dev,)),
+        ],
         compiler_params=pltpu.CompilerParams(vmem_limit_bytes=16 * MIB),
         cost_estimate=pl.CostEstimate(
             flops=4 * rows_dev * steps * heads * latent_cache.shape[1] * latent_cache.shape[2],
@@ -258,10 +284,10 @@
         lengths,
     )
     first, context = lax.optimization_barrier((first, context))
-    third = swap(add(near[3 * size :], third), 3 * high)
-    second = swap(add(near[2 * size : 3 * size], second), 2 * high)
+    third = swap(add(near[3 * size :], third), 2 * high)
+    second = swap(add(near[2 * size : 3 * size], second), 3 * high)
     total = add(near[: 2 * size], first)
-    pieces = [total[:size], swap(total[size:], high), second, third]
+    pieces = [total[:size], swap(total[size:], 1 * high), second, third]
     for bit in range(bits - 3, 1, -1):
         value = add(*pieces)
         middle = value.shape[0] // 2

time: 39.6 us -> 39.2 us (0.990)
  waiting for transfers between devices: 12.3 us -> 13.1 us
  starting transfers between devices: 18.1 us -> 17.4 us
  Pallas kernels: 7.84 us -> 7.4 us
    ppermute x17, waiting for transfers between devices: 12.3 us -> 13.1 us  [swap(): return lax.ppermute(value, PEERS, [(i, i ^ mask) for i in range(size)])]
    ppermute x17, starting transfers between devices: 18.1 us -> 17.4 us  [swap(): return lax.ppermute(value, PEERS, [(i, i ^ mask) for i in range(size)])]
    pallas_call x1, Pallas kernels: 2.74 us -> 2.3 us  [per_device(): pl.pallas_call(attend_kernel, out_shape=jax.ShapeDtypeStruct((steps, rows...]
  transfers between devices with their start and end apart: 17 -> 17, of which waited for: 7 -> 8; matrix products, arithmetic and copies ran while one was open for 1% -> 1% of each run, Pallas kernels for 7% -> 6%
where the time goes in v4:
time: 39.2 us; the launch traced here: 39 us
  starting transfers between devices  17.4 us (44%)
  waiting for transfers between devices  13.1 us (33%)
  Pallas kernels  7.4 us (19%)
  between operations  0.9 us (2%)
    ppermute x17, starting transfers between devices, swap(): return lax.ppermute(value, PEERS, [(i, i ^ mask) for i in range(size)])  17.4 us
    ppermute x17, waiting for transfers between devices, swap(): return lax.ppermute(value, PEERS, [(i, i ^ mask) for i in range(size)])  13.1 us
    pallas_call x1, Pallas kernels, per_device(): pl.pallas_call(functools.partial(expert_kernel, experts, tile, len(parts)...  3.32 us
    pallas_call x1, Pallas kernels, per_device(): pl.pallas_call(attend_kernel, out_shape=jax.ShapeDtypeStruct((steps, rows...  2.3 us
    pallas_call x1, Pallas kernels, per_device(): pl.pallas_call(functools.partial(pack_kernel, experts), out_shape=jax.Sha...  1.1 us
  transfers between devices with their start and end apart: 17, of which 8 were waited for; matrix products, arithmetic and copies ran while one was open for 1% of the time, Pallas kernels for 6%

profile of v4, /device:TPU:0, one launch (start us, length us, event | category | flops | bytes accessed | tf_op | source)
XLA Modules:
  0.0 39.0 jit_solution(14307203472267113749)
XLA Ops:
  0.6 1.1 %pack.1.refs_0_ = bf16[8,3712]{1,0:T(8,128)(2,1)S(1)} custom-call(bf16[4,2,3584]{2,1,0:T(2,128)(2,1)} %refs_0_.1, s32[2,2,8]{2,1,0:T(2,128)} %refs_1_.1, s32[2,2,8]{2,1,0:T(2,128)} %refs_2_.1, f32[4,2,8]{2,1,0:T(2,128)} %refs_3_.1, s32[2]{0:T(128)} %refs_4_.1), custom_call_target="tpu_custom_call" | custom-call | tf_op jit(solution)/shard_map/pack/pallas_call | solution.py:206
  1.7 3.1 %collective-permute-start = (bf16[8,3712]{1,0:T(8,128)(2,1)S(1)}, bf16[8,3712]{1,0:T(8,128)(2,1)S(1)}, u32[]{:S(2)}, u32[]{:S(2)}) collective-permute-start(bf16[8,3712]{1,0:T(8,128)(2,1)S(1)} %pack.1.refs_0_), channel_id=1, source_target_pairs={{0,4},{1,5},{2,6},{3,7},{4,0},{5,1},{6,2},{7,3},{8,12},{9,13},{10,... | collective-permute-start | bytes 178184 | tf_op jit(solution)/shard_map/ppermute | solution.py:168
  4.8 2.6 %collective-permute-start.2 = (bf16[8,3712]{1,0:T(8,128)(2,1)S(1)}, bf16[8,3712]{1,0:T(8,128)(2,1)S(1)}, u32[]{:S(2)}, u32[]{:S(2)}) collective-permute-start(bf16[8,3712]{1,0:T(8,128)(2,1)S(1)} %pack.1.refs_0_), channel_id=1, source_target_pairs={{0,8},{1,9},{2,10},{3,11},{4,12},{5,13},{6,14},{7,15},{8,0},{9,1},... | collective-permute-start | bytes 178184 | tf_op jit(solution)/shard_map/ppermute | solution.py:168
  7.4 0.0 collective-permute-start.1
  7.4 0.0 collective-permute-done.refs_1_
  7.4 0.0 slice-start.2
  7.4 0.0 slice-start.4
  7.5 0.0 slice-start.1
  7.5 0.0 slice-start.3
  7.5 0.0 slice-start.5
  7.5 1.8 %collective-permute-start.3 = (bf16[16,3712]{1,0:T(8,128)(2,1)S(1)}, bf16[16,3712]{1,0:T(8,128)(2,1)S(1)}, u32[]{:S(2)}, u32[]{:S(2)}) collective-permute-start(bf16[16,3712]{1,0:T(8,128)(2,1)S(1)} %join.2.refs_0_), channel_id=1, source_target_pairs={{0,2},{1,3},{2,0},{3,1},{4,6},{5,7},{6,4},{7,5},{8,10},{9,11},{10,... | collective-permute-start | bytes 356360 | tf_op jit(solution)/shard_map/ppermute | solution.py:168
  9.3 1.8 %collective-permute-done.2.refs_1_ = bf16[8,3712]{1,0:T(8,128)(2,1)S(1)} collective-permute-done((bf16[8,3712]{1,0:T(8,128)(2,1)S(1)}, bf16[8,3712]{1,0:T(8,128)(2,1)S(1)}, u32[]{:S(2)}, u32[]{:S(2)}) %collective-permute-start.2) | collective-permute-done | bytes 59424 | tf_op jit(solution)/shard_map/ppermute | solution.py:168
  11.1 2.3 %collective-permute-done.1.refs_0_ = bf16[8,3712]{1,0:T(8,128)(2,1)S(1)} collective-permute-done((bf16[8,3712]{1,0:T(8,128)(2,1)S(1)}, bf16[8,3712]{1,0:T(8,128)(2,1)S(1)}, u32[]{:S(2)}, u32[]{:S(2)}) %collective-permute-start.1) | collective-permute-done | bytes 59424 | tf_op jit(solution)/shard_map/ppermute | solution.py:168
  13.4 0.0 copy-start
  13.4 0.0 copy-start.1
  13.5 0.0 copy-start.2
  13.5 0.0 copy-start.3
  13.5 1.6 %collective-permute-start.4 = (bf16[16,3712]{1,0:T(8,128)(2,1)S(1)}, bf16[16,3712]{1,0:T(8,128)(2,1)S(1)}, u32[]{:S(2)}, u32[]{:S(2)}) collective-permute-start(bf16[16,3712]{1,0:T(8,128)(2,1)S(1)} %join.3.refs_1_), channel_id=1, source_target_pairs={{0,2},{1,3},{2,0},{3,1},{4,6},{5,7},{6,4},{7,5},{8,10},{9,11},{10,... | collective-permute-start | bytes 356360 | tf_op jit(solution)/shard_map/ppermute | solution.py:168
  15.1 0.0 collective-permute-start.5
  15.1 0.5 %collective-permute-start.6 = (bf16[16,3712]{1,0:T(8,128)(2,1)S(1)}, bf16[16,3712]{1,0:T(8,128)(2,1)S(1)}, u32[]{:S(2)}, u32[]{:S(2)}) collective-permute-start(bf16[16,3712]{1,0:T(8,128)(2,1)S(1)} %join.3.refs_1_), channel_id=1, source_target_pairs={{0,1},{1,0},{2,3},{3,2},{4,5},{5,4},{6,7},{7,6},{8,9},{9,8},{10,11... | collective-permute-start | bytes 356360 | tf_op jit(solution)/shard_map/ppermute | solution.py:168
  15.6 0.0 collective-permute-done.3.refs_2_
  15.6 0.0 collective-permute-start.7
  15.6 2.8 %collective-permute-done.4.refs_3_ = bf16[16,3712]{1,0:T(8,128)(2,1)S(1)} collective-permute-done((bf16[16,3712]{1,0:T(8,128)(2,1)S(1)}, bf16[16,3712]{1,0:T(8,128)(2,1)S(1)}, u32[]{:S(2)}, u32[]{:S(2)}) %collective-permute-start.4) | collective-permute-done | bytes 118816 | tf_op jit(solution)/shard_map/ppermute | solution.py:168
  18.4 0.0 collective-permute-start.8
  18.4 0.0 collective-permute-done.5.refs_4_
  18.4 0.0 collective-permute-done.6.refs_5_
  18.4 0.0 collective-permute-done.7.refs_6_
  18.4 1.3 %collective-permute-done.8.refs_7_ = bf16[16,3712]{1,0:T(8,128)(2,1)S(1)} collective-permute-done((bf16[16,3712]{1,0:T(8,128)(2,1)S(1)}, bf16[16,3712]{1,0:T(8,128)(2,1)S(1)}, u32[]{:S(2)}, u32[]{:S(2)}) %collective-permute-start.8) | collective-permute-done | bytes 118816 | tf_op jit(solution)/shard_map/ppermute | solution.py:168
  19.8 3.3 %experts.1 = (bf16[32,3584]{1,0:T(8,128)(2,1)S(1)}, bf16[32,3584]{1,0:T(8,128)(2,1)S(1)}, bf16[32,3584]{1,0:T(8,128)(2,1)S(1)}, bf16[32,3584]{1,0:T(8,128)(2,1)S(1)}) custom-call(bf16[16,3712]{1,0:T(8,128)(2,1)S(1)} %join.2.refs_0_, bf16[16,3712]{1,0:T(8,128)(2,1)S(1)} %join.3.refs_1_, bf16[16,3712]{1,0:T(8,128)(2,1)S(1)} %collective-permute-done.3.refs_2_, ...), custom_call_target="tpu_custom_call" | custom-call | flops 2818572288 | bytes 22020096 | tf_op jit(solution)/shard_map/experts/pallas_call | solution.py:235
  23.1 0.2 collective-permute-start.9
  23.3 0.4 collective-permute-start.11
  23.7 1.0 %collective-permute-done.9 = bf16[32,3584]{1,0:T(8,128)(2,1)S(1)} collective-permute-done((bf16[32,3584]{1,0:T(8,128)(2,1)S(1)}, bf16[32,3584]{1,0:T(8,128)(2,1)S(1)}, u32[]{:S(2)}, u32[]{:S(2)}) %collective-permute-start.9) | collective-permute-done | bytes 229408 | tf_op jit(solution)/shard_map/ppermute | solution.py:168
  24.7 0.1 add_convert_fusion.1
  24.8 1.6 %collective-permute-start.15 = (bf16[8,3584]{1,0:T(8,128)(2,1)S(1)}, bf16[8,3584]{1,0:T(8,128)(2,1)S(1)}, u32[]{:S(2)}, u32[]{:S(2)}) collective-permute-start(bf16[8,3584]{1,0:T(8,128)(2,1)S(1)} %get-tuple-element.17), channel_id=1, source_target_pairs={{0,2},{1,3},{2,0},{3,1},{4,6},{5,7},{6,4},{7,5},{8,10},{9,11},{10,... | collective-permute-start | bytes 172040 | tf_op jit(solution)/shard_map/ppermute | solution.py:168
  26.4 0.5 %collective-permute-start.13 = (bf16[8,3584]{1,0:T(8,128)(2,1)S(1)}, bf16[8,3584]{1,0:T(8,128)(2,1)S(1)}, u32[]{:S(2)}, u32[]{:S(2)}) collective-permute-start(bf16[8,3584]{1,0:T(8,128)(2,1)S(1)} %get-tuple-element.20), channel_id=1, source_target_pairs={{0,2},{1,3},{2,0},{3,1},{4,6},{5,7},{6,4},{7,5},{8,10},{9,11},{10,... | collective-permute-start | bytes 172040 | tf_op jit(solution)/shard_map/ppermute | solution.py:168
  26.9 1.5 %collective-permute-start.10 = (bf16[16,3584]{1,0:T(8,128)(2,1)S(1)}, bf16[16,3584]{1,0:T(8,128)(2,1)S(1)}, u32[]{:S(2)}, u32[]{:S(2)}) collective-permute-start(bf16[16,3584]{1,0:T(8,128)(2,1)S(1)} %slice.32), channel_id=1, source_target_pairs={{0,2},{1,3},{2,0},{3,1},{4,6},{5,7},{6,4},{7,5},{8,10},{9,11},{10,... | collective-permute-start | bytes 344072 | tf_op jit(solution)/shard_map/ppermute | solution.py:168
  28.4 0.0 collective-permute-done.11
  28.4 0.1 add_convert_fusion
  28.5 2.3 %attend.1 = bf16[4,2,64,512]{3,2,1,0:T(8,128)(2,1)} custom-call(bf16[4,2,64,576]{3,2,1,0:T(8,128)(2,1)S(1)} %copy-done, bf16[2,576,256]{2,1,0:T(8,128)(2,1)S(1)} %bitcast.7, bf16[4,2,576]{2,1,0:T(2,128)(2,1)S(1)} %copy-done.2, s32[2]{0:T(128)S(1)} %copy-done.3), custom_call_target="tpu_custom_call" | custom-call | flops 301989888 | bytes 1769472 | tf_op jit(solution)/shard_map/attend/pallas_call | solution.py:261
  30.8 0.0 collective-permute-done.15
  30.8 0.4 collective-permute-done.13
  31.2 1.2 %collective-permute-start.16 = (bf16[8,3584]{1,0:T(8,128)(2,1)S(1)}, bf16[8,3584]{1,0:T(8,128)(2,1)S(1)}, u32[]{:S(2)}, u32[]{:S(2)}) collective-permute-start(bf16[8,3584]{1,0:T(8,128)(2,1)S(1)} %get-tuple-element.18), channel_id=1, source_target_pairs={{0,8},{1,9},{2,10},{3,11},{4,12},{5,13},{6,14},{7,15},{8,0},{9,1},... | collective-permute-start | bytes 172040 | tf_op jit(solution)/shard_map/ppermute | solution.py:168
  32.4 0.7 %collective-permute-start.14 = (bf16[8,3584]{1,0:T(8,128)(2,1)S(1)}, bf16[8,3584]{1,0:T(8,128)(2,1)S(1)}, u32[]{:S(2)}, u32[]{:S(2)}) collective-permute-start(bf16[8,3584]{1,0:T(8,128)(2,1)S(1)} %get-tuple-element.19), channel_id=1, source_target_pairs={{0,12},{1,13},{2,14},{3,15},{4,8},{5,9},{6,10},{7,11},{8,4},{9,5},... | collective-permute-start | bytes 172040 | tf_op jit(solution)/shard_map/ppermute | solution.py:168
  33.1 0.0 collective-permute-done.10
  33.2 1.7 %collective-permute-start.12 = (bf16[8,3584]{1,0:T(8,128)(2,1)S(1)}, bf16[8,3584]{1,0:T(8,128)(2,1)S(1)}, u32[]{:S(2)}, u32[]{:S(2)}) collective-permute-start(bf16[8,3584]{1,0:T(8,128)(2,1)S(1)} %get-tuple-element.22), channel_id=1, source_target_pairs={{0,4},{1,5},{2,6},{3,7},{4,0},{5,1},{6,2},{7,3},{8,12},{9,13},{10,... | collective-permute-start | bytes 172040 | tf_op jit(solution)/shard_map/ppermute | solution.py:168
  34.9 1.9 %collective-permute-done.16.refs_3_ = bf16[8,3584]{1,0:T(8,128)(2,1)S(1)} collective-permute-done((bf16[8,3584]{1,0:T(8,128)(2,1)S(1)}, bf16[8,3584]{1,0:T(8,128)(2,1)S(1)}, u32[]{:S(2)}, u32[]{:S(2)}) %collective-permute-start.16) | collective-permute-done | bytes 57376 | tf_op jit(solution)/shard_map/ppermute | solution.py:168
  36.8 1.6 %collective-permute-done.14.refs_2_ = bf16[8,3584]{1,0:T(8,128)(2,1)S(1)} collective-permute-done((bf16[8,3584]{1,0:T(8,128)(2,1)S(1)}, bf16[8,3584]{1,0:T(8,128)(2,1)S(1)}, u32[]{:S(2)}, u32[]{:S(2)}) %collective-permute-start.14) | collective-permute-done | bytes 57376 | tf_op jit(solution)/shard_map/ppermute | solution.py:168
  38.4 0.7 %total.1 = bf16[4,2,3584]{2,1,0:T(2,128)(2,1)} custom-call(bf16[8,3584]{1,0:T(8,128)(2,1)S(1)} %get-tuple-element.23.refs_0_, bf16[8,3584]{1,0:T(8,128)(2,1)S(1)} %collective-permute-done.12.refs_1_, bf16[8,3584]{1,0:T(8,128)(2,1)S(1)} %collective-permute-done.14.refs_2_, bf16[8,3584]{1,0:T(8,128)(2,1)S(1)} %collective-permute-done.16.refs_3_), custom_call_target="tpu_custom_call" | custom-call | tf_op jit(solution)/shard_map/total/pallas_call | solution.py:295
  (22 shorter events, 0.1 us)
Async XLA Ops:
  1.7 5.7 %collective-permute-start = (bf16[8,3712]{1,0:T(8,128)(2,1)S(1)}, bf16[8,3712]{1,0:T(8,128)(2,1)S(1)}, u32[]{:S(2)}, u32[]{:S(2)}) collective-permute-start(bf16[8,3712]{1,0:T(8,128)(2,1)S(1)} %pack.1.refs_0_), channel_id=1, source_target_pairs={{0,4},{1,5},{2,6},{3,7},{4,0},{5,1},{6,2},{7,3},{8,12},{9,13},{10,... | collective-permute-start | bytes 178184 | tf_op jit(solution)/shard_map/ppermute | solution.py:168
  4.8 6.3 %collective-permute-start.2 = (bf16[8,3712]{1,0:T(8,128)(2,1)S(1)}, bf16[8,3712]{1,0:T(8,128)(2,1)S(1)}, u32[]{:S(2)}, u32[]{:S(2)}) collective-permute-start(bf16[8,3712]{1,0:T(8,128)(2,1)S(1)} %pack.1.refs_0_), channel_id=1, source_target_pairs={{0,8},{1,9},{2,10},{3,11},{4,12},{5,13},{6,14},{7,15},{8,0},{9,1},... | collective-permute-start | bytes 178184 | tf_op jit(solution)/shard_map/ppermute | solution.py:168
  7.4 6.0 %collective-permute-start.1 = (bf16[8,3712]{1,0:T(8,128)(2,1)S(1)}, bf16[8,3712]{1,0:T(8,128)(2,1)S(1)}, u32[]{:S(2)}, u32[]{:S(2)}) collective-permute-start(bf16[8,3712]{1,0:T(8,128)(2,1)S(1)} %pack.1.refs_0_), channel_id=1, source_target_pairs={{0,12},{1,13},{2,14},{3,15},{4,8},{5,9},{6,10},{7,11},{8,4},{9,5},... | collective-permute-start | bytes 178184 | tf_op jit(solution)/shard_map/ppermute | solution.py:168
  7.4 12.3 %slice-start = ((s8[7340032]{0:T(1024)(128)(4,1)}), s8[4194304]{0:T(1024)(128)(4,1)S(1)}, s32[]{:S(2)}) async-start(s8[7340032]{0:T(1024)(128)(4,1)} %bitcast.1), calls=%async_computation | async-start | bytes 8388608
  7.4 12.3 %slice-start.2 = ((s8[7340032]{0:T(1024)(128)(4,1)}), s8[4194304]{0:T(1024)(128)(4,1)S(1)}, s32[]{:S(2)}) async-start(s8[7340032]{0:T(1024)(128)(4,1)} %bitcast.3), calls=%async_computation.2 | async-start | bytes 8388608
  7.4 12.3 %slice-start.4 = ((s8[7340032]{0:T(1024)(128)(4,1)}), s8[4194304]{0:T(1024)(128)(4,1)S(1)}, s32[]{:S(2)}) async-start(s8[7340032]{0:T(1024)(128)(4,1)} %bitcast.5), calls=%async_computation.4 | async-start | bytes 8388608
  7.5 12.2 %slice-start.1 = ((s8[7340032]{0:T(1024)(128)(4,1)}), s8[3145728]{0:T(1024)(128)(4,1)S(1)}, s32[]{:S(2)}) async-start(s8[7340032]{0:T(1024)(128)(4,1)} %bitcast.1), calls=%async_computation.1 | async-start | bytes 6291456
  7.5 12.2 %slice-start.3 = ((s8[7340032]{0:T(1024)(128)(4,1)}), s8[3145728]{0:T(1024)(128)(4,1)S(1)}, s32[]{:S(2)}) async-start(s8[7340032]{0:T(1024)(128)(4,1)} %bitcast.3), calls=%async_computation.3 | async-start | bytes 6291456
  7.5 12.2 %slice-start.5 = ((s8[7340032]{0:T(1024)(128)(4,1)}), s8[3145728]{0:T(1024)(128)(4,1)S(1)}, s32[]{:S(2)}) async-start(s8[7340032]{0:T(1024)(128)(4,1)} %bitcast.5), calls=%async_computation.5 | async-start | bytes 6291456
  7.5 8.1 %collective-permute-start.3 = (bf16[16,3712]{1,0:T(8,128)(2,1)S(1)}, bf16[16,3712]{1,0:T(8,128)(2,1)S(1)}, u32[]{:S(2)}, u32[]{:S(2)}) collective-permute-start(bf16[16,3712]{1,0:T(8,128)(2,1)S(1)} %join.2.refs_0_), channel_id=1, source_target_pairs={{0,2},{1,3},{2,0},{3,1},{4,6},{5,7},{6,4},{7,5},{8,10},{9,11},{10,... | collective-permute-start | bytes 356360 | tf_op jit(solution)/shard_map/ppermute | solution.py:168
  13.4 15.0 %copy-start = (bf16[4,2,64,576]{3,2,1,0:T(8,128)(2,1)S(1)}, bf16[4,2,64,576]{3,2,1,0:T(8,128)(2,1)}, u32[]{:S(2)}) copy-start(bf16[4,2,64,576]{3,2,1,0:T(8,128)(2,1)} %queries_ref.1) | copy-start | bytes 1769476
  13.4 15.0 %copy-start.1 = (bf16[2,256,576]{1,2,0:T(8,128)(2,1)S(1)}, bf16[2,256,576]{1,2,0:T(8,128)(2,1)}, u32[]{:S(2)}) copy-start(bf16[2,256,576]{1,2,0:T(8,128)(2,1)} %param.13) | copy-start | bytes 1769476
  13.5 15.0 %copy-start.2 = (bf16[4,2,576]{2,1,0:T(2,128)(2,1)S(1)}, bf16[4,2,576]{2,1,0:T(2,128)(2,1)}, u32[]{:S(2)}) copy-start(bf16[4,2,576]{2,1,0:T(2,128)(2,1)} %new_ref.1) | copy-start | bytes 27652
  13.5 15.0 %copy-start.3 = (s32[2]{0:T(128)S(1)}, s32[2]{0:T(128)}, u32[]{:S(2)}) copy-start(s32[2]{0:T(128)} %lengths_ref) | copy-start | bytes 28
  13.5 4.9 %collective-permute-start.4 = (bf16[16,3712]{1,0:T(8,128)(2,1)S(1)}, bf16[16,3712]{1,0:T(8,128)(2,1)S(1)}, u32[]{:S(2)}, u32[]{:S(2)}) collective-permute-start(bf16[16,3712]{1,0:T(8,128)(2,1)S(1)} %join.3.refs_1_), channel_id=1, source_target_pairs={{0,2},{1,3},{2,0},{3,1},{4,6},{5,7},{6,4},{7,5},{8,10},{9,11},{10,... | collective-permute-start | bytes 356360 | tf_op jit(solution)/shard_map/ppermute | solution.py:168
  15.1 3.3 %collective-permute-start.5 = (bf16[16,3712]{1,0:T(8,128)(2,1)S(1)}, bf16[16,3712]{1,0:T(8,128)(2,1)S(1)}, u32[]{:S(2)}, u32[]{:S(2)}) collective-permute-start(bf16[16,3712]{1,0:T(8,128)(2,1)S(1)} %join.2.refs_0_), channel_id=1, source_target_pairs={{0,1},{1,0},{2,3},{3,2},{4,5},{5,4},{6,7},{7,6},{8,9},{9,8},{10,11... | collective-permute-start | bytes 356360 | tf_op jit(solution)/shard_map/ppermute | solution.py:168
  15.1 3.3 %collective-permute-start.6 = (bf16[16,3712]{1,0:T(8,128)(2,1)S(1)}, bf16[16,3712]{1,0:T(8,128)(2,1)S(1)}, u32[]{:S(2)}, u32[]{:S(2)}) collective-permute-start(bf16[16,3712]{1,0:T(8,128)(2,1)S(1)} %join.3.refs_1_), channel_id=1, source_target_pairs={{0,1},{1,0},{2,3},{3,2},{4,5},{5,4},{6,7},{7,6},{8,9},{9,8},{10,11... | collective-permute-start | bytes 356360 | tf_op jit(solution)/shard_map/ppermute | solution.py:168
  15.6 2.8 %collective-permute-start.7 = (bf16[16,3712]{1,0:T(8,128)(2,1)S(1)}, bf16[16,3712]{1,0:T(8,128)(2,1)S(1)}, u32[]{:S(2)}, u32[]{:S(2)}) collective-permute-start(bf16[16,3712]{1,0:T(8,128)(2,1)S(1)} %collective-permute-done.3.refs_2_), channel_id=1, source_target_pairs={{0,1},{1,0},{2,3},{3,2},{4,5},{5,4},{6,7},{7,6},{8,9},{9,8},{10,11... | collective-permute-start | bytes 356360 | tf_op jit(solution)/shard_map/ppermute | solution.py:168
  18.4 1.3 %collective-permute-start.8 = (bf16[16,3712]{1,0:T(8,128)(2,1)S(1)}, bf16[16,3712]{1,0:T(8,128)(2,1)S(1)}, u32[]{:S(2)}, u32[]{:S(2)}) collective-permute-start(bf16[16,3712]{1,0:T(8,128)(2,1)S(1)} %collective-permute-done.4.refs_3_), channel_id=1, source_target_pairs={{0,1},{1,0},{2,3},{3,2},{4,5},{5,4},{6,7},{7,6},{8,9},{9,8},{10,11... | collective-permute-start | bytes 356360 | tf_op jit(solution)/shard_map/ppermute | solution.py:168
  23.1 1.6 %collective-permute-start.9 = (bf16[32,3584]{1,0:T(8,128)(2,1)S(1)}, bf16[32,3584]{1,0:T(8,128)(2,1)S(1)}, u32[]{:S(2)}, u32[]{:S(2)}) collective-permute-start(bf16[32,3584]{1,0:T(8,128)(2,1)S(1)} %get-tuple-element.11), channel_id=1, source_target_pairs={{0,1},{1,0},{2,3},{3,2},{4,5},{5,4},{6,7},{7,6},{8,9},{9,8},{10,11... | collective-permute-start | bytes 688136 | tf_op jit(solution)/shard_map/ppermute | solution.py:168
  23.3 5.1 %collective-permute-start.11 = (bf16[32,3584]{1,0:T(8,128)(2,1)S(1)}, bf16[32,3584]{1,0:T(8,128)(2,1)S(1)}, u32[]{:S(2)}, u32[]{:S(2)}) collective-permute-start(bf16[32,3584]{1,0:T(8,128)(2,1)S(1)} %get-tuple-element.15), channel_id=1, source_target_pairs={{0,1},{1,0},{2,3},{3,2},{4,5},{5,4},{6,7},{7,6},{8,9},{9,8},{10,11... | collective-permute-start | bytes 688136 | tf_op jit(solution)/shard_map/ppermute | solution.py:168
  24.8 6.0 %collective-permute-start.15 = (bf16[8,3584]{1,0:T(8,128)(2,1)S(1)}, bf16[8,3584]{1,0:T(8,128)(2,1)S(1)}, u32[]{:S(2)}, u32[]{:S(2)}) collective-permute-start(bf16[8,3584]{1,0:T(8,128)(2,1)S(1)} %get-tuple-element.17), channel_id=1, source_target_pairs={{0,2},{1,3},{2,0},{3,1},{4,6},{5,7},{6,4},{7,5},{8,10},{9,11},{10,... | collective-permute-start | bytes 172040 | tf_op jit(solution)/shard_map/ppermute | solution.py:168
  26.4 4.8 %collective-permute-start.13 = (bf16[8,3584]{1,0:T(8,128)(2,1)S(1)}, bf16[8,3584]{1,0:T(8,128)(2,1)S(1)}, u32[]{:S(2)}, u32[]{:S(2)}) collective-permute-start(bf16[8,3584]{1,0:T(8,128)(2,1)S(1)} %get-tuple-element.20), channel_id=1, source_target_pairs={{0,2},{1,3},{2,0},{3,1},{4,6},{5,7},{6,4},{7,5},{8,10},{9,11},{10,... | collective-permute-start | bytes 172040 | tf_op jit(solution)/shard_map/ppermute | solution.py:168
  26.9 6.3 %collective-permute-start.10 = (bf16[16,3584]{1,0:T(8,128)(2,1)S(1)}, bf16[16,3584]{1,0:T(8,128)(2,1)S(1)}, u32[]{:S(2)}, u32[]{:S(2)}) collective-permute-start(bf16[16,3584]{1,0:T(8,128)(2,1)S(1)} %slice.32), channel_id=1, source_target_pairs={{0,2},{1,3},{2,0},{3,1},{4,6},{5,7},{6,4},{7,5},{8,10},{9,11},{10,... | collective-permute-start | bytes 344072 | tf_op jit(solution)/shard_map/ppermute | solution.py:168
  31.2 5.6 %collective-permute-start.16 = (bf16[8,3584]{1,0:T(8,128)(2,1)S(1)}, bf16[8,3584]{1,0:T(8,128)(2,1)S(1)}, u32[]{:S(2)}, u32[]{:S(2)}) collective-permute-start(bf16[8,3584]{1,0:T(8,128)(2,1)S(1)} %get-tuple-element.18), channel_id=1, source_target_pairs={{0,8},{1,9},{2,10},{3,11},{4,12},{5,13},{6,14},{7,15},{8,0},{9,1},... | collective-permute-start | bytes 172040 | tf_op jit(solution)/shard_map/ppermute | solution.py:168
  32.4 6.0 %collective-permute-start.14 = (bf16[8,3584]{1,0:T(8,128)(2,1)S(1)}, bf16[8,3584]{1,0:T(8,128)(2,1)S(1)}, u32[]{:S(2)}, u32[]{:S(2)}) collective-permute-start(bf16[8,3584]{1,0:T(8,128)(2,1)S(1)} %get-tuple-element.19), channel_id=1, source_target_pairs={{0,12},{1,13},{2,14},{3,15},{4,8},{5,9},{6,10},{7,11},{8,4},{9,5},... | collective-permute-start | bytes 172040 | tf_op jit(solution)/shard_map/ppermute | solution.py:168
  33.2 5.2 %collective-permute-start.12 = (bf16[8,3584]{1,0:T(8,128)(2,1)S(1)}, bf16[8,3584]{1,0:T(8,128)(2,1)S(1)}, u32[]{:S(2)}, u32[]{:S(2)}) collective-permute-start(bf16[8,3584]{1,0:T(8,128)(2,1)S(1)} %get-tuple-element.22), channel_id=1, source_target_pairs={{0,4},{1,5},{2,6},{3,7},{4,0},{5,1},{6,2},{7,3},{8,12},{9,13},{10,... | collective-permute-start | bytes 172040 | tf_op jit(solution)/shard_map/ppermute | solution.py:168

commit v5 on v4

--- a/solution.py
+++ b/solution.py
@@ -134,9 +134,8 @@
 
 def join_kernel(*refs):
     *in_refs, out_ref = refs
-    size = in_refs[0].shape[0]
-    for i, ref in enumerate(in_refs):
-        out_ref[i * size : (i + 1) * size] = ref[...]
+    blocks = [ref[...].astype(jnp.float32) for ref in in_refs]
+    out_ref[...] = jnp.concatenate(blocks, axis=0).astype(jnp.bfloat16)
 
 
 def join(blocks):
@@ -166,6 +165,24 @@
 def swap(value, mask):
     size = lax.axis_size(PEERS)
     return lax.ppermute(value, PEERS, [(i, i ^ mask) for i in range(size)])
+
+
+def rows_kernel(begin, whole_ref, part_ref, out_ref):
+    size = part_ref.shape[0]
+    whole = whole_ref[...].astype(jnp.float32)
+    total = whole[begin : begin + size] + part_ref[...].astype(jnp.float32)
+    out_ref[...] = total.astype(jnp.bfloat16)
+
+
+def add_rows(whole, part, begin):
+    return pl.pallas_call(
+        functools.partial(rows_kernel, begin),
+        out_shape=jax.ShapeDtypeStruct(part.shape, jnp.bfloat16),
+        in_specs=[VMEM, VMEM],
+        out_specs=VMEM,
+        compiler_params=pltpu.CompilerParams(vmem_limit_bytes=8 * MIB),
+        name="add_rows",
+    )(whole, part)
 
 
 def add(*values):
@@ -253,10 +270,25 @@
     far = add(keep_far, swap(send_far, 1))
     near = add(keep_near, swap(send_near, 1))
     far_third, far_second, far_first = far[3 * size :], far[2 * size : 3 * size], far[: 2 * size]
-    far_third, lengths = lax.optimization_barrier((far_third, lengths))
     third = swap(far_third, 2)
     second = swap(far_second, 2)
     first = swap(far_first, 2)
+    third = swap(add_rows(near, third, 3 * size), 2 * high)
+    second = swap(add_rows(near, second, 2 * size), 3 * high)
+    total = add_rows(near, first, 0)
+    pieces = [total[:size], swap(total[size:], 1 * high), second, third]
+    for bit in range(bits - 3, 1, -1):
+        value = add(*pieces)
+        middle = value.shape[0] // 2
+        pieces = [value[:middle], swap(value[middle:], 1 << bit)]
+    moe_out = pl.pallas_call(
+        sum_kernel,
+        out_shape=jax.ShapeDtypeStruct((steps, rows_dev, width), jnp.bfloat16),
+        in_specs=[VMEM] * len(pieces),
+        out_specs=VMEM,
+        compiler_params=pltpu.CompilerParams(vmem_limit_bytes=4 * MIB),
+        name="total",
+    )(*pieces)
     heads = queries.shape[2]
     context = pl.pallas_call(
         attend_kernel,
@@ -283,23 +315,6 @@
         new_latents,
         lengths,
     )
-    first, context = lax.optimization_barrier((first, context))
-    third = swap(add(near[3 * size :], third), 2 * high)
-    second = swap(add(near[2 * size : 3 * size], second), 3 * high)
-    total = add(near[: 2 * size], first)
-    pieces = [total[:size], swap(total[size:], 1 * high), second, third]
-    for bit in range(bits - 3, 1, -1):
-        value = add(*pieces)
-        middle = value.shape[0] // 2
-        pieces = [value[:middle], swap(value[middle:], 1 << bit)]
-    moe_out = pl.pallas_call(
-        sum_kernel,
-        out_shape=jax.ShapeDtypeStruct((steps, rows_dev, width), jnp.bfloat16),
-        in_specs=[VMEM] * len(pieces),
-        out_specs=VMEM,
-        compiler_params=pltpu.CompilerParams(vmem_limit_bytes=4 * MIB),
-        name="total",
-    )(*pieces)
     return (context, moe_out)
 
 

time: 39.2 us -> 38.4 us (0.980)
  starting transfers between devices: 17.4 us -> 16.7 us
    ppermute x17, starting transfers between devices: 17.4 us -> 16.7 us  [swap(): return lax.ppermute(value, PEERS, [(i, i ^ mask) for i in range(size)])]
  transfers between devices with their start and end apart: 17 -> 17, of which waited for: 8 -> 9; matrix products, arithmetic and copies ran while one was open for 1% -> 0% of each run, Pallas kernels for 6% -> 6%
where the time goes in v5:
time: 38.4 us; the launch traced here: 38.3 us
  starting transfers between devices  16.7 us (43%)
  waiting for transfers between devices  13 us (34%)
  Pallas kernels  7.47 us (19%)
  between operations  0.87 us (2%)
    ppermute x17, starting transfers between devices, swap(): return lax.ppermute(value, PEERS, [(i, i ^ mask) for i in range(size)])  16.7 us
    ppermute x17, waiting for transfers between devices, swap(): return lax.ppermute(value, PEERS, [(i, i ^ mask) for i in range(size)])  13 us
    pallas_call x1, Pallas kernels, per_device(): pl.pallas_call(functools.partial(expert_kernel, experts, tile, len(parts)...  3.32 us
    pallas_call x1, Pallas kernels, per_device(): pl.pallas_call(attend_kernel, out_shape=jax.ShapeDtypeStruct((steps, rows...  2.3 us
    pallas_call x1, Pallas kernels, per_device(): pl.pallas_call(functools.partial(pack_kernel, experts), out_shape=jax.Sha...  1.1 us
  transfers between devices with their start and end apart: 17, of which 9 were waited for; matrix products, arithmetic and copies ran while one was open for 0% of the time, Pallas kernels for 6%

profile of v5, /device:TPU:0, one launch (start us, length us, event | category | flops | bytes accessed | tf_op | source)
XLA Modules:
  0.0 38.3 jit_solution(16128388748514936584)
XLA Ops:
  0.6 1.1 %pack.1.refs_0_ = bf16[8,3712]{1,0:T(8,128)(2,1)S(1)} custom-call(bf16[4,2,3584]{2,1,0:T(2,128)(2,1)} %refs_0_.1, s32[2,2,8]{2,1,0:T(2,128)} %refs_1_.1, s32[2,2,8]{2,1,0:T(2,128)} %refs_2_.1, f32[4,2,8]{2,1,0:T(2,128)} %refs_3_.1, s32[2]{0:T(128)} %refs_4_.1), custom_call_target="tpu_custom_call" | custom-call | tf_op jit(solution)/shard_map/pack/pallas_call | solution.py:223
  1.7 3.1 %collective-permute-start = (bf16[8,3712]{1,0:T(8,128)(2,1)S(1)}, bf16[8,3712]{1,0:T(8,128)(2,1)S(1)}, u32[]{:S(2)}, u32[]{:S(2)}) collective-permute-start(bf16[8,3712]{1,0:T(8,128)(2,1)S(1)} %pack.1.refs_0_), channel_id=1, source_target_pairs={{0,4},{1,5},{2,6},{3,7},{4,0},{5,1},{6,2},{7,3},{8,12},{9,13},{10,... | collective-permute-start | bytes 178184 | tf_op jit(solution)/shard_map/ppermute | solution.py:167
  4.8 2.6 %collective-permute-start.2 = (bf16[8,3712]{1,0:T(8,128)(2,1)S(1)}, bf16[8,3712]{1,0:T(8,128)(2,1)S(1)}, u32[]{:S(2)}, u32[]{:S(2)}) collective-permute-start(bf16[8,3712]{1,0:T(8,128)(2,1)S(1)} %pack.1.refs_0_), channel_id=1, source_target_pairs={{0,8},{1,9},{2,10},{3,11},{4,12},{5,13},{6,14},{7,15},{8,0},{9,1},... | collective-permute-start | bytes 178184 | tf_op jit(solution)/shard_map/ppermute | solution.py:167
  7.4 0.0 collective-permute-start.1
  7.4 0.0 collective-permute-done.refs_1_
  7.4 0.0 slice-start.2
  7.4 0.0 slice-start.4
  7.5 0.0 slice-start.1
  7.5 0.0 slice-start.3
  7.5 0.0 slice-start.5
  7.5 1.8 %collective-permute-start.3 = (bf16[16,3712]{1,0:T(8,128)(2,1)S(1)}, bf16[16,3712]{1,0:T(8,128)(2,1)S(1)}, u32[]{:S(2)}, u32[]{:S(2)}) collective-permute-start(bf16[16,3712]{1,0:T(8,128)(2,1)S(1)} %join.2.refs_0_), channel_id=1, source_target_pairs={{0,2},{1,3},{2,0},{3,1},{4,6},{5,7},{6,4},{7,5},{8,10},{9,11},{10,... | collective-permute-start | bytes 356360 | tf_op jit(solution)/shard_map/ppermute | solution.py:167
  9.3 1.8 %collective-permute-done.2.refs_1_ = bf16[8,3712]{1,0:T(8,128)(2,1)S(1)} collective-permute-done((bf16[8,3712]{1,0:T(8,128)(2,1)S(1)}, bf16[8,3712]{1,0:T(8,128)(2,1)S(1)}, u32[]{:S(2)}, u32[]{:S(2)}) %collective-permute-start.2) | collective-permute-done | bytes 59424 | tf_op jit(solution)/shard_map/ppermute | solution.py:167
  11.1 2.3 %collective-permute-done.1.refs_0_ = bf16[8,3712]{1,0:T(8,128)(2,1)S(1)} collective-permute-done((bf16[8,3712]{1,0:T(8,128)(2,1)S(1)}, bf16[8,3712]{1,0:T(8,128)(2,1)S(1)}, u32[]{:S(2)}, u32[]{:S(2)}) %collective-permute-start.1) | collective-permute-done | bytes 59424 | tf_op jit(solution)/shard_map/ppermute | solution.py:167
  13.4 0.0 copy-start
  13.4 0.0 copy-start.1
  13.5 0.0 copy-start.2
  13.5 0.0 copy-start.3
  13.5 1.6 %collective-permute-start.4 = (bf16[16,3712]{1,0:T(8,128)(2,1)S(1)}, bf16[16,3712]{1,0:T(8,128)(2,1)S(1)}, u32[]{:S(2)}, u32[]{:S(2)}) collective-permute-start(bf16[16,3712]{1,0:T(8,128)(2,1)S(1)} %join.3.refs_1_), channel_id=1, source_target_pairs={{0,2},{1,3},{2,0},{3,1},{4,6},{5,7},{6,4},{7,5},{8,10},{9,11},{10,... | collective-permute-start | bytes 356360 | tf_op jit(solution)/shard_map/ppermute | solution.py:167
  15.1 0.0 collective-permute-start.5
  15.1 0.5 %collective-permute-start.6 = (bf16[16,3712]{1,0:T(8,128)(2,1)S(1)}, bf16[16,3712]{1,0:T(8,128)(2,1)S(1)}, u32[]{:S(2)}, u32[]{:S(2)}) collective-permute-start(bf16[16,3712]{1,0:T(8,128)(2,1)S(1)} %join.3.refs_1_), channel_id=1, source_target_pairs={{0,1},{1,0},{2,3},{3,2},{4,5},{5,4},{6,7},{7,6},{8,9},{9,8},{10,11... | collective-permute-start | bytes 356360 | tf_op jit(solution)/shard_map/ppermute | solution.py:167
  15.6 0.0 collective-permute-done.3.refs_2_
  15.6 0.0 collective-permute-start.7
  15.6 2.8 %collective-permute-done.4.refs_3_ = bf16[16,3712]{1,0:T(8,128)(2,1)S(1)} collective-permute-done((bf16[16,3712]{1,0:T(8,128)(2,1)S(1)}, bf16[16,3712]{1,0:T(8,128)(2,1)S(1)}, u32[]{:S(2)}, u32[]{:S(2)}) %collective-permute-start.4) | collective-permute-done | bytes 118816 | tf_op jit(solution)/shard_map/ppermute | solution.py:167
  18.4 0.0 collective-permute-start.8
  18.4 0.0 collective-permute-done.5.refs_4_
  18.4 0.0 collective-permute-done.6.refs_5_
  18.4 0.0 collective-permute-done.7.refs_6_
  18.4 1.3 %collective-permute-done.8.refs_7_ = bf16[16,3712]{1,0:T(8,128)(2,1)S(1)} collective-permute-done((bf16[16,3712]{1,0:T(8,128)(2,1)S(1)}, bf16[16,3712]{1,0:T(8,128)(2,1)S(1)}, u32[]{:S(2)}, u32[]{:S(2)}) %collective-permute-start.8) | collective-permute-done | bytes 118816 | tf_op jit(solution)/shard_map/ppermute | solution.py:167
  19.8 3.3 %experts.1 = (bf16[32,3584]{1,0:T(8,128)(2,1)S(1)}, bf16[32,3584]{1,0:T(8,128)(2,1)S(1)}, bf16[32,3584]{1,0:T(8,128)(2,1)S(1)}, bf16[32,3584]{1,0:T(8,128)(2,1)S(1)}) custom-call(bf16[16,3712]{1,0:T(8,128)(2,1)S(1)} %join.2.refs_0_, bf16[16,3712]{1,0:T(8,128)(2,1)S(1)} %join.3.refs_1_, bf16[16,3712]{1,0:T(8,128)(2,1)S(1)} %collective-permute-done.3.refs_2_, ...), custom_call_target="tpu_custom_call" | custom-call | flops 2818572288 | bytes 22020096 | tf_op jit(solution)/shard_map/experts/pallas_call | solution.py:252
  23.1 0.2 collective-permute-start.10
  23.3 0.4 collective-permute-start.9
  23.7 1.0 %collective-permute-done.10 = bf16[32,3584]{1,0:T(8,128)(2,1)S(1)} collective-permute-done((bf16[32,3584]{1,0:T(8,128)(2,1)S(1)}, bf16[32,3584]{1,0:T(8,128)(2,1)S(1)}, u32[]{:S(2)}, u32[]{:S(2)}) %collective-permute-start.10) | collective-permute-done | bytes 229408 | tf_op jit(solution)/shard_map/ppermute | solution.py:167
  24.7 0.1 add_convert_fusion
  24.8 1.6 %collective-permute-start.15 = (bf16[8,3584]{1,0:T(8,128)(2,1)S(1)}, bf16[8,3584]{1,0:T(8,128)(2,1)S(1)}, u32[]{:S(2)}, u32[]{:S(2)}) collective-permute-start(bf16[8,3584]{1,0:T(8,128)(2,1)S(1)} %get-tuple-element.10), channel_id=1, source_target_pairs={{0,2},{1,3},{2,0},{3,1},{4,6},{5,7},{6,4},{7,5},{8,10},{9,11},{10,... | collective-permute-start | bytes 172040 | tf_op jit(solution)/shard_map/ppermute | solution.py:167
  26.4 0.5 %collective-permute-start.13 = (bf16[8,3584]{1,0:T(8,128)(2,1)S(1)}, bf16[8,3584]{1,0:T(8,128)(2,1)S(1)}, u32[]{:S(2)}, u32[]{:S(2)}) collective-permute-start(bf16[8,3584]{1,0:T(8,128)(2,1)S(1)} %get-tuple-element.11), channel_id=1, source_target_pairs={{0,2},{1,3},{2,0},{3,1},{4,6},{5,7},{6,4},{7,5},{8,10},{9,11},{10,... | collective-permute-start | bytes 172040 | tf_op jit(solution)/shard_map/ppermute | solution.py:167
  26.8 1.5 %collective-permute-start.11 = (bf16[16,3584]{1,0:T(8,128)(2,1)S(1)}, bf16[16,3584]{1,0:T(8,128)(2,1)S(1)}, u32[]{:S(2)}, u32[]{:S(2)}) collective-permute-start(bf16[16,3584]{1,0:T(8,128)(2,1)S(1)} %slice.20), channel_id=1, source_target_pairs={{0,2},{1,3},{2,0},{3,1},{4,6},{5,7},{6,4},{7,5},{8,10},{9,11},{10,... | collective-permute-start | bytes 344072 | tf_op jit(solution)/shard_map/ppermute | solution.py:167
  28.4 0.0 collective-permute-done.9
  28.4 0.1 add_convert_fusion.1.whole_ref
  28.4 0.8 %collective-permute-done.15.part_ref = bf16[8,3584]{1,0:T(8,128)(2,1)S(1)} collective-permute-done((bf16[8,3584]{1,0:T(8,128)(2,1)S(1)}, bf16[8,3584]{1,0:T(8,128)(2,1)S(1)}, u32[]{:S(2)}, u32[]{:S(2)}) %collective-permute-start.15) | collective-permute-done | bytes 57376 | tf_op jit(solution)/shard_map/ppermute | solution.py:167
  29.3 1.2 %collective-permute-start.16 = (bf16[8,3584]{1,0:T(8,128)(2,1)S(1)}, bf16[8,3584]{1,0:T(8,128)(2,1)S(1)}, u32[]{:S(2)}, u32[]{:S(2)}) collective-permute-start(bf16[8,3584]{1,0:T(8,128)(2,1)S(1)} %add_rows.5), channel_id=1, source_target_pairs={{0,8},{1,9},{2,10},{3,11},{4,12},{5,13},{6,14},{7,15},{8,0},{9,1},... | collective-permute-start | bytes 172040 | tf_op jit(solution)/shard_map/ppermute | solution.py:167
  30.5 0.7 %collective-permute-done.13.part_ref = bf16[8,3584]{1,0:T(8,128)(2,1)S(1)} collective-permute-done((bf16[8,3584]{1,0:T(8,128)(2,1)S(1)}, bf16[8,3584]{1,0:T(8,128)(2,1)S(1)}, u32[]{:S(2)}, u32[]{:S(2)}) %collective-permute-start.13) | collective-permute-done | bytes 57376 | tf_op jit(solution)/shard_map/ppermute | solution.py:167
  31.2 1.5 %collective-permute-start.14 = (bf16[8,3584]{1,0:T(8,128)(2,1)S(1)}, bf16[8,3584]{1,0:T(8,128)(2,1)S(1)}, u32[]{:S(2)}, u32[]{:S(2)}) collective-permute-start(bf16[8,3584]{1,0:T(8,128)(2,1)S(1)} %add_rows.4), channel_id=1, source_target_pairs={{0,12},{1,13},{2,14},{3,15},{4,8},{5,9},{6,10},{7,11},{8,4},{9,5},... | collective-permute-start | bytes 172040 | tf_op jit(solution)/shard_map/ppermute | solution.py:167
  32.6 0.0 collective-permute-done.11.part_ref
  32.7 0.3 collective-permute-start.12
  33.1 2.3 %attend.1 = bf16[4,2,64,512]{3,2,1,0:T(8,128)(2,1)} custom-call(bf16[4,2,64,576]{3,2,1,0:T(8,128)(2,1)S(1)} %copy-done, bf16[2,576,256]{2,1,0:T(8,128)(2,1)S(1)} %bitcast.7, bf16[4,2,576]{2,1,0:T(2,128)(2,1)S(1)} %copy-done.2, s32[2]{0:T(128)S(1)} %copy-done.3), custom_call_target="tpu_custom_call" | custom-call | flops 301989888 | bytes 1769472 | tf_op jit(solution)/shard_map/attend/pallas_call | solution.py:293
  35.4 1.9 %collective-permute-done.14.refs_2_ = bf16[8,3584]{1,0:T(8,128)(2,1)S(1)} collective-permute-done((bf16[8,3584]{1,0:T(8,128)(2,1)S(1)}, bf16[8,3584]{1,0:T(8,128)(2,1)S(1)}, u32[]{:S(2)}, u32[]{:S(2)}) %collective-permute-start.14) | collective-permute-done | bytes 57376 | tf_op jit(solution)/shard_map/ppermute | solution.py:167
  37.3 0.3 collective-permute-done.12.refs_1_
  37.6 0.7 %total.1 = bf16[4,2,3584]{2,1,0:T(2,128)(2,1)} custom-call(bf16[8,3584]{1,0:T(8,128)(2,1)S(1)} %get-tuple-element.13.refs_0_, bf16[8,3584]{1,0:T(8,128)(2,1)S(1)} %collective-permute-done.12.refs_1_, bf16[8,3584]{1,0:T(8,128)(2,1)S(1)} %collective-permute-done.14.refs_2_, bf16[8,3584]{1,0:T(8,128)(2,1)S(1)} %collective-permute-done.16.refs_3_), custom_call_target="tpu_custom_call" | custom-call | tf_op jit(solution)/shard_map/total/pallas_call | solution.py:284
  (23 shorter events, 0.1 us)
Async XLA Ops:
  1.7 5.7 %collective-permute-start = (bf16[8,3712]{1,0:T(8,128)(2,1)S(1)}, bf16[8,3712]{1,0:T(8,128)(2,1)S(1)}, u32[]{:S(2)}, u32[]{:S(2)}) collective-permute-start(bf16[8,3712]{1,0:T(8,128)(2,1)S(1)} %pack.1.refs_0_), channel_id=1, source_target_pairs={{0,4},{1,5},{2,6},{3,7},{4,0},{5,1},{6,2},{7,3},{8,12},{9,13},{10,... | collective-permute-start | bytes 178184 | tf_op jit(solution)/shard_map/ppermute | solution.py:167
  4.8 6.3 %collective-permute-start.2 = (bf16[8,3712]{1,0:T(8,128)(2,1)S(1)}, bf16[8,3712]{1,0:T(8,128)(2,1)S(1)}, u32[]{:S(2)}, u32[]{:S(2)}) collective-permute-start(bf16[8,3712]{1,0:T(8,128)(2,1)S(1)} %pack.1.refs_0_), channel_id=1, source_target_pairs={{0,8},{1,9},{2,10},{3,11},{4,12},{5,13},{6,14},{7,15},{8,0},{9,1},... | collective-permute-start | bytes 178184 | tf_op jit(solution)/shard_map/ppermute | solution.py:167
  7.4 6.0 %collective-permute-start.1 = (bf16[8,3712]{1,0:T(8,128)(2,1)S(1)}, bf16[8,3712]{1,0:T(8,128)(2,1)S(1)}, u32[]{:S(2)}, u32[]{:S(2)}) collective-permute-start(bf16[8,3712]{1,0:T(8,128)(2,1)S(1)} %pack.1.refs_0_), channel_id=1, source_target_pairs={{0,12},{1,13},{2,14},{3,15},{4,8},{5,9},{6,10},{7,11},{8,4},{9,5},... | collective-permute-start | bytes 178184 | tf_op jit(solution)/shard_map/ppermute | solution.py:167
  7.4 12.3 %slice-start = ((s8[7340032]{0:T(1024)(128)(4,1)}), s8[4194304]{0:T(1024)(128)(4,1)S(1)}, s32[]{:S(2)}) async-start(s8[7340032]{0:T(1024)(128)(4,1)} %bitcast.1), calls=%async_computation | async-start | bytes 8388608
  7.4 12.3 %slice-start.2 = ((s8[7340032]{0:T(1024)(128)(4,1)}), s8[4194304]{0:T(1024)(128)(4,1)S(1)}, s32[]{:S(2)}) async-start(s8[7340032]{0:T(1024)(128)(4,1)} %bitcast.3), calls=%async_computation.2 | async-start | bytes 8388608
  7.4 12.3 %slice-start.4 = ((s8[7340032]{0:T(1024)(128)(4,1)}), s8[4194304]{0:T(1024)(128)(4,1)S(1)}, s32[]{:S(2)}) async-start(s8[7340032]{0:T(1024)(128)(4,1)} %bitcast.5), calls=%async_computation.4 | async-start | bytes 8388608
  7.5 12.2 %slice-start.1 = ((s8[7340032]{0:T(1024)(128)(4,1)}), s8[3145728]{0:T(1024)(128)(4,1)S(1)}, s32[]{:S(2)}) async-start(s8[7340032]{0:T(1024)(128)(4,1)} %bitcast.1), calls=%async_computation.1 | async-start | bytes 6291456
  7.5 12.2 %slice-start.3 = ((s8[7340032]{0:T(1024)(128)(4,1)}), s8[3145728]{0:T(1024)(128)(4,1)S(1)}, s32[]{:S(2)}) async-start(s8[7340032]{0:T(1024)(128)(4,1)} %bitcast.3), calls=%async_computation.3 | async-start | bytes 6291456
  7.5 12.2 %slice-start.5 = ((s8[7340032]{0:T(1024)(128)(4,1)}), s8[3145728]{0:T(1024)(128)(4,1)S(1)}, s32[]{:S(2)}) async-start(s8[7340032]{0:T(1024)(128)(4,1)} %bitcast.5), calls=%async_computation.5 | async-start | bytes 6291456
  7.5 8.1 %collective-permute-start.3 = (bf16[16,3712]{1,0:T(8,128)(2,1)S(1)}, bf16[16,3712]{1,0:T(8,128)(2,1)S(1)}, u32[]{:S(2)}, u32[]{:S(2)}) collective-permute-start(bf16[16,3712]{1,0:T(8,128)(2,1)S(1)} %join.2.refs_0_), channel_id=1, source_target_pairs={{0,2},{1,3},{2,0},{3,1},{4,6},{5,7},{6,4},{7,5},{8,10},{9,11},{10,... | collective-permute-start | bytes 356360 | tf_op jit(solution)/shard_map/ppermute | solution.py:167
  13.4 19.6 %copy-start = (bf16[4,2,64,576]{3,2,1,0:T(8,128)(2,1)S(1)}, bf16[4,2,64,576]{3,2,1,0:T(8,128)(2,1)}, u32[]{:S(2)}) copy-start(bf16[4,2,64,576]{3,2,1,0:T(8,128)(2,1)} %queries_ref.1) | copy-start | bytes 1769476
  13.4 19.6 %copy-start.1 = (bf16[2,256,576]{1,2,0:T(8,128)(2,1)S(1)}, bf16[2,256,576]{1,2,0:T(8,128)(2,1)}, u32[]{:S(2)}) copy-start(bf16[2,256,576]{1,2,0:T(8,128)(2,1)} %param.13) | copy-start | bytes 1769476
  13.5 19.6 %copy-start.2 = (bf16[4,2,576]{2,1,0:T(2,128)(2,1)S(1)}, bf16[4,2,576]{2,1,0:T(2,128)(2,1)}, u32[]{:S(2)}) copy-start(bf16[4,2,576]{2,1,0:T(2,128)(2,1)} %new_ref.1) | copy-start | bytes 27652
  13.5 19.6 %copy-start.3 = (s32[2]{0:T(128)S(1)}, s32[2]{0:T(128)}, u32[]{:S(2)}) copy-start(s32[2]{0:T(128)} %lengths_ref.1) | copy-start | bytes 28
  13.5 4.9 %collective-permute-start.4 = (bf16[16,3712]{1,0:T(8,128)(2,1)S(1)}, bf16[16,3712]{1,0:T(8,128)(2,1)S(1)}, u32[]{:S(2)}, u32[]{:S(2)}) collective-permute-start(bf16[16,3712]{1,0:T(8,128)(2,1)S(1)} %join.3.refs_1_), channel_id=1, source_target_pairs={{0,2},{1,3},{2,0},{3,1},{4,6},{5,7},{6,4},{7,5},{8,10},{9,11},{10,... | collective-permute-start | bytes 356360 | tf_op jit(solution)/shard_map/ppermute | solution.py:167
  15.1 3.3 %collective-permute-start.5 = (bf16[16,3712]{1,0:T(8,128)(2,1)S(1)}, bf16[16,3712]{1,0:T(8,128)(2,1)S(1)}, u32[]{:S(2)}, u32[]{:S(2)}) collective-permute-start(bf16[16,3712]{1,0:T(8,128)(2,1)S(1)} %join.2.refs_0_), channel_id=1, source_target_pairs={{0,1},{1,0},{2,3},{3,2},{4,5},{5,4},{6,7},{7,6},{8,9},{9,8},{10,11... | collective-permute-start | bytes 356360 | tf_op jit(solution)/shard_map/ppermute | solution.py:167
  15.1 3.3 %collective-permute-start.6 = (bf16[16,3712]{1,0:T(8,128)(2,1)S(1)}, bf16[16,3712]{1,0:T(8,128)(2,1)S(1)}, u32[]{:S(2)}, u32[]{:S(2)}) collective-permute-start(bf16[16,3712]{1,0:T(8,128)(2,1)S(1)} %join.3.refs_1_), channel_id=1, source_target_pairs={{0,1},{1,0},{2,3},{3,2},{4,5},{5,4},{6,7},{7,6},{8,9},{9,8},{10,11... | collective-permute-start | bytes 356360 | tf_op jit(solution)/shard_map/ppermute | solution.py:167
  15.6 2.8 %collective-permute-start.7 = (bf16[16,3712]{1,0:T(8,128)(2,1)S(1)}, bf16[16,3712]{1,0:T(8,128)(2,1)S(1)}, u32[]{:S(2)}, u32[]{:S(2)}) collective-permute-start(bf16[16,3712]{1,0:T(8,128)(2,1)S(1)} %collective-permute-done.3.refs_2_), channel_id=1, source_target_pairs={{0,1},{1,0},{2,3},{3,2},{4,5},{5,4},{6,7},{7,6},{8,9},{9,8},{10,11... | collective-permute-start | bytes 356360 | tf_op jit(solution)/shard_map/ppermute | solution.py:167
  18.4 1.3 %collective-permute-start.8 = (bf16[16,3712]{1,0:T(8,128)(2,1)S(1)}, bf16[16,3712]{1,0:T(8,128)(2,1)S(1)}, u32[]{:S(2)}, u32[]{:S(2)}) collective-permute-start(bf16[16,3712]{1,0:T(8,128)(2,1)S(1)} %collective-permute-done.4.refs_3_), channel_id=1, source_target_pairs={{0,1},{1,0},{2,3},{3,2},{4,5},{5,4},{6,7},{7,6},{8,9},{9,8},{10,11... | collective-permute-start | bytes 356360 | tf_op jit(solution)/shard_map/ppermute | solution.py:167
  23.1 1.6 %collective-permute-start.10 = (bf16[32,3584]{1,0:T(8,128)(2,1)S(1)}, bf16[32,3584]{1,0:T(8,128)(2,1)S(1)}, u32[]{:S(2)}, u32[]{:S(2)}) collective-permute-start(bf16[32,3584]{1,0:T(8,128)(2,1)S(1)} %get-tuple-element.9), channel_id=1, source_target_pairs={{0,1},{1,0},{2,3},{3,2},{4,5},{5,4},{6,7},{7,6},{8,9},{9,8},{10,11... | collective-permute-start | bytes 688136 | tf_op jit(solution)/shard_map/ppermute | solution.py:167
  23.3 5.1 %collective-permute-start.9 = (bf16[32,3584]{1,0:T(8,128)(2,1)S(1)}, bf16[32,3584]{1,0:T(8,128)(2,1)S(1)}, u32[]{:S(2)}, u32[]{:S(2)}) collective-permute-start(bf16[32,3584]{1,0:T(8,128)(2,1)S(1)} %get-tuple-element.7), channel_id=1, source_target_pairs={{0,1},{1,0},{2,3},{3,2},{4,5},{5,4},{6,7},{7,6},{8,9},{9,8},{10,11... | collective-permute-start | bytes 688136 | tf_op jit(solution)/shard_map/ppermute | solution.py:167
  24.8 4.5 %collective-permute-start.15 = (bf16[8,3584]{1,0:T(8,128)(2,1)S(1)}, bf16[8,3584]{1,0:T(8,128)(2,1)S(1)}, u32[]{:S(2)}, u32[]{:S(2)}) collective-permute-start(bf16[8,3584]{1,0:T(8,128)(2,1)S(1)} %get-tuple-element.10), channel_id=1, source_target_pairs={{0,2},{1,3},{2,0},{3,1},{4,6},{5,7},{6,4},{7,5},{8,10},{9,11},{10,... | collective-permute-start | bytes 172040 | tf_op jit(solution)/shard_map/ppermute | solution.py:167
  26.4 4.8 %collective-permute-start.13 = (bf16[8,3584]{1,0:T(8,128)(2,1)S(1)}, bf16[8,3584]{1,0:T(8,128)(2,1)S(1)}, u32[]{:S(2)}, u32[]{:S(2)}) collective-permute-start(bf16[8,3584]{1,0:T(8,128)(2,1)S(1)} %get-tuple-element.11), channel_id=1, source_target_pairs={{0,2},{1,3},{2,0},{3,1},{4,6},{5,7},{6,4},{7,5},{8,10},{9,11},{10,... | collective-permute-start | bytes 172040 | tf_op jit(solution)/shard_map/ppermute | solution.py:167
  26.8 5.8 %collective-permute-start.11 = (bf16[16,3584]{1,0:T(8,128)(2,1)S(1)}, bf16[16,3584]{1,0:T(8,128)(2,1)S(1)}, u32[]{:S(2)}, u32[]{:S(2)}) collective-permute-start(bf16[16,3584]{1,0:T(8,128)(2,1)S(1)} %slice.20), channel_id=1, source_target_pairs={{0,2},{1,3},{2,0},{3,1},{4,6},{5,7},{6,4},{7,5},{8,10},{9,11},{10,... | collective-permute-start | bytes 344072 | tf_op jit(solution)/shard_map/ppermute | solution.py:167
  29.3 6.1 %collective-permute-start.16 = (bf16[8,3584]{1,0:T(8,128)(2,1)S(1)}, bf16[8,3584]{1,0:T(8,128)(2,1)S(1)}, u32[]{:S(2)}, u32[]{:S(2)}) collective-permute-start(bf16[8,3584]{1,0:T(8,128)(2,1)S(1)} %add_rows.5), channel_id=1, source_target_pairs={{0,8},{1,9},{2,10},{3,11},{4,12},{5,13},{6,14},{7,15},{8,0},{9,1},... | collective-permute-start | bytes 172040 | tf_op jit(solution)/shard_map/ppermute | solution.py:167
  31.2 6.1 %collective-permute-start.14 = (bf16[8,3584]{1,0:T(8,128)(2,1)S(1)}, bf16[8,3584]{1,0:T(8,128)(2,1)S(1)}, u32[]{:S(2)}, u32[]{:S(2)}) collective-permute-start(bf16[8,3584]{1,0:T(8,128)(2,1)S(1)} %add_rows.4), channel_id=1, source_target_pairs={{0,12},{1,13},{2,14},{3,15},{4,8},{5,9},{6,10},{7,11},{8,4},{9,5},... | collective-permute-start | bytes 172040 | tf_op jit(solution)/shard_map/ppermute | solution.py:167
  32.7 4.9 %collective-permute-start.12 = (bf16[8,3584]{1,0:T(8,128)(2,1)S(1)}, bf16[8,3584]{1,0:T(8,128)(2,1)S(1)}, u32[]{:S(2)}, u32[]{:S(2)}) collective-permute-start(bf16[8,3584]{1,0:T(8,128)(2,1)S(1)} %get-tuple-element.12), channel_id=1, source_target_pairs={{0,4},{1,5},{2,6},{3,7},{4,0},{5,1},{6,2},{7,3},{8,12},{9,13},{10,... | collective-permute-start | bytes 172040 | tf_op jit(solution)/shard_map/ppermute | solution.py:167

commit v6 on v5

--- a/solution.py
+++ b/solution.py
@@ -247,7 +247,7 @@
     parts = parts + [swap(part, 1) for part in parts]
 
     count = 16 * size
-    tile = min(256, units)
+    tile = min(512, units)
     half = jax.ShapeDtypeStruct((4 * size, width), jnp.bfloat16)
     keep_far, send_far, keep_near, send_near = pl.pallas_call(
         functools.partial(expert_kernel, experts, tile, len(parts)),

time: 38.4 us -> 38.2 us (level)
  no operation moved by 1% of the time
where the time goes in v6:
time: 38.2 us; the launch traced here: 38 us
  starting transfers between devices  16.8 us (44%)
  waiting for transfers between devices  13 us (34%)
  Pallas kernels  7.25 us (19%)
  between operations  0.87 us (2%)
    ppermute x17, starting transfers between devices, swap(): return lax.ppermute(value, PEERS, [(i, i ^ mask) for i in range(size)])  16.8 us
    ppermute x17, waiting for transfers between devices, swap(): return lax.ppermute(value, PEERS, [(i, i ^ mask) for i in range(size)])  13 us
    pallas_call x1, Pallas kernels, per_device(): pl.pallas_call(functools.partial(expert_kernel, experts, tile, len(parts)...  3.1 us
    pallas_call x1, Pallas kernels, per_device(): pl.pallas_call(attend_kernel, out_shape=jax.ShapeDtypeStruct((steps, rows...  2.3 us
    pallas_call x1, Pallas kernels, per_device(): pl.pallas_call(functools.partial(pack_kernel, experts), out_shape=jax.Sha...  1.1 us
  transfers between devices with their start and end apart: 17, of which 9 were waited for; matrix products, arithmetic and copies ran while one was open for 0% of the time, Pallas kernels for 6%

profile of v6, /device:TPU:0, one launch (start us, length us, event | category | flops | bytes accessed | tf_op | source)
XLA Modules:
  0.0 38.0 jit_solution(7912213515551929601)
XLA Ops:
  0.6 1.1 %pack.1.refs_0_ = bf16[8,3712]{1,0:T(8,128)(2,1)S(1)} custom-call(bf16[4,2,3584]{2,1,0:T(2,128)(2,1)} %refs_0_.1, s32[2,2,8]{2,1,0:T(2,128)} %refs_1_.1, s32[2,2,8]{2,1,0:T(2,128)} %refs_2_.1, f32[4,2,8]{2,1,0:T(2,128)} %refs_3_.1, s32[2]{0:T(128)} %refs_4_.1), custom_call_target="tpu_custom_call" | custom-call | tf_op jit(solution)/shard_map/pack/pallas_call | solution.py:223
  1.7 3.1 %collective-permute-start = (bf16[8,3712]{1,0:T(8,128)(2,1)S(1)}, bf16[8,3712]{1,0:T(8,128)(2,1)S(1)}, u32[]{:S(2)}, u32[]{:S(2)}) collective-permute-start(bf16[8,3712]{1,0:T(8,128)(2,1)S(1)} %pack.1.refs_0_), channel_id=1, source_target_pairs={{0,4},{1,5},{2,6},{3,7},{4,0},{5,1},{6,2},{7,3},{8,12},{9,13},{10,... | collective-permute-start | bytes 178184 | tf_op jit(solution)/shard_map/ppermute | solution.py:167
  4.8 2.6 %collective-permute-start.2 = (bf16[8,3712]{1,0:T(8,128)(2,1)S(1)}, bf16[8,3712]{1,0:T(8,128)(2,1)S(1)}, u32[]{:S(2)}, u32[]{:S(2)}) collective-permute-start(bf16[8,3712]{1,0:T(8,128)(2,1)S(1)} %pack.1.refs_0_), channel_id=1, source_target_pairs={{0,8},{1,9},{2,10},{3,11},{4,12},{5,13},{6,14},{7,15},{8,0},{9,1},... | collective-permute-start | bytes 178184 | tf_op jit(solution)/shard_map/ppermute | solution.py:167
  7.4 0.0 collective-permute-done.refs_1_
  7.4 0.0 slice-start.2
  7.4 0.0 slice-start.4
  7.5 0.0 slice-start.1
  7.5 0.0 slice-start.3
  7.5 0.0 slice-start.5
  7.5 1.8 %collective-permute-start.3 = (bf16[16,3712]{1,0:T(8,128)(2,1)S(1)}, bf16[16,3712]{1,0:T(8,128)(2,1)S(1)}, u32[]{:S(2)}, u32[]{:S(2)}) collective-permute-start(bf16[16,3712]{1,0:T(8,128)(2,1)S(1)} %join.2.refs_0_), channel_id=1, source_target_pairs={{0,2},{1,3},{2,0},{3,1},{4,6},{5,7},{6,4},{7,5},{8,10},{9,11},{10,... | collective-permute-start | bytes 356360 | tf_op jit(solution)/shard_map/ppermute | solution.py:167
  9.3 1.8 %collective-permute-done.2.refs_1_ = bf16[8,3712]{1,0:T(8,128)(2,1)S(1)} collective-permute-done((bf16[8,3712]{1,0:T(8,128)(2,1)S(1)}, bf16[8,3712]{1,0:T(8,128)(2,1)S(1)}, u32[]{:S(2)}, u32[]{:S(2)}) %collective-permute-start.2) | collective-permute-done | bytes 59424 | tf_op jit(solution)/shard_map/ppermute | solution.py:167
  11.1 2.3 %collective-permute-done.1.refs_0_ = bf16[8,3712]{1,0:T(8,128)(2,1)S(1)} collective-permute-done((bf16[8,3712]{1,0:T(8,128)(2,1)S(1)}, bf16[8,3712]{1,0:T(8,128)(2,1)S(1)}, u32[]{:S(2)}, u32[]{:S(2)}) %collective-permute-start.1) | collective-permute-done | bytes 59424 | tf_op jit(solution)/shard_map/ppermute | solution.py:167
  13.4 0.0 copy-start
  13.4 0.0 copy-start.1
  13.5 0.0 copy-start.2
  13.5 0.0 copy-start.3
  13.5 1.6 %collective-permute-start.4 = (bf16[16,3712]{1,0:T(8,128)(2,1)S(1)}, bf16[16,3712]{1,0:T(8,128)(2,1)S(1)}, u32[]{:S(2)}, u32[]{:S(2)}) collective-permute-start(bf16[16,3712]{1,0:T(8,128)(2,1)S(1)} %join.3.refs_1_), channel_id=1, source_target_pairs={{0,2},{1,3},{2,0},{3,1},{4,6},{5,7},{6,4},{7,5},{8,10},{9,11},{10,... | collective-permute-start | bytes 356360 | tf_op jit(solution)/shard_map/ppermute | solution.py:167
  15.1 0.0 collective-permute-start.5
  15.1 0.5 %collective-permute-start.6 = (bf16[16,3712]{1,0:T(8,128)(2,1)S(1)}, bf16[16,3712]{1,0:T(8,128)(2,1)S(1)}, u32[]{:S(2)}, u32[]{:S(2)}) collective-permute-start(bf16[16,3712]{1,0:T(8,128)(2,1)S(1)} %join.3.refs_1_), channel_id=1, source_target_pairs={{0,1},{1,0},{2,3},{3,2},{4,5},{5,4},{6,7},{7,6},{8,9},{9,8},{10,11... | collective-permute-start | bytes 356360 | tf_op jit(solution)/shard_map/ppermute | solution.py:167
  15.6 0.0 collective-permute-done.3.refs_2_
  15.6 0.0 collective-permute-start.7
  15.6 2.8 %collective-permute-done.4.refs_3_ = bf16[16,3712]{1,0:T(8,128)(2,1)S(1)} collective-permute-done((bf16[16,3712]{1,0:T(8,128)(2,1)S(1)}, bf16[16,3712]{1,0:T(8,128)(2,1)S(1)}, u32[]{:S(2)}, u32[]{:S(2)}) %collective-permute-start.4) | collective-permute-done | bytes 118816 | tf_op jit(solution)/shard_map/ppermute | solution.py:167
  18.4 0.0 collective-permute-start.8
  18.4 0.0 collective-permute-done.5.refs_4_
  18.4 0.0 collective-permute-done.6.refs_5_
  18.4 0.0 collective-permute-done.7.refs_6_
  18.4 1.3 %collective-permute-done.8.refs_7_ = bf16[16,3712]{1,0:T(8,128)(2,1)S(1)} collective-permute-done((bf16[16,3712]{1,0:T(8,128)(2,1)S(1)}, bf16[16,3712]{1,0:T(8,128)(2,1)S(1)}, u32[]{:S(2)}, u32[]{:S(2)}) %collective-permute-start.8) | collective-permute-done | bytes 118816 | tf_op jit(solution)/shard_map/ppermute | solution.py:167
  19.8 3.1 %experts.1 = (bf16[32,3584]{1,0:T(8,128)(2,1)S(1)}, bf16[32,3584]{1,0:T(8,128)(2,1)S(1)}, bf16[32,3584]{1,0:T(8,128)(2,1)S(1)}, bf16[32,3584]{1,0:T(8,128)(2,1)S(1)}) custom-call(bf16[16,3712]{1,0:T(8,128)(2,1)S(1)} %join.2.refs_0_, bf16[16,3712]{1,0:T(8,128)(2,1)S(1)} %join.3.refs_1_, bf16[16,3712]{1,0:T(8,128)(2,1)S(1)} %collective-permute-done.3.refs_2_, ...), custom_call_target="tpu_custom_call" | custom-call | flops 2818572288 | bytes 22020096 | tf_op jit(solution)/shard_map/experts/pallas_call | solution.py:252
  22.9 0.2 collective-permute-start.10
  23.1 0.4 collective-permute-start.9
  23.5 1.0 %collective-permute-done.10 = bf16[32,3584]{1,0:T(8,128)(2,1)S(1)} collective-permute-done((bf16[32,3584]{1,0:T(8,128)(2,1)S(1)}, bf16[32,3584]{1,0:T(8,128)(2,1)S(1)}, u32[]{:S(2)}, u32[]{:S(2)}) %collective-permute-start.10) | collective-permute-done | bytes 229408 | tf_op jit(solution)/shard_map/ppermute | solution.py:167
  24.4 0.1 add_convert_fusion
  24.5 1.6 %collective-permute-start.15 = (bf16[8,3584]{1,0:T(8,128)(2,1)S(1)}, bf16[8,3584]{1,0:T(8,128)(2,1)S(1)}, u32[]{:S(2)}, u32[]{:S(2)}) collective-permute-start(bf16[8,3584]{1,0:T(8,128)(2,1)S(1)} %get-tuple-element.10), channel_id=1, source_target_pairs={{0,2},{1,3},{2,0},{3,1},{4,6},{5,7},{6,4},{7,5},{8,10},{9,11},{10,... | collective-permute-start | bytes 172040 | tf_op jit(solution)/shard_map/ppermute | solution.py:167
  26.1 0.5 %collective-permute-start.13 = (bf16[8,3584]{1,0:T(8,128)(2,1)S(1)}, bf16[8,3584]{1,0:T(8,128)(2,1)S(1)}, u32[]{:S(2)}, u32[]{:S(2)}) collective-permute-start(bf16[8,3584]{1,0:T(8,128)(2,1)S(1)} %get-tuple-element.11), channel_id=1, source_target_pairs={{0,2},{1,3},{2,0},{3,1},{4,6},{5,7},{6,4},{7,5},{8,10},{9,11},{10,... | collective-permute-start | bytes 172040 | tf_op jit(solution)/shard_map/ppermute | solution.py:167
  26.6 1.5 %collective-permute-start.11 = (bf16[16,3584]{1,0:T(8,128)(2,1)S(1)}, bf16[16,3584]{1,0:T(8,128)(2,1)S(1)}, u32[]{:S(2)}, u32[]{:S(2)}) collective-permute-start(bf16[16,3584]{1,0:T(8,128)(2,1)S(1)} %slice.20), channel_id=1, source_target_pairs={{0,2},{1,3},{2,0},{3,1},{4,6},{5,7},{6,4},{7,5},{8,10},{9,11},{10,... | collective-permute-start | bytes 344072 | tf_op jit(solution)/shard_map/ppermute | solution.py:167
  28.2 0.0 collective-permute-done.9
  28.2 0.1 add_convert_fusion.1.whole_ref
  28.2 0.8 %collective-permute-done.15.part_ref = bf16[8,3584]{1,0:T(8,128)(2,1)S(1)} collective-permute-done((bf16[8,3584]{1,0:T(8,128)(2,1)S(1)}, bf16[8,3584]{1,0:T(8,128)(2,1)S(1)}, u32[]{:S(2)}, u32[]{:S(2)}) %collective-permute-start.15) | collective-permute-done | bytes 57376 | tf_op jit(solution)/shard_map/ppermute | solution.py:167
  29.1 1.2 %collective-permute-start.16 = (bf16[8,3584]{1,0:T(8,128)(2,1)S(1)}, bf16[8,3584]{1,0:T(8,128)(2,1)S(1)}, u32[]{:S(2)}, u32[]{:S(2)}) collective-permute-start(bf16[8,3584]{1,0:T(8,128)(2,1)S(1)} %add_rows.5), channel_id=1, source_target_pairs={{0,8},{1,9},{2,10},{3,11},{4,12},{5,13},{6,14},{7,15},{8,0},{9,1},... | collective-permute-start | bytes 172040 | tf_op jit(solution)/shard_map/ppermute | solution.py:167
  30.3 0.7 %collective-permute-done.13.part_ref = bf16[8,3584]{1,0:T(8,128)(2,1)S(1)} collective-permute-done((bf16[8,3584]{1,0:T(8,128)(2,1)S(1)}, bf16[8,3584]{1,0:T(8,128)(2,1)S(1)}, u32[]{:S(2)}, u32[]{:S(2)}) %collective-permute-start.13) | collective-permute-done | bytes 57376 | tf_op jit(solution)/shard_map/ppermute | solution.py:167
  31.0 1.5 %collective-permute-start.14 = (bf16[8,3584]{1,0:T(8,128)(2,1)S(1)}, bf16[8,3584]{1,0:T(8,128)(2,1)S(1)}, u32[]{:S(2)}, u32[]{:S(2)}) collective-permute-start(bf16[8,3584]{1,0:T(8,128)(2,1)S(1)} %add_rows.4), channel_id=1, source_target_pairs={{0,12},{1,13},{2,14},{3,15},{4,8},{5,9},{6,10},{7,11},{8,4},{9,5},... | collective-permute-start | bytes 172040 | tf_op jit(solution)/shard_map/ppermute | solution.py:167
  32.4 0.0 collective-permute-done.11.part_ref
  32.5 0.3 collective-permute-start.12
  32.9 2.3 %attend.1 = bf16[4,2,64,512]{3,2,1,0:T(8,128)(2,1)} custom-call(bf16[4,2,64,576]{3,2,1,0:T(8,128)(2,1)S(1)} %copy-done, bf16[2,576,256]{2,1,0:T(8,128)(2,1)S(1)} %bitcast.7, bf16[4,2,576]{2,1,0:T(2,128)(2,1)S(1)} %copy-done.2, s32[2]{0:T(128)S(1)} %copy-done.3), custom_call_target="tpu_custom_call" | custom-call | flops 301989888 | bytes 1769472 | tf_op jit(solution)/shard_map/attend/pallas_call | solution.py:293
  35.2 0.0 collective-permute-done.16.refs_3_
  35.2 1.9 %collective-permute-done.14.refs_2_ = bf16[8,3584]{1,0:T(8,128)(2,1)S(1)} collective-permute-done((bf16[8,3584]{1,0:T(8,128)(2,1)S(1)}, bf16[8,3584]{1,0:T(8,128)(2,1)S(1)}, u32[]{:S(2)}, u32[]{:S(2)}) %collective-permute-start.14) | collective-permute-done | bytes 57376 | tf_op jit(solution)/shard_map/ppermute | solution.py:167
  37.1 0.3 collective-permute-done.12.refs_1_
  37.4 0.7 %total.1 = bf16[4,2,3584]{2,1,0:T(2,128)(2,1)} custom-call(bf16[8,3584]{1,0:T(8,128)(2,1)S(1)} %get-tuple-element.13.refs_0_, bf16[8,3584]{1,0:T(8,128)(2,1)S(1)} %collective-permute-done.12.refs_1_, bf16[8,3584]{1,0:T(8,128)(2,1)S(1)} %collective-permute-done.14.refs_2_, bf16[8,3584]{1,0:T(8,128)(2,1)S(1)} %collective-permute-done.16.refs_3_), custom_call_target="tpu_custom_call" | custom-call | tf_op jit(solution)/shard_map/total/pallas_call | solution.py:284
  (23 shorter events, 0.1 us)
Async XLA Ops:
  1.7 5.7 %collective-permute-start = (bf16[8,3712]{1,0:T(8,128)(2,1)S(1)}, bf16[8,3712]{1,0:T(8,128)(2,1)S(1)}, u32[]{:S(2)}, u32[]{:S(2)}) collective-permute-start(bf16[8,3712]{1,0:T(8,128)(2,1)S(1)} %pack.1.refs_0_), channel_id=1, source_target_pairs={{0,4},{1,5},{2,6},{3,7},{4,0},{5,1},{6,2},{7,3},{8,12},{9,13},{10,... | collective-permute-start | bytes 178184 | tf_op jit(solution)/shard_map/ppermute | solution.py:167
  4.8 6.3 %collective-permute-start.2 = (bf16[8,3712]{1,0:T(8,128)(2,1)S(1)}, bf16[8,3712]{1,0:T(8,128)(2,1)S(1)}, u32[]{:S(2)}, u32[]{:S(2)}) collective-permute-start(bf16[8,3712]{1,0:T(8,128)(2,1)S(1)} %pack.1.refs_0_), channel_id=1, source_target_pairs={{0,8},{1,9},{2,10},{3,11},{4,12},{5,13},{6,14},{7,15},{8,0},{9,1},... | collective-permute-start | bytes 178184 | tf_op jit(solution)/shard_map/ppermute | solution.py:167
  7.4 6.0 %collective-permute-start.1 = (bf16[8,3712]{1,0:T(8,128)(2,1)S(1)}, bf16[8,3712]{1,0:T(8,128)(2,1)S(1)}, u32[]{:S(2)}, u32[]{:S(2)}) collective-permute-start(bf16[8,3712]{1,0:T(8,128)(2,1)S(1)} %pack.1.refs_0_), channel_id=1, source_target_pairs={{0,12},{1,13},{2,14},{3,15},{4,8},{5,9},{6,10},{7,11},{8,4},{9,5},... | collective-permute-start | bytes 178184 | tf_op jit(solution)/shard_map/ppermute | solution.py:167
  7.4 12.3 %slice-start = ((s8[7340032]{0:T(1024)(128)(4,1)}), s8[4194304]{0:T(1024)(128)(4,1)S(1)}, s32[]{:S(2)}) async-start(s8[7340032]{0:T(1024)(128)(4,1)} %bitcast.1), calls=%async_computation | async-start | bytes 8388608
  7.4 12.3 %slice-start.2 = ((s8[7340032]{0:T(1024)(128)(4,1)}), s8[4194304]{0:T(1024)(128)(4,1)S(1)}, s32[]{:S(2)}) async-start(s8[7340032]{0:T(1024)(128)(4,1)} %bitcast.3), calls=%async_computation.2 | async-start | bytes 8388608
  7.4 12.3 %slice-start.4 = ((s8[7340032]{0:T(1024)(128)(4,1)}), s8[4194304]{0:T(1024)(128)(4,1)S(1)}, s32[]{:S(2)}) async-start(s8[7340032]{0:T(1024)(128)(4,1)} %bitcast.5), calls=%async_computation.4 | async-start | bytes 8388608
  7.5 12.2 %slice-start.1 = ((s8[7340032]{0:T(1024)(128)(4,1)}), s8[3145728]{0:T(1024)(128)(4,1)S(1)}, s32[]{:S(2)}) async-start(s8[7340032]{0:T(1024)(128)(4,1)} %bitcast.1), calls=%async_computation.1 | async-start | bytes 6291456
  7.5 12.2 %slice-start.3 = ((s8[7340032]{0:T(1024)(128)(4,1)}), s8[3145728]{0:T(1024)(128)(4,1)S(1)}, s32[]{:S(2)}) async-start(s8[7340032]{0:T(1024)(128)(4,1)} %bitcast.3), calls=%async_computation.3 | async-start | bytes 6291456
  7.5 12.2 %slice-start.5 = ((s8[7340032]{0:T(1024)(128)(4,1)}), s8[3145728]{0:T(1024)(128)(4,1)S(1)}, s32[]{:S(2)}) async-start(s8[7340032]{0:T(1024)(128)(4,1)} %bitcast.5), calls=%async_computation.5 | async-start | bytes 6291456
  7.5 8.1 %collective-permute-start.3 = (bf16[16,3712]{1,0:T(8,128)(2,1)S(1)}, bf16[16,3712]{1,0:T(8,128)(2,1)S(1)}, u32[]{:S(2)}, u32[]{:S(2)}) collective-permute-start(bf16[16,3712]{1,0:T(8,128)(2,1)S(1)} %join.2.refs_0_), channel_id=1, source_target_pairs={{0,2},{1,3},{2,0},{3,1},{4,6},{5,7},{6,4},{7,5},{8,10},{9,11},{10,... | collective-permute-start | bytes 356360 | tf_op jit(solution)/shard_map/ppermute | solution.py:167
  13.4 19.4 %copy-start = (bf16[4,2,64,576]{3,2,1,0:T(8,128)(2,1)S(1)}, bf16[4,2,64,576]{3,2,1,0:T(8,128)(2,1)}, u32[]{:S(2)}) copy-start(bf16[4,2,64,576]{3,2,1,0:T(8,128)(2,1)} %queries_ref.1) | copy-start | bytes 1769476
  13.4 19.4 %copy-start.1 = (bf16[2,256,576]{1,2,0:T(8,128)(2,1)S(1)}, bf16[2,256,576]{1,2,0:T(8,128)(2,1)}, u32[]{:S(2)}) copy-start(bf16[2,256,576]{1,2,0:T(8,128)(2,1)} %param.13) | copy-start | bytes 1769476
  13.5 19.4 %copy-start.2 = (bf16[4,2,576]{2,1,0:T(2,128)(2,1)S(1)}, bf16[4,2,576]{2,1,0:T(2,128)(2,1)}, u32[]{:S(2)}) copy-start(bf16[4,2,576]{2,1,0:T(2,128)(2,1)} %new_ref.1) | copy-start | bytes 27652
  13.5 19.4 %copy-start.3 = (s32[2]{0:T(128)S(1)}, s32[2]{0:T(128)}, u32[]{:S(2)}) copy-start(s32[2]{0:T(128)} %lengths_ref.1) | copy-start | bytes 28
  13.5 4.9 %collective-permute-start.4 = (bf16[16,3712]{1,0:T(8,128)(2,1)S(1)}, bf16[16,3712]{1,0:T(8,128)(2,1)S(1)}, u32[]{:S(2)}, u32[]{:S(2)}) collective-permute-start(bf16[16,3712]{1,0:T(8,128)(2,1)S(1)} %join.3.refs_1_), channel_id=1, source_target_pairs={{0,2},{1,3},{2,0},{3,1},{4,6},{5,7},{6,4},{7,5},{8,10},{9,11},{10,... | collective-permute-start | bytes 356360 | tf_op jit(solution)/shard_map/ppermute | solution.py:167
  15.1 3.3 %collective-permute-start.5 = (bf16[16,3712]{1,0:T(8,128)(2,1)S(1)}, bf16[16,3712]{1,0:T(8,128)(2,1)S(1)}, u32[]{:S(2)}, u32[]{:S(2)}) collective-permute-start(bf16[16,3712]{1,0:T(8,128)(2,1)S(1)} %join.2.refs_0_), channel_id=1, source_target_pairs={{0,1},{1,0},{2,3},{3,2},{4,5},{5,4},{6,7},{7,6},{8,9},{9,8},{10,11... | collective-permute-start | bytes 356360 | tf_op jit(solution)/shard_map/ppermute | solution.py:167
  15.1 3.3 %collective-permute-start.6 = (bf16[16,3712]{1,0:T(8,128)(2,1)S(1)}, bf16[16,3712]{1,0:T(8,128)(2,1)S(1)}, u32[]{:S(2)}, u32[]{:S(2)}) collective-permute-start(bf16[16,3712]{1,0:T(8,128)(2,1)S(1)} %join.3.refs_1_), channel_id=1, source_target_pairs={{0,1},{1,0},{2,3},{3,2},{4,5},{5,4},{6,7},{7,6},{8,9},{9,8},{10,11... | collective-permute-start | bytes 356360 | tf_op jit(solution)/shard_map/ppermute | solution.py:167
  15.6 2.8 %collective-permute-start.7 = (bf16[16,3712]{1,0:T(8,128)(2,1)S(1)}, bf16[16,3712]{1,0:T(8,128)(2,1)S(1)}, u32[]{:S(2)}, u32[]{:S(2)}) collective-permute-start(bf16[16,3712]{1,0:T(8,128)(2,1)S(1)} %collective-permute-done.3.refs_2_), channel_id=1, source_target_pairs={{0,1},{1,0},{2,3},{3,2},{4,5},{5,4},{6,7},{7,6},{8,9},{9,8},{10,11... | collective-permute-start | bytes 356360 | tf_op jit(solution)/shard_map/ppermute | solution.py:167
  18.4 1.3 %collective-permute-start.8 = (bf16[16,3712]{1,0:T(8,128)(2,1)S(1)}, bf16[16,3712]{1,0:T(8,128)(2,1)S(1)}, u32[]{:S(2)}, u32[]{:S(2)}) collective-permute-start(bf16[16,3712]{1,0:T(8,128)(2,1)S(1)} %collective-permute-done.4.refs_3_), channel_id=1, source_target_pairs={{0,1},{1,0},{2,3},{3,2},{4,5},{5,4},{6,7},{7,6},{8,9},{9,8},{10,11... | collective-permute-start | bytes 356360 | tf_op jit(solution)/shard_map/ppermute | solution.py:167
  22.9 1.6 %collective-permute-start.10 = (bf16[32,3584]{1,0:T(8,128)(2,1)S(1)}, bf16[32,3584]{1,0:T(8,128)(2,1)S(1)}, u32[]{:S(2)}, u32[]{:S(2)}) collective-permute-start(bf16[32,3584]{1,0:T(8,128)(2,1)S(1)} %get-tuple-element.9), channel_id=1, source_target_pairs={{0,1},{1,0},{2,3},{3,2},{4,5},{5,4},{6,7},{7,6},{8,9},{9,8},{10,11... | collective-permute-start | bytes 688136 | tf_op jit(solution)/shard_map/ppermute | solution.py:167
  23.1 5.1 %collective-permute-start.9 = (bf16[32,3584]{1,0:T(8,128)(2,1)S(1)}, bf16[32,3584]{1,0:T(8,128)(2,1)S(1)}, u32[]{:S(2)}, u32[]{:S(2)}) collective-permute-start(bf16[32,3584]{1,0:T(8,128)(2,1)S(1)} %get-tuple-element.7), channel_id=1, source_target_pairs={{0,1},{1,0},{2,3},{3,2},{4,5},{5,4},{6,7},{7,6},{8,9},{9,8},{10,11... | collective-permute-start | bytes 688136 | tf_op jit(solution)/shard_map/ppermute | solution.py:167
  24.5 4.5 %collective-permute-start.15 = (bf16[8,3584]{1,0:T(8,128)(2,1)S(1)}, bf16[8,3584]{1,0:T(8,128)(2,1)S(1)}, u32[]{:S(2)}, u32[]{:S(2)}) collective-permute-start(bf16[8,3584]{1,0:T(8,128)(2,1)S(1)} %get-tuple-element.10), channel_id=1, source_target_pairs={{0,2},{1,3},{2,0},{3,1},{4,6},{5,7},{6,4},{7,5},{8,10},{9,11},{10,... | collective-permute-start | bytes 172040 | tf_op jit(solution)/shard_map/ppermute | solution.py:167
  26.1 4.8 %collective-permute-start.13 = (bf16[8,3584]{1,0:T(8,128)(2,1)S(1)}, bf16[8,3584]{1,0:T(8,128)(2,1)S(1)}, u32[]{:S(2)}, u32[]{:S(2)}) collective-permute-start(bf16[8,3584]{1,0:T(8,128)(2,1)S(1)} %get-tuple-element.11), channel_id=1, source_target_pairs={{0,2},{1,3},{2,0},{3,1},{4,6},{5,7},{6,4},{7,5},{8,10},{9,11},{10,... | collective-permute-start | bytes 172040 | tf_op jit(solution)/shard_map/ppermute | solution.py:167
  26.6 5.8 %collective-permute-start.11 = (bf16[16,3584]{1,0:T(8,128)(2,1)S(1)}, bf16[16,3584]{1,0:T(8,128)(2,1)S(1)}, u32[]{:S(2)}, u32[]{:S(2)}) collective-permute-start(bf16[16,3584]{1,0:T(8,128)(2,1)S(1)} %slice.20), channel_id=1, source_target_pairs={{0,2},{1,3},{2,0},{3,1},{4,6},{5,7},{6,4},{7,5},{8,10},{9,11},{10,... | collective-permute-start | bytes 344072 | tf_op jit(solution)/shard_map/ppermute | solution.py:167
  29.1 6.1 %collective-permute-start.16 = (bf16[8,3584]{1,0:T(8,128)(2,1)S(1)}, bf16[8,3584]{1,0:T(8,128)(2,1)S(1)}, u32[]{:S(2)}, u32[]{:S(2)}) collective-permute-start(bf16[8,3584]{1,0:T(8,128)(2,1)S(1)} %add_rows.5), channel_id=1, source_target_pairs={{0,8},{1,9},{2,10},{3,11},{4,12},{5,13},{6,14},{7,15},{8,0},{9,1},... | collective-permute-start | bytes 172040 | tf_op jit(solution)/shard_map/ppermute | solution.py:167
  31.0 6.1 %collective-permute-start.14 = (bf16[8,3584]{1,0:T(8,128)(2,1)S(1)}, bf16[8,3584]{1,0:T(8,128)(2,1)S(1)}, u32[]{:S(2)}, u32[]{:S(2)}) collective-permute-start(bf16[8,3584]{1,0:T(8,128)(2,1)S(1)} %add_rows.4), channel_id=1, source_target_pairs={{0,12},{1,13},{2,14},{3,15},{4,8},{5,9},{6,10},{7,11},{8,4},{9,5},... | collective-permute-start | bytes 172040 | tf_op jit(solution)/shard_map/ppermute | solution.py:167
  32.5 4.9 %collective-permute-start.12 = (bf16[8,3584]{1,0:T(8,128)(2,1)S(1)}, bf16[8,3584]{1,0:T(8,128)(2,1)S(1)}, u32[]{:S(2)}, u32[]{:S(2)}) collective-permute-start(bf16[8,3584]{1,0:T(8,128)(2,1)S(1)} %get-tuple-element.12), channel_id=1, source_target_pairs={{0,4},{1,5},{2,6},{3,7},{4,0},{5,1},{6,2},{7,3},{8,12},{9,13},{10,... | collective-permute-start | bytes 172040 | tf_op jit(solution)/shard_map/ppermute | solution.py:167
